TPU v7x, 512 devices: a whole 4x8x8 slice. The times are simulated.
512 devices in a mesh: gz: 16 (over y, core), xy: 32 (over z, x).
Axes of the slice: x: 4, y: 8, z: 8, core: 2. Of those that a mesh axis runs over, the one named last changes fastest.
Arguments:
- patches: bfloat16 [16, 256, 128, 128], P('gz', 'xy'), may hold values from -30 to 30
- peak_offsets: int32 [16, 256, 2], P('gz', 'xy'), may hold values from -4 to 4
- tiles: bfloat16 [16, 64, 512, 512], P('gz', 'xy'), may hold values from -6 to 6
- band_offsets: int32 [16, 64, 2], P('gz', 'xy'), may hold values from -3 to 3
- routes: int32 [16, 2048, 1], P('gz', 'xy'), may hold values from 0 to 63; in each aligned block of 64 rows (0 to 63, 64 to 127, ..., all dimensions but the last counted through in order) at most 3 rows name the same one
Outputs:
- positions: float32 [16, 2, 256], P('gz', None, 'xy')
- rendered: bfloat16 [16, 64, 512, 512], P('gz', 'xy')
Inputs may be any that keep to these rules, and one draw needn't show every extreme that they name: `routes`: in the rows of one device (the 64 pieces of its tiles) no group is named more than 3 times, a bound that some block reaches.
All inputs are finite; a program needn't handle non-finite values.
Results may differ from a plain program's by a relative error of at most 0.0067.
Values may be sent and summed in bfloat16 or wider, within the bound.
No kernel may reach another device: no remote copies, remote signals or barrier semaphores. Data moves between devices by JAX's collectives and lax.ppermute only.
A program may use at most 64 MiB of HBM per device.

v0:
```python
import math

import jax
import jax.numpy as jnp
from jax import lax
from jax.sharding import PartitionSpec as P

PIECES = 32
OC = 2
BAND = 6
RELAX = 3


EPSILON = 1e-06
STEP_SIZE = 0.25
ANCHOR_WEIGHT = 0.5
MIP_SCALE = 0.0625
SCORE_GAIN = 6.0


def shifted(value, axis, steps):
    count = lax.axis_size(axis)
    initial, last = (max(0, -steps), min(count, count - steps))
    return lax.ppermute(value, axis, [(source, source + steps) for source in range(initial, last)])


def entering(x, axis, combine, identity):
    count, place = (lax.axis_size(axis), lax.axis_index(axis))
    everything = lax.all_gather(x, axis)
    start = jnp.broadcast_to(jnp.asarray(identity, x.dtype), x.shape)

    def step(k, before):
        reached = k < place
        new = combine(before, everything[k])
        return jnp.where(reached, new, before)

    return lax.fori_loop(0, count, step, start)


def with_halo(block, sides, width):
    for axis, dim in sides:
        count = lax.axis_size(axis)
        forward = [(i, i + 1) for i in range(count - 1)]
        backward = [(target, source) for source, target in forward]
        low = lax.ppermute(
            lax.slice_in_dim(block, block.shape[dim] - width, None, axis=dim), axis, forward
        )
        high = lax.ppermute(lax.slice_in_dim(block, 0, width, axis=dim), axis, backward)
        block = jnp.concatenate([low, block, high], axis=dim)
    return block


def centroid(correlation, energy_now, energy_low, offsets):
    extent = correlation.shape[-1]
    scores = (
        SCORE_GAIN
        / extent
        * correlation
        / jnp.sqrt(energy_now * energy_low + EPSILON)[:, None, None]
    )
    half_extent = extent // 2
    offset_grid = jnp.arange(extent, dtype=jnp.int32)
    relative_y = jnp.mod(offset_grid[None, :] - offsets[:, 0:1] + half_extent, extent) - half_extent
    relative_x = jnp.mod(offset_grid[None, :] - offsets[:, 1:2] + half_extent, extent) - half_extent
    inside_y = (relative_y >= -(extent // 4)) & (relative_y < extent // 4)
    inside_x = (relative_x >= -(extent // 4)) & (relative_x < extent // 4)
    in_window = inside_y[:, :, None] & inside_x[:, None, :]
    masked = jnp.where(in_window, scores, -jnp.inf)
    peak_score = jnp.max(masked, axis=(1, 2), keepdims=True)
    weights = jnp.exp(masked - peak_score)
    weight_sum = jnp.sum(weights, axis=(1, 2))
    centre_y = (
        jnp.sum(weights * relative_y[:, :, None].astype(jnp.float32), axis=(1, 2)) / weight_sum
    )
    centre_x = (
        jnp.sum(weights * relative_x[:, None, :].astype(jnp.float32), axis=(1, 2)) / weight_sum
    )
    flow_y = offsets[:, 0].astype(jnp.float32) + centre_y
    flow_x = offsets[:, 1].astype(jnp.float32) + centre_x
    return jnp.stack([flow_y, flow_x], 0)


def band_taps(residual):
    tap_offsets = jnp.arange(-BAND, BAND + 1).astype(jnp.float32)
    raw_weights = 1.0 / (1.0 + (tap_offsets - residual) ** 2)
    return raw_weights / jnp.sum(raw_weights)


def band_matrix(residual, offset, tile_edge):
    tap_values = band_taps(residual).astype(jnp.bfloat16)
    row_index = jnp.arange(tile_edge, dtype=jnp.int32)[:, None]
    col_index = jnp.arange(tile_edge, dtype=jnp.int32)[None, :]
    band_index = col_index - row_index - offset + BAND
    matrix = jnp.zeros((tile_edge, tile_edge), jnp.bfloat16)
    for tap_index in range(2 * BAND + 1):
        matrix = jnp.where(band_index == tap_index, tap_values[tap_index], matrix)
    return matrix


def dft_tables(extent):
    index_line = jnp.arange(extent, dtype=jnp.int32)
    phase = jnp.mod(index_line[:, None] * index_line[None, :], extent).astype(jnp.float32) * (
        2.0 * math.pi / extent
    )
    return (jnp.cos(phase), jnp.sin(phase))


def forward(field, cos_table, sin_table):
    highest = lax.Precision.HIGHEST
    left_cos = jnp.einsum("kn,pnm->pkm", cos_table, field, precision=highest)
    left_sin = jnp.einsum("kn,pnm->pkm", sin_table, field, precision=highest)
    real_part = jnp.einsum("pkm,lm->pkl", left_cos, cos_table, precision=highest) - jnp.einsum(
        "pkm,lm->pkl", left_sin, sin_table, precision=highest
    )
    imag_part = -(
        jnp.einsum("pkm,lm->pkl", left_cos, sin_table, precision=highest)
        + jnp.einsum("pkm,lm->pkl", left_sin, cos_table, precision=highest)
    )
    return (real_part, imag_part)


def inverse(cross_real, cross_imag, cos_table, sin_table):
    highest = lax.Precision.HIGHEST
    extent = cross_real.shape[-1]
    outer_real = jnp.einsum("kn,pnm->pkm", cos_table, cross_real, precision=highest) - jnp.einsum(
        "kn,pnm->pkm", sin_table, cross_imag, precision=highest
    )
    outer_imag = jnp.einsum("kn,pnm->pkm", sin_table, cross_real, precision=highest) + jnp.einsum(
        "kn,pnm->pkm", cos_table, cross_imag, precision=highest
    )
    result = jnp.einsum("pkm,lm->pkl", outer_real, cos_table, precision=highest) - jnp.einsum(
        "pkm,lm->pkl", outer_imag, sin_table, precision=highest
    )
    return result / float(extent * extent)


def add_arrays(earlier, later):
    return earlier + later


def body(patches, peak_offsets, tiles, band_offsets, routes):
    extent = patches.shape[-1]
    cos_table, sin_table = dft_tables(extent)
    current = patches[0].astype(jnp.float32)
    current_real, current_imag = forward(current, cos_table, sin_table)
    energy_now = jnp.mean(current * current, axis=(1, 2))
    below_patches = shifted(patches, "gz", 1)[0].astype(jnp.float32)
    lower_real, lower_imag = forward(below_patches, cos_table, sin_table)
    energy_low = jnp.mean(below_patches * below_patches, axis=(1, 2))
    cross_real = current_real * lower_real + current_imag * lower_imag
    cross_imag = current_imag * lower_real - current_real * lower_imag
    correlation = inverse(cross_real, cross_imag, cos_table, sin_table)
    flow_field = centroid(correlation, energy_now, energy_low, peak_offsets[0])
    section = lax.axis_index("gz")
    section_total = lax.axis_size("gz")
    before = entering(flow_field, "gz", add_arrays, jnp.zeros_like(flow_field))
    positions = before + flow_field
    for sweep in range(RELAX):
        stacked = jnp.stack([positions, flow_field], 0)[:, None]
        extended = with_halo(stacked, (("gz", 1),), 1)
        lower_term = jnp.where(section > 0, extended[0, 0] + flow_field - positions, 0.0)
        upper_term = jnp.where(
            section < section_total - 1, extended[0, 2] - extended[1, 2] - positions, 0.0
        )
        positions = positions + STEP_SIZE * (lower_term + upper_term - ANCHOR_WEIGHT * positions)
    positions_out = positions[None]
    tile_count = tiles.shape[1]
    tile_edge = tiles.shape[-1]
    shifts = MIP_SCALE * jnp.mean(
        positions.reshape(2, tile_count, positions.shape[1] // tile_count), axis=2
    )
    first_passes = []
    row_residuals = []
    for which_tile in range(tile_count):
        residual_x = shifts[1, which_tile] - band_offsets[0, which_tile, 1].astype(jnp.float32)
        col_band = band_matrix(residual_x, band_offsets[0, which_tile, 1], tile_edge)
        first_passes.append(
            jnp.dot(tiles[0, which_tile], col_band.T, preferred_element_type=jnp.float32).astype(
                jnp.bfloat16
            )
        )
        row_residuals.append(
            shifts[0, which_tile] - band_offsets[0, which_tile, 0].astype(jnp.float32)
        )
    destination = routes[0, :, 0]
    piece_count = destination.shape[0]
    piece_height = tile_edge // PIECES
    xy_devices = lax.axis_size("xy")
    group_total = OC * xy_devices
    most_per_group = max(3, 2 * piece_count // group_total)
    per_owner = OC * most_per_group
    slot_total = xy_devices * per_owner
    position_line = jnp.arange(piece_count, dtype=jnp.int32)
    same_group = destination[:, None] == destination[None, :]
    earlier_count = jnp.sum(
        (same_group & (position_line[None, :] < position_line[:, None])).astype(jnp.int32), axis=1
    )
    slot_index = destination // OC * per_owner + destination % OC * most_per_group + earlier_count
    selection = slot_index[None, :] == jnp.arange(slot_total, dtype=jnp.int32)[:, None]
    packing = selection.astype(jnp.bfloat16)
    piece_label = jnp.sum(
        jnp.where(selection, (position_line % PIECES + 1)[None, :], 0), axis=1
    ).astype(jnp.bfloat16)
    rendered_list = []
    for which_tile in range(tile_count):
        row_band = band_matrix(row_residuals[which_tile], band_offsets[0, which_tile, 0], tile_edge)
        rendered_list.append(
            jnp.dot(row_band, first_passes[which_tile], preferred_element_type=jnp.float32).astype(
                jnp.bfloat16
            )
        )
    piece_rows_flat = jnp.stack(rendered_list, 0).reshape(piece_count, piece_height * tile_edge)
    piece_buffer = jnp.dot(packing, piece_rows_flat, preferred_element_type=jnp.float32).astype(
        jnp.bfloat16
    )
    received_pieces, received_labels = (
        lax.all_to_all(
            piece_buffer.reshape(xy_devices, per_owner, piece_height * tile_edge),
            "xy",
            split_axis=0,
            concat_axis=0,
            tiled=True,
        ),
        lax.all_to_all(
            piece_label.reshape(xy_devices, per_owner),
            "xy",
            split_axis=0,
            concat_axis=0,
            tiled=True,
        ),
    )
    arrived = received_pieces.reshape(slot_total, piece_height * tile_edge)
    label_values = received_labels.reshape(slot_total).astype(jnp.int32)
    local_group = jnp.arange(slot_total, dtype=jnp.int32) % per_owner // most_per_group
    target_row = jnp.where(label_values > 0, local_group * PIECES + label_values - 1, -1)
    collect = target_row[None, :] == jnp.arange(OC * PIECES, dtype=jnp.int32)[:, None]
    group_sums = jnp.dot(collect.astype(jnp.bfloat16), arrived, preferred_element_type=jnp.float32)
    group_counts = jnp.sum(collect.astype(jnp.float32), axis=1)
    averaged = group_sums / jnp.maximum(group_counts, 1.0)[:, None]
    rendered_out = averaged.astype(jnp.bfloat16).reshape(1, OC, tile_edge, tile_edge)
    return (positions_out, rendered_out)


def solution(mesh):
    placed = (
        P("gz", "xy", None, None),
        P("gz", "xy", None),
        P("gz", "xy", None, None),
        P("gz", "xy", None),
        P("gz", "xy", None),
    )
    return jax.shard_map(
        body,
        mesh=mesh,
        in_specs=placed,
        out_specs=(P("gz", None, "xy"), P("gz", "xy", None, None)),
        check_vma=False,
    )
```

profile of v0, /device:TPU:1, one launch (start us, length us, event | category | flops | bytes accessed | tf_op | source)
XLA Modules:
  0.0 249.2 jit_solution(7125950154162886880)
XLA Ops:
  0.7 4.7 %collective-permute-start = (bf16[1,8,128,128]{3,2,1,0:T(8,128)(2,1)}, bf16[1,8,128,128]{3,2,1,0:T(8,128)(2,1)S(1)}, u32[]{:S(2)}, u32[]{:S(2)}) collective-permute-start(bf16[1,8,128,128]{3,2,1,0:T(8,128)(2,1)} %param.7), channel_id=1, source_target_pairs={{0,32},{32,64},{64,96},{96,128},{128,160},{160,192},{192,224},{224... | collective-permute-start | bytes 786440 | tf_op jit(solution)/shard_map/ppermute | solution.py:24
  5.4 0.9 convert_reduce_fusion.1
  7.8 12.9 %all-to-all-start = ((bf16[32,1,6]{2,1,0:T(2,128)(2,1)}), bf16[32,1,6]{2,1,0:T(2,128)(2,1)S(1)}, u32[]{:S(2)}, u32[]{:S(2)}) async-start(bf16[32,1,6]{2,1,0:T(2,128)(2,1)} %convert_element_type.204), calls=%async_computation | async-start | bytes 32768 | tf_op jit(solution)/shard_map/all_to_all | solution.py:224
  20.7 1.5 convolution_bitcast_fusion.3
  22.3 1.5 convolution_bitcast_fusion.2
  32.5 0.9 multiply_subtract_fusion
  33.4 1.1 fusion.275
  34.5 1.1 fusion.289
  35.7 1.3 fusion.6
  37.0 1.1 fusion.7
  38.1 1.1 fusion.287
  39.4 1.3 fusion.499
  41.1 16.5 %all-gather.1 = f32[16,2,8]{2,1,0:T(2,128)S(1)} all-gather(f32[1,2,8]{2,1,0:T(2,128)S(1)} %fusion.491), channel_id=2, replica_groups=mesh['gz'=16,'xy'=32] {'gz'}, dimensions={0}, use_global_device_ids=true | all-gather | bytes 1088 | tf_op jit(solution)/shard_map/all_gather | solution.py:29
  58.2 1.9 collective-permute-start.1
  60.1 2.4 collective-permute-start.2
  63.2 1.9 collective-permute-done.2
  65.0 2.0 collective-permute-start.3
  67.0 2.4 collective-permute-start.4
  69.9 2.0 collective-permute-done.4
  71.9 2.0 collective-permute-start.5
  73.9 2.4 collective-permute-start.6
  77.0 1.8 collective-permute-done.6
  90.0 19.6 %fusion.1 = bf16[1,512,512]{2,1,0:T(8,128)(2,1)S(1)} fusion(bf16[1,2,512,512]{3,2,1,0:T(8,128)(2,1)S(1)} %copy-done.4, s32[]{:T(128)} %bitcast.47, s32[]{:T(128)} %bitcast.32, bf16[]{:T(256)} %bitcast.61, bf16[]{:T(256)} %bitcast.60, bf16[]{:T(256)} %bitcast.59, bf16[]{:T(256)} %bitcast.58, bf16[]{:T(256)} %bitcast.57, bf16[]{:T(256)} %bitcast.56, ...), kind=kOutput, calls=%fused_computation.8 | convolution fusion | flops 552599552 | bytes 1048636 | tf_op jit(solution)/shard_map/dot_general | solution.py:208
  109.6 19.6 %fusion.2 = bf16[1,512,512]{2,1,0:T(8,128)(2,1)S(1)} fusion(bf16[1,2,512,512]{3,2,1,0:T(8,128)(2,1)S(1)} %copy-done.4, s32[]{:T(128)} %bitcast.79, s32[]{:T(128)} %bitcast.64, bf16[]{:T(256)} %bitcast.93, bf16[]{:T(256)} %bitcast.92, bf16[]{:T(256)} %bitcast.91, bf16[]{:T(256)} %bitcast.90, bf16[]{:T(256)} %bitcast.89, bf16[]{:T(256)} %bitcast.88, ...), kind=kOutput, calls=%fused_computation.9 | convolution fusion | flops 552599552 | bytes 1048636 | tf_op jit(solution)/shard_map/dot_general | solution.py:208
  129.3 1.3 reshape.312
  130.6 2.3 convolution_convert_fusion
  132.9 2.9 %reshape.313 = bf16[32,6,8192]{2,1,0:T(8,128)(2,1)} reshape(bf16[192,8192]{1,0:T(8,128)(2,1)S(1)} %convolution_convert_fusion) | data formatting | bytes 6291456 | tf_op jit(solution)/shard_map/reshape | solution.py:218
  135.9 9.6 %all-to-all-start.1 = ((bf16[32,6,8192]{2,1,0:T(8,128)(2,1)}), bf16[32,6,8192]{2,1,0:T(8,128)(2,1)}, u32[]{:S(2)}, u32[]{:S(2)}) async-start(bf16[32,6,8192]{2,1,0:T(8,128)(2,1)} %reshape.313), calls=%async_computation.1 | async-start | bytes 8388608 | tf_op jit(solution)/shard_map/all_to_all | solution.py:217
  145.8 95.9 %all-to-all-done.1 = bf16[32,6,8192]{2,1,0:T(8,128)(2,1)} async-done(((bf16[32,6,8192]{2,1,0:T(8,128)(2,1)}), bf16[32,6,8192]{2,1,0:T(8,128)(2,1)}, u32[]{:S(2)}, u32[]{:S(2)}) %all-to-all-start.1) | async-done | bytes 3145760 | tf_op jit(solution)/shard_map/all_to_all | solution.py:217
  241.7 3.4 %reshape.314 = bf16[192,8192]{1,0:T(8,128)(2,1)S(1)} reshape(bf16[32,6,8192]{2,1,0:T(8,128)(2,1)} %all-to-all-done.1) | data formatting | bytes 6291456 | tf_op jit(solution)/shard_map/reshape | solution.py:232
  245.2 1.7 fusion
  246.9 2.3 reshape.315
  (85 shorter events, 19.9 us)
Async XLA Ops:
  0.6 24.8 %copy-start = (bf16[1,8,128,128]{3,2,1,0:T(8,128)(2,1)S(1)}, bf16[1,8,128,128]{3,2,1,0:T(8,128)(2,1)}, u32[]{:S(2)}) copy-start(bf16[1,8,128,128]{3,2,1,0:T(8,128)(2,1)} %param.7) | copy-start | bytes 786436
  0.6 25.0 %copy-start.2 = (s32[1,8,2]{1,2,0:T(2,128)S(1)}, s32[1,8,2]{1,2,0:T(2,128)}, u32[]{:S(2)}) copy-start(s32[1,8,2]{1,2,0:T(2,128)} %param.8) | copy-start | bytes 196
  0.7 25.2 %copy-start.3 = (s32[1,2,2]{2,1,0:T(2,128)S(1)}, s32[1,2,2]{2,1,0:T(2,128)}, u32[]{:S(2)}) copy-start(s32[1,2,2]{2,1,0:T(2,128)} %param.10) | copy-start | bytes 52
  0.7 27.3 %collective-permute-start = (bf16[1,8,128,128]{3,2,1,0:T(8,128)(2,1)}, bf16[1,8,128,128]{3,2,1,0:T(8,128)(2,1)S(1)}, u32[]{:S(2)}, u32[]{:S(2)}) collective-permute-start(bf16[1,8,128,128]{3,2,1,0:T(8,128)(2,1)} %param.7), channel_id=1, source_target_pairs={{0,32},{32,64},{64,96},{96,128},{128,160},{160,192},{192,224},{224... | collective-permute-start | bytes 786440 | tf_op jit(solution)/shard_map/ppermute | solution.py:24
  7.8 128.0 %all-to-all-start = ((bf16[32,1,6]{2,1,0:T(2,128)(2,1)}), bf16[32,1,6]{2,1,0:T(2,128)(2,1)S(1)}, u32[]{:S(2)}, u32[]{:S(2)}) async-start(bf16[32,1,6]{2,1,0:T(2,128)(2,1)} %convert_element_type.204), calls=%async_computation | async-start | bytes 32768 | tf_op jit(solution)/shard_map/all_to_all | solution.py:224
  37.0 53.0 %copy-start.4 = (bf16[1,2,512,512]{3,2,1,0:T(8,128)(2,1)S(1)}, bf16[1,2,512,512]{3,2,1,0:T(8,128)(2,1)}, u32[]{:S(2)}) copy-start(bf16[1,2,512,512]{3,2,1,0:T(8,128)(2,1)} %param.9) | copy-start | bytes 3145732
  58.2 5.0 %collective-permute-start.1 = (f32[2,1,2,8]{3,2,0,1:T(2,128)S(1)}, f32[2,1,2,8]{3,2,0,1:T(2,128)S(1)}, u32[]{:S(2)}, u32[]{:S(2)}) collective-permute-start(f32[2,1,2,8]{3,2,0,1:T(2,128)S(1)} %fusion.331), channel_id=1, source_target_pairs={{0,32},{32,64},{64,96},{96,128},{128,160},{160,192},{192,224},{224... | collective-permute-start | bytes 392 | tf_op jit(solution)/shard_map/ppermute | solution.py:45
  60.1 4.9 %collective-permute-start.2 = (f32[2,1,2,8]{3,2,0,1:T(2,128)S(1)}, f32[2,1,2,8]{3,2,0,1:T(2,128)S(1)}, u32[]{:S(2)}, u32[]{:S(2)}) collective-permute-start(f32[2,1,2,8]{3,2,0,1:T(2,128)S(1)} %fusion.331), channel_id=1, source_target_pairs={{32,0},{64,32},{96,64},{128,96},{160,128},{192,160},{224,192},{256... | collective-permute-start | bytes 392 | tf_op jit(solution)/shard_map/ppermute | solution.py:48
  65.0 4.9 %collective-permute-start.3 = (f32[2,1,2,8]{3,2,0,1:T(2,128)S(1)}, f32[2,1,2,8]{3,2,0,1:T(2,128)S(1)}, u32[]{:S(2)}, u32[]{:S(2)}) collective-permute-start(f32[2,1,2,8]{3,2,0,1:T(2,128)S(1)} %fusion.332), channel_id=1, source_target_pairs={{0,32},{32,64},{64,96},{96,128},{128,160},{160,192},{192,224},{224... | collective-permute-start | bytes 392 | tf_op jit(solution)/shard_map/ppermute | solution.py:45
  67.0 4.9 %collective-permute-start.4 = (f32[2,1,2,8]{3,2,0,1:T(2,128)S(1)}, f32[2,1,2,8]{3,2,0,1:T(2,128)S(1)}, u32[]{:S(2)}, u32[]{:S(2)}) collective-permute-start(f32[2,1,2,8]{3,2,0,1:T(2,128)S(1)} %fusion.332), channel_id=1, source_target_pairs={{32,0},{64,32},{96,64},{128,96},{160,128},{192,160},{224,192},{256... | collective-permute-start | bytes 392 | tf_op jit(solution)/shard_map/ppermute | solution.py:48
  71.9 5.0 %collective-permute-start.5 = (f32[2,1,2,8]{3,2,0,1:T(2,128)S(1)}, f32[2,1,2,8]{3,2,0,1:T(2,128)S(1)}, u32[]{:S(2)}, u32[]{:S(2)}) collective-permute-start(f32[2,1,2,8]{3,2,0,1:T(2,128)S(1)} %fusion.333), channel_id=1, source_target_pairs={{0,32},{32,64},{64,96},{96,128},{128,160},{160,192},{192,224},{224... | collective-permute-start | bytes 392 | tf_op jit(solution)/shard_map/ppermute | solution.py:45
  73.9 4.9 %collective-permute-start.6 = (f32[2,1,2,8]{3,2,0,1:T(2,128)S(1)}, f32[2,1,2,8]{3,2,0,1:T(2,128)S(1)}, u32[]{:S(2)}, u32[]{:S(2)}) collective-permute-start(f32[2,1,2,8]{3,2,0,1:T(2,128)S(1)} %fusion.333), channel_id=1, source_target_pairs={{32,0},{64,32},{96,64},{128,96},{160,128},{192,160},{224,192},{256... | collective-permute-start | bytes 392 | tf_op jit(solution)/shard_map/ppermute | solution.py:48
  78.8 30.8 %copy-start.1 = (f32[2,8]{1,0:T(2,128)}, f32[2,8]{1,0:T(2,128)S(1)}, u32[]{:S(2)}) copy-start(f32[2,8]{1,0:T(2,128)S(1)} %multiply_add_fusion.1) | copy-start | bytes 196
  135.9 105.9 %all-to-all-start.1 = ((bf16[32,6,8192]{2,1,0:T(8,128)(2,1)}), bf16[32,6,8192]{2,1,0:T(8,128)(2,1)}, u32[]{:S(2)}, u32[]{:S(2)}) async-start(bf16[32,6,8192]{2,1,0:T(8,128)(2,1)} %reshape.313), calls=%async_computation.1 | async-start | bytes 8388608 | tf_op jit(solution)/shard_map/all_to_all | solution.py:217
where the time goes:
time: 250 us; the launch traced here: 249 us
  waiting for transfers between devices  102 us (41%)
  matrix products  61.1 us (24%)
  starting transfers between devices  40.2 us (16%)
  blocking collectives  16.5 us (7%)
  local copies, waits for them, and re-layouts  15 us (6%)
  other arithmetic  8.33 us (3%)
  between operations  6.12 us (2%)
    all_to_all x1, waiting for transfers between devices, body(): lax.all_to_all(piece_buffer.reshape(xy_devices, per_owner, piece_height *...  95.9 us
    dot_general x2, matrix products, body(): jnp.dot(row_band, first_passes[which_tile], preferred_element_type=jnp.fl...  39.2 us
    all_gather x1, blocking collectives, entering(): everything = lax.all_gather(x, axis)  16.5 us
    all_to_all x1, starting transfers between devices, body(): lax.all_to_all(piece_label.reshape(xy_devices, per_owner), 'xy', split_ax...  12.9 us
    all_to_all x1, starting transfers between devices, body(): lax.all_to_all(piece_buffer.reshape(xy_devices, per_owner, piece_height *...  9.63 us
    ppermute x3, starting transfers between devices, with_halo(): lax.ppermute(lax.slice_in_dim(block, 0, width, axis=dim), axis, backward)  7.14 us
    ppermute x3, starting transfers between devices, with_halo(): lax.ppermute(lax.slice_in_dim(block, block.shape[dim] - width, None, axis...  5.83 us
    ppermute x3, waiting for transfers between devices, with_halo(): lax.ppermute(lax.slice_in_dim(block, 0, width, axis=dim), axis, backward)  5.64 us
  transfers between devices with their start and end apart: 9, of which 4 were waited for; matrix products, arithmetic and copies ran while one was open for 31% of the time, Pallas kernels for 0%

commit v1 on v0

v1 whole, which is shorter than its diff:
```python
import functools
import math

import jax
import jax.numpy as jnp
import numpy as np
from jax import lax
from jax.experimental import pallas as pl
from jax.experimental.pallas import tpu as pltpu
from jax.sharding import PartitionSpec as P

PIECES = 32
BAND = 6
RELAX = 3
EPSILON = 1e-06
STEP_SIZE = 0.25
ANCHOR_WEIGHT = 0.5
MIP_SCALE = 0.0625
SCORE_GAIN = 6.0

EXTENT = 128
HALF = 72
REACH = 40
BF = jnp.bfloat16
F32 = jnp.float32


def high_low(table):
    high = table.astype(jnp.bfloat16)
    low = (table - high.astype(np.float64)).astype(jnp.bfloat16)
    return high, low


def dft_constants():
    line = np.arange(EXTENT)
    phase = 2.0 * np.pi * ((line[:, None] * line[None, :]) % EXTENT) / EXTENT
    cos, sin = np.cos(phase), np.sin(phase)
    first = np.concatenate([cos[:HALF], sin[:HALF]], 0)
    first = np.concatenate(high_low(first), 1)
    second_high, second_low = high_low(np.concatenate([cos, sin], 1))
    second = np.concatenate([second_high, second_high, second_low], 0)
    third_high, third_low = high_low(np.block([[cos, sin], [-sin, cos]]))
    third = np.concatenate([third_high, third_high, third_low], 0)
    weight = np.where(line[:HALF] <= EXTENT // 2, 2.0, 0.0)
    weight[0] = weight[EXTENT // 2] = 1.0
    rows = (np.arange(-REACH, REACH) % EXTENT)[:, None]
    angle = 2.0 * np.pi * ((rows * line[None, :HALF]) % EXTENT) / EXTENT
    fourth = np.concatenate([weight * np.cos(angle), -weight * np.sin(angle)], 1)
    fourth_high, fourth_low = high_low(fourth / float(EXTENT * EXTENT))
    fourth = np.concatenate([fourth_high, fourth_high, fourth_low], 1)
    return first, second, third, fourth


def relaxation_map(sections):
    flow = np.eye(sections)
    positions = np.tril(np.ones((sections, sections)))
    for _ in range(RELAX):
        lower = np.zeros_like(positions)
        upper = np.zeros_like(positions)
        lower[1:] = positions[:-1] + flow[1:] - positions[1:]
        upper[:-1] = positions[1:] - flow[1:] - positions[:-1]
        positions = positions + STEP_SIZE * (lower + upper - ANCHOR_WEIGHT * positions)
    return positions.astype(np.float32)


def split(value):
    high = value.astype(BF)
    return high, (value - high.astype(F32)).astype(BF)


def dot(a, b):
    return jnp.dot(a, b, preferred_element_type=F32)


def flow_kernel(peak_ref, now_ref, low_ref, first_ref, second_ref, third_ref, fourth_ref, out_ref):
    count = now_ref.shape[0]
    correlations = []
    for pair in range(count // 2):
        halves = []
        for ref in (now_ref, low_ref):
            both = jnp.concatenate([ref[2 * pair], ref[2 * pair + 1]], 1)
            lines = dot(first_ref[...], jnp.concatenate([both, both], 0))
            halves += [lines[:, :EXTENT], lines[:, EXTENT:]]
        high, low = split(jnp.concatenate(halves, 0))
        spectra = dot(jnp.concatenate([high, low, high], 1), second_ref[...])
        parts = []
        for k in range(4):
            a = spectra[2 * HALF * k : 2 * HALF * k + HALF]
            b = spectra[2 * HALF * k + HALF : 2 * HALF * (k + 1)]
            parts.append(
                (a[:, :EXTENT] - b[:, EXTENT:], -(a[:, EXTENT:] + b[:, :EXTENT]))
            )
        crosses = []
        for k in range(2):
            (nr, ni), (lr, li) = parts[k], parts[k + 2]
            crosses.append(jnp.concatenate([nr * lr + ni * li, ni * lr - nr * li], 1))
        high, low = split(jnp.concatenate(crosses, 0))
        outer = dot(jnp.concatenate([high, low, high], 1), third_ref[...])
        columns = []
        for k in range(2):
            block = outer[HALF * k : HALF * (k + 1)]
            columns.append(jnp.concatenate([block[:, :EXTENT], block[:, EXTENT:]], 0))
        high, low = split(jnp.concatenate(columns, 1))
        result = dot(fourth_ref[...], jnp.concatenate([high, low, high], 0))
        correlations += [result[:, :EXTENT], result[:, EXTENT:]]

    def energy(ref):
        rows = []
        for n in range(count):
            value = ref[n].astype(F32)
            rows.append(jnp.sum(value * value, axis=0, keepdims=True))
        total = jnp.sum(jnp.concatenate(rows, 0), axis=1, keepdims=True)
        return total * (1.0 / (EXTENT * EXTENT))

    scale = (SCORE_GAIN / EXTENT) / jnp.sqrt(energy(now_ref) * energy(low_ref) + EPSILON)
    shape = (2 * REACH, EXTENT)
    row = lax.broadcasted_iota(jnp.int32, shape, 0) - REACH
    column = lax.broadcasted_iota(jnp.int32, shape, 1)
    scores, relatives, tops = [], [], []
    for n in range(count):
        rel_y = row - peak_ref[n, 0]
        rel_x = ((column - peak_ref[n, 1] + EXTENT // 2) & (EXTENT - 1)) - EXTENT // 2
        quarter = EXTENT // 4
        inside = (rel_y >= -quarter) & (rel_y < quarter) & (rel_x >= -quarter) & (rel_x < quarter)
        score = jnp.where(inside, correlations[n] * scale[n : n + 1], -1e30)
        scores.append(score)
        relatives.append((rel_y.astype(F32), rel_x[:1].astype(F32)))
        tops.append(jnp.max(score, axis=0, keepdims=True))
    top = jnp.max(jnp.concatenate(tops, 0), axis=1, keepdims=True)
    sums, sums_y, sums_x = [], [], []
    for n in range(count):
        weight = jnp.exp(scores[n] - top[n : n + 1])
        rel_y, rel_x = relatives[n]
        along = jnp.sum(weight, axis=0, keepdims=True)
        sums.append(along)
        sums_y.append(jnp.sum(weight * rel_y, axis=0, keepdims=True))
        sums_x.append(along * rel_x)
    total, total_y, total_x = (
        jnp.sum(jnp.concatenate(s, 0), axis=1, keepdims=True) for s in (sums, sums_y, sums_x)
    )
    node = lax.broadcasted_iota(jnp.int32, (count, EXTENT), 0)
    lane = lax.broadcasted_iota(jnp.int32, (count, EXTENT), 1)
    peak_y = jnp.zeros((count, EXTENT), jnp.int32)
    peak_x = jnp.zeros((count, EXTENT), jnp.int32)
    for n in range(count):
        peak_y = jnp.where(node == n, peak_ref[n, 0], peak_y)
        peak_x = jnp.where(node == n, peak_ref[n, 1], peak_x)
    flow_y = peak_y.astype(F32) + total_y / total
    flow_x = peak_x.astype(F32) + total_x / total
    flow = jnp.where(lane == 0, flow_y, jnp.where(lane == 1, flow_x, 0.0))
    out_ref[...] = jnp.broadcast_to(flow[None], out_ref.shape)


def fill_band(target_ref, residual, offset, sub_sign):
    block = 128
    lane = lax.broadcasted_iota(jnp.int32, (1, block), 1)
    tap = (lane - BAND).astype(F32) - residual
    raw = jnp.where(lane <= 2 * BAND, 1.0 / (1.0 + tap * tap), 0.0)
    norm = jnp.sum(raw, axis=1, keepdims=True)
    a = lax.broadcasted_iota(jnp.int32, (block, block), 0)
    b = lax.broadcasted_iota(jnp.int32, (block, block), 1)
    d = sub_sign * (a - b) - offset
    k = ((d + block // 2) & (block - 1)) - block // 2
    away = k.astype(F32) - residual
    value = (1.0 / (1.0 + away * away)) / norm
    blocks = {}
    for step in (-1, 0, 1):
        near = jnp.abs(d + sub_sign * step * block) <= BAND
        blocks[step] = jnp.where(near, value, 0.0).astype(BF)
    zero = jnp.zeros((block, block), BF)
    count = target_ref.shape[0] // block
    for i in range(count):
        for j in range(count):
            target_ref[i * block : (i + 1) * block, j * block : (j + 1) * block] = blocks.get(
                i - j, zero
            )


def render_kernel(map_ref, band_ref, flow_ref, tile_ref, position_ref, send_ref, col_ref, row_ref, pass_ref):
    sections, nodes, _ = flow_ref.shape
    tile_count, edge, _ = tile_ref.shape
    position = jnp.zeros(flow_ref.shape[1:], F32)
    for s in range(sections):
        position = position + map_ref[0, s] * flow_ref[s]
    position_ref[...] = position
    per_tile = nodes // tile_count
    height = edge // PIECES
    chunk = 128
    for t in range(tile_count):
        mean = jnp.sum(position[t * per_tile : (t + 1) * per_tile], axis=0, keepdims=True)
        shift = (MIP_SCALE / per_tile) * mean
        offset_y, offset_x = band_ref[t, 0], band_ref[t, 1]
        fill_band(col_ref, shift[:, 1:2] - offset_x.astype(F32), offset_x, 1)
        fill_band(row_ref, shift[:, 0:1] - offset_y.astype(F32), offset_y, -1)
        for c in range(edge // chunk):
            rows = slice(c * chunk, (c + 1) * chunk)
            pass_ref[rows, :] = dot(tile_ref[t, rows, :], col_ref[...]).astype(BF)
        for c in range(edge // chunk):
            rows = slice(c * chunk, (c + 1) * chunk)
            done = dot(row_ref[rows, :], pass_ref[...]).astype(BF)
            send_ref[c * chunk // height : (c + 1) * chunk // height, t * height : (t + 1) * height, :] = (
                done.reshape(chunk // height, height, edge)
            )


def gather_kernel(label_ref, inverse_ref, piece_ref, out_ref, total_ref):
    owners, rows, _ = piece_ref.shape
    groups, height, _ = total_ref.shape
    total_ref[...] = jnp.zeros(total_ref.shape, F32)
    per_owner = rows // height

    def add(owner, carry):
        for t in range(per_owner):
            group = label_ref[owner, t]
            piece = piece_ref[owner, t * height : (t + 1) * height, :].astype(F32)
            total_ref[group] = total_ref[group] + piece
        return carry

    lax.fori_loop(0, owners, add, 0)
    share = groups // owners

    def finish(owner, carry):
        for t in range(share):
            value = total_ref[owner * share + t] * inverse_ref[owner, t]
            out_ref[owner, t * height : (t + 1) * height, :] = value.astype(BF)
        return carry

    lax.fori_loop(0, owners, finish, 0)


def in_vmem():
    return pl.BlockSpec(memory_space=pltpu.VMEM)


def in_smem():
    return pl.BlockSpec(memory_space=pltpu.SMEM)


def params():
    return pltpu.CompilerParams(vmem_limit_bytes=40 * 1024 * 1024)


def exchange(value, axis):
    return lax.all_to_all(value, axis, split_axis=0, concat_axis=0, tiled=True)


def body(patches, peak_offsets, tiles, band_offsets, routes):
    sections = lax.axis_size("gz")
    owners = lax.axis_size("xy")
    section = lax.axis_index("gz")
    tile_count, edge = tiles.shape[1], tiles.shape[-1]
    height = edge // PIECES
    groups = 2 * owners

    below = lax.ppermute(patches, "gz", [(i, i + 1) for i in range(sections - 1)])
    label = routes[0, :, 0].reshape(tile_count, PIECES).T.astype(F32)
    label = jnp.pad(label, ((0, 0), (0, EXTENT - tile_count)))[:, None, :]
    label = exchange(label, "xy")[:, 0, :tile_count].astype(jnp.int32)
    match = label.reshape(-1)[:, None] == jnp.arange(groups, dtype=jnp.int32)[None, :]
    inverse = 1.0 / jnp.maximum(jnp.sum(match.astype(F32), axis=0), 1.0)
    inverse = inverse.reshape(owners, groups // owners)

    tables = [jnp.asarray(t) for t in dft_constants()]
    count = patches.shape[1]
    flow = pl.pallas_call(
        flow_kernel,
        out_shape=jax.ShapeDtypeStruct((sections, count, EXTENT), F32),
        in_specs=[in_smem()] + [in_vmem()] * 6,
        out_specs=in_vmem(),
        compiler_params=params(),
        name="flow",
    )(peak_offsets[0], patches[0], below[0], *tables)
    flow = exchange(flow, "gz")

    linear = lax.dynamic_slice_in_dim(jnp.asarray(relaxation_map(sections)), section, 1, 0)
    position, pieces = pl.pallas_call(
        render_kernel,
        out_shape=(
            jax.ShapeDtypeStruct((count, EXTENT), F32),
            jax.ShapeDtypeStruct((PIECES, tile_count * height, edge), BF),
        ),
        in_specs=[in_smem(), in_smem(), in_vmem(), in_vmem()],
        out_specs=(in_vmem(), in_vmem()),
        scratch_shapes=[pltpu.VMEM((edge, edge), BF)] * 3,
        compiler_params=params(),
        name="render",
    )(linear, band_offsets[0], flow, tiles[0])
    pieces = exchange(pieces, "xy")

    cells = pl.pallas_call(
        gather_kernel,
        out_shape=jax.ShapeDtypeStruct((owners, groups // owners * height, edge), BF),
        in_specs=[in_smem(), in_smem(), in_vmem()],
        out_specs=in_vmem(),
        scratch_shapes=[pltpu.VMEM((groups, height, edge), F32)],
        compiler_params=params(),
        name="gather",
    )(label, inverse, pieces)
    cells = exchange(cells, "xy")
    rendered = cells.reshape(PIECES, groups // owners, height, edge).transpose(1, 0, 2, 3)
    rendered = rendered.reshape(1, groups // owners, edge, edge)
    return position[:, :2].T[None], rendered


def solution(mesh):
    placed = (
        P("gz", "xy", None, None),
        P("gz", "xy", None),
        P("gz", "xy", None, None),
        P("gz", "xy", None),
        P("gz", "xy", None),
    )
    return jax.shard_map(
        body,
        mesh=mesh,
        in_specs=placed,
        out_specs=(P("gz", None, "xy"), P("gz", "xy", None, None)),
        check_vma=False,
    )
```

time: 250 us -> 128 us (0.51)
  the two profiles are of different devices: /device:TPU:1 before, /device:TPU:2 now
where the time goes in v1:
time: 128 us; the launch traced here: 127 us
  waiting for transfers between devices  65.4 us (51%)
  starting transfers between devices  40.2 us (31%)
  Pallas kernels  11.2 us (9%)
  local copies, waits for them, and re-layouts  9.44 us (7%)
    all_to_all x4, waiting for transfers between devices, exchange(): return lax.all_to_all(value, axis, split_axis=0, concat_axis=0, tiled=True)  64.8 us
    all_to_all x4, starting transfers between devices, exchange(): return lax.all_to_all(value, axis, split_axis=0, concat_axis=0, tiled=True)  38.3 us
    unnamed x16, local copies, waits for them, and re-layouts  5.32 us
    pallas_call x1, Pallas kernels, body(): pl.pallas_call(flow_kernel, out_shape=jax.ShapeDtypeStruct((sections, cou...  4.94 us
    pallas_call x1, Pallas kernels, body(): pl.pallas_call(render_kernel, out_shape=(jax.ShapeDtypeStruct((count, EXT...  3.33 us
    pallas_call x1, Pallas kernels, body(): pl.pallas_call(gather_kernel, out_shape=jax.ShapeDtypeStruct((owners, gro...  2.91 us
  transfers between devices with their start and end apart: 5, of which 5 were waited for; matrix products, arithmetic and copies ran while one was open for 3% of the time, Pallas kernels for 3%

profile of v1, /device:TPU:2, one launch (start us, length us, event | category | flops | bytes accessed | tf_op | source)
XLA Modules:
  0.0 127.2 jit_solution(3866543160728448436)
XLA Ops:
  0.6 0.0 copy-start
  0.6 1.9 %collective-permute-start = (bf16[1,8,128,128]{3,2,1,0:T(8,128)(2,1)}, bf16[1,8,128,128]{3,2,1,0:T(8,128)(2,1)S(1)}, u32[]{:S(2)}, u32[]{:S(2)}) collective-permute-start(bf16[1,8,128,128]{3,2,1,0:T(8,128)(2,1)} %param.10), channel_id=1, source_target_pairs={{0,32},{32,64},{64,96},{96,128},{128,160},{160,192},{192,224},{224... | collective-permute-start | bytes 786440 | tf_op jit(solution)/shard_map/ppermute | solution.py:255
  2.5 0.8 copy.28.peak_ref
  3.3 0.6 collective-permute-done
  3.9 1.0 copy-done.1
  4.9 0.9 copy-done.2
  5.8 0.9 copy-done.3
  6.8 0.9 copy-done.4
  7.6 0.9 copy-done.5
  8.5 4.9 %flow.1 = f32[16,8,128]{2,1,0:T(8,128)} custom-call(s32[8,2]{1,0:T(8,128)S(1)} %copy.28.peak_ref, bf16[8,128,128]{2,1,0:T(8,128)(2,1)S(1)} %bitcast.17, bf16[8,128,128]{2,1,0:T(8,128)(2,1)S(1)} %bitcast.18, bf16[144,256]{1,0:T(8,128)(2,1)S(1)} %copy-done.5, bf16[384,256]{1,0:T(8,128)(2,1)S(1)} %copy-done.3, bf16[768,256]{1,0:T(8,128)(2,1)S(1)} %copy-done.1, ...), custom_call_target="tpu_custom_call" | custom-call | tf_op jit(solution)/shard_map/flow/pallas_call | solution.py:265
  13.5 13.3 %all-to-all-start = ((f32[16,8,128]{2,1,0:T(8,128)}), f32[16,8,128]{2,1,0:T(8,128)S(1)}, u32[]{:S(2)}, u32[]{:S(2)}) async-start(f32[16,8,128]{2,1,0:T(8,128)} %flow.1), calls=%async_computation | async-start | bytes 131072 | tf_op jit(solution)/shard_map/all_to_all | solution.py:244
  26.8 0.0 copy-done.7
  26.9 0.1 convert_element_type.22
  26.9 0.7 copy.30
  27.6 7.1 %all-to-all-done.flow_ref = f32[16,8,128]{2,1,0:T(8,128)S(1)} async-done(((f32[16,8,128]{2,1,0:T(8,128)}), f32[16,8,128]{2,1,0:T(8,128)S(1)}, u32[]{:S(2)}, u32[]{:S(2)}) %all-to-all-start) | async-done | bytes 65568 | tf_op jit(solution)/shard_map/all_to_all | solution.py:244
  34.7 13.5 %all-to-all-start.1 = ((f32[32,1,128]{2,1,0:T(1,128)}), f32[32,1,128]{2,1,0:T(1,128)S(1)}, u32[]{:S(2)}, u32[]{:S(2)}) async-start(f32[32,1,128]{2,1,0:T(1,128)} %copy.30), calls=%async_computation.1 | async-start | bytes 32768 | tf_op jit(solution)/shard_map/all_to_all | solution.py:244
  48.2 0.7 constant_dynamic-slice_fusion.map_ref
  48.9 0.0 copy-done
  48.9 0.7 copy-done.6
  49.5 3.3 %render.1 = (f32[8,128]{1,0:T(8,128)S(1)}, bf16[32,32,512]{2,1,0:T(8,128)(2,1)}) custom-call(f32[1,16]{1,0:T(1,128)S(1)} %constant_dynamic-slice_fusion.map_ref, s32[2,2]{1,0:T(2,128)S(1)} %bitcast.20, f32[16,8,128]{2,1,0:T(8,128)S(1)} %all-to-all-done.flow_ref, bf16[2,512,512]{2,1,0:T(8,128)(2,1)S(1)} %bitcast.16), custom_call_target="tpu_custom_call" | custom-call | tf_op jit(solution)/shard_map/render/pallas_call | solution.py:276
  52.9 3.8 %all-to-all-done.1 = f32[32,1,128]{2,1,0:T(1,128)S(1)} async-done(((f32[32,1,128]{2,1,0:T(1,128)}), f32[32,1,128]{2,1,0:T(1,128)S(1)}, u32[]{:S(2)}, u32[]{:S(2)}) %all-to-all-start.1) | async-done | bytes 16416 | tf_op jit(solution)/shard_map/all_to_all | solution.py:244
  56.7 6.0 %all-to-all-start.2 = ((bf16[32,32,512]{2,1,0:T(8,128)(2,1)}), bf16[32,32,512]{2,1,0:T(8,128)(2,1)S(1)}, u32[]{:S(2)}, u32[]{:S(2)}) async-start(bf16[32,32,512]{2,1,0:T(8,128)(2,1)} %get-tuple-element.5), calls=%async_computation.2 | async-start | bytes 2097152 | tf_op jit(solution)/shard_map/all_to_all | solution.py:244
  62.7 0.1 fusion
  62.7 0.1 convert_element_type.26
  62.8 0.1 convert_reduce_fusion
  62.9 0.1 div.8.inverse_ref
  63.1 27.6 %all-to-all-done.2.piece_ref = bf16[32,32,512]{2,1,0:T(8,128)(2,1)S(1)} async-done(((bf16[32,32,512]{2,1,0:T(8,128)(2,1)}), bf16[32,32,512]{2,1,0:T(8,128)(2,1)S(1)}, u32[]{:S(2)}, u32[]{:S(2)}) %all-to-all-start.2) | async-done | bytes 1048608 | tf_op jit(solution)/shard_map/all_to_all | solution.py:244
  90.7 2.9 %gather.1 = bf16[32,32,512]{2,1,0:T(8,128)(2,1)} custom-call(s32[32,2]{1,0:T(8,128)S(1)} %bitcast.19, f32[32,2]{1,0:T(8,128)S(1)} %div.8.inverse_ref, bf16[32,32,512]{2,1,0:T(8,128)(2,1)S(1)} %all-to-all-done.2.piece_ref), custom_call_target="tpu_custom_call" | custom-call | tf_op jit(solution)/shard_map/gather/pallas_call | solution.py:290
  93.6 5.6 %all-to-all-start.3 = ((bf16[32,32,512]{2,1,0:T(8,128)(2,1)}), bf16[32,32,512]{2,1,0:T(8,128)(2,1)S(1)}, u32[]{:S(2)}, u32[]{:S(2)}) async-start(bf16[32,32,512]{2,1,0:T(8,128)(2,1)} %gather.1), calls=%async_computation.3 | async-start | bytes 2097152 | tf_op jit(solution)/shard_map/all_to_all | solution.py:244
  99.2 0.6 copy.29
  99.8 26.3 %all-to-all-done.3 = bf16[32,32,512]{2,1,0:T(8,128)(2,1)S(1)} async-done(((bf16[32,32,512]{2,1,0:T(8,128)(2,1)}), bf16[32,32,512]{2,1,0:T(8,128)(2,1)S(1)}, u32[]{:S(2)}, u32[]{:S(2)}) %all-to-all-start.3) | async-done | bytes 1048608 | tf_op jit(solution)/shard_map/all_to_all | solution.py:244
  126.2 1.1 copy.33
  (12 shorter events, 0.1 us)
Async XLA Ops:
  0.6 48.2 %copy-start = (bf16[1,2,512,512]{3,2,1,0:T(8,128)(2,1)S(1)}, bf16[1,2,512,512]{3,2,1,0:T(8,128)(2,1)}, u32[]{:S(2)}) copy-start(bf16[1,2,512,512]{3,2,1,0:T(8,128)(2,1)} %param.12) | copy-start | bytes 3145732
  0.6 3.2 %collective-permute-start = (bf16[1,8,128,128]{3,2,1,0:T(8,128)(2,1)}, bf16[1,8,128,128]{3,2,1,0:T(8,128)(2,1)S(1)}, u32[]{:S(2)}, u32[]{:S(2)}) collective-permute-start(bf16[1,8,128,128]{3,2,1,0:T(8,128)(2,1)} %param.10), channel_id=1, source_target_pairs={{0,32},{32,64},{64,96},{96,128},{128,160},{160,192},{192,224},{224... | collective-permute-start | bytes 786440 | tf_op jit(solution)/shard_map/ppermute | solution.py:255
  3.9 1.0 copy-start.1
  4.9 0.9 copy-start.2
  5.8 0.9 copy-start.3
  6.7 0.9 copy-start.4
  7.6 0.9 copy-start.5
  13.5 13.4 %copy-start.7 = (s32[1,64,1]{1,2,0:T(1,128)S(1)}, s32[1,64,1]{1,2,0:T(1,128)}, u32[]{:S(2)}) copy-start(s32[1,64,1]{1,2,0:T(1,128)} %param.14) | copy-start | bytes 772
  13.5 21.2 %all-to-all-start = ((f32[16,8,128]{2,1,0:T(8,128)}), f32[16,8,128]{2,1,0:T(8,128)S(1)}, u32[]{:S(2)}, u32[]{:S(2)}) async-start(f32[16,8,128]{2,1,0:T(8,128)} %flow.1), calls=%async_computation | async-start | bytes 131072 | tf_op jit(solution)/shard_map/all_to_all | solution.py:244
  34.7 22.0 %all-to-all-start.1 = ((f32[32,1,128]{2,1,0:T(1,128)}), f32[32,1,128]{2,1,0:T(1,128)S(1)}, u32[]{:S(2)}, u32[]{:S(2)}) async-start(f32[32,1,128]{2,1,0:T(1,128)} %copy.30), calls=%async_computation.1 | async-start | bytes 32768 | tf_op jit(solution)/shard_map/all_to_all | solution.py:244
  48.9 0.7 copy-start.6
  56.7 34.0 %all-to-all-start.2 = ((bf16[32,32,512]{2,1,0:T(8,128)(2,1)}), bf16[32,32,512]{2,1,0:T(8,128)(2,1)S(1)}, u32[]{:S(2)}, u32[]{:S(2)}) async-start(bf16[32,32,512]{2,1,0:T(8,128)(2,1)} %get-tuple-element.5), calls=%async_computation.2 | async-start | bytes 2097152 | tf_op jit(solution)/shard_map/all_to_all | solution.py:244
  93.6 32.6 %all-to-all-start.3 = ((bf16[32,32,512]{2,1,0:T(8,128)(2,1)}), bf16[32,32,512]{2,1,0:T(8,128)(2,1)S(1)}, u32[]{:S(2)}, u32[]{:S(2)}) async-start(bf16[32,32,512]{2,1,0:T(8,128)(2,1)} %gather.1), calls=%async_computation.3 | async-start | bytes 2097152 | tf_op jit(solution)/shard_map/all_to_all | solution.py:244

commit v2 on v1

--- a/solution.py
+++ b/solution.py
@@ -1,6 +1,3 @@
-import functools
-import math
-
 import jax
 import jax.numpy as jnp
 import numpy as np
@@ -48,7 +45,9 @@
     fourth = np.concatenate([weight * np.cos(angle), -weight * np.sin(angle)], 1)
     fourth_high, fourth_low = high_low(fourth / float(EXTENT * EXTENT))
     fourth = np.concatenate([fourth_high, fourth_high, fourth_low], 1)
-    return first, second, third, fourth
+    fourth = np.pad(fourth, ((0, 0), (0, 4 * EXTENT - fourth.shape[1])))
+    parts = [first, second, third, fourth[:, : 2 * EXTENT], fourth[:, 2 * EXTENT :]]
+    return np.concatenate(parts, 0)
 
 
 def relaxation_map(sections):
@@ -60,7 +59,11 @@
         lower[1:] = positions[:-1] + flow[1:] - positions[1:]
         upper[:-1] = positions[1:] - flow[1:] - positions[:-1]
         positions = positions + STEP_SIZE * (lower + upper - ANCHOR_WEIGHT * positions)
-    return positions.astype(np.float32)
+    line = np.arange(sections)
+    by_distance = positions[line[:, None], line[:, None] ^ line[None, :]]
+    table = np.zeros((sections, EXTENT), np.float32)
+    table[:, : 2 * sections] = np.repeat(by_distance, 2, axis=1)
+    return table
 
 
 def split(value):
@@ -72,8 +75,13 @@
     return jnp.dot(a, b, preferred_element_type=F32)
 
 
-def flow_kernel(peak_ref, now_ref, low_ref, first_ref, second_ref, third_ref, fourth_ref, out_ref):
+def flow_kernel(peak_ref, now_ref, low_ref, table_ref, out_ref):
     count = now_ref.shape[0]
+    ends = np.cumsum([0, 2 * HALF, 3 * EXTENT, 6 * EXTENT, 2 * REACH, 2 * REACH])
+    first_ref, second_ref, third_ref, left_ref, right_ref = (
+        table_ref.at[int(a) : int(b)] for a, b in zip(ends[:-1], ends[1:])
+    )
+    fourth = jnp.concatenate([left_ref[...], right_ref[:, : 6 * HALF - 2 * EXTENT]], 1)
     correlations = []
     for pair in range(count // 2):
         halves = []
@@ -101,7 +109,7 @@
             block = outer[HALF * k : HALF * (k + 1)]
             columns.append(jnp.concatenate([block[:, :EXTENT], block[:, EXTENT:]], 0))
         high, low = split(jnp.concatenate(columns, 1))
-        result = dot(fourth_ref[...], jnp.concatenate([high, low, high], 0))
+        result = dot(fourth, jnp.concatenate([high, low, high], 0))
         correlations += [result[:, :EXTENT], result[:, EXTENT:]]
 
     def energy(ref):
@@ -147,16 +155,20 @@
         peak_x = jnp.where(node == n, peak_ref[n, 1], peak_x)
     flow_y = peak_y.astype(F32) + total_y / total
     flow_x = peak_x.astype(F32) + total_x / total
-    flow = jnp.where(lane == 0, flow_y, jnp.where(lane == 1, flow_x, 0.0))
-    out_ref[...] = jnp.broadcast_to(flow[None], out_ref.shape)
+    out_ref[...] = jnp.where(lane == 0, flow_y, jnp.where(lane == 1, flow_x, 0.0))
+
+
+def taps(residual):
+    lane = lax.broadcasted_iota(jnp.int32, (1, EXTENT), 1)
+    away = (lane - BAND).astype(F32) - residual
+    raw = jnp.where(lane <= 2 * BAND, 1.0 / (1.0 + away * away), 0.0)
+    norm = jnp.sum(raw, axis=1, keepdims=True)
+    return raw / norm, norm
 
 
 def fill_band(target_ref, residual, offset, sub_sign):
     block = 128
-    lane = lax.broadcasted_iota(jnp.int32, (1, block), 1)
-    tap = (lane - BAND).astype(F32) - residual
-    raw = jnp.where(lane <= 2 * BAND, 1.0 / (1.0 + tap * tap), 0.0)
-    norm = jnp.sum(raw, axis=1, keepdims=True)
+    _, norm = taps(residual)
     a = lax.broadcasted_iota(jnp.int32, (block, block), 0)
     b = lax.broadcasted_iota(jnp.int32, (block, block), 1)
     d = sub_sign * (a - b) - offset
@@ -176,47 +188,119 @@
             )
 
 
-def render_kernel(map_ref, band_ref, flow_ref, tile_ref, position_ref, send_ref, col_ref, row_ref, pass_ref):
-    sections, nodes, _ = flow_ref.shape
-    tile_count, edge, _ = tile_ref.shape
-    position = jnp.zeros(flow_ref.shape[1:], F32)
-    for s in range(sections):
-        position = position + map_ref[0, s] * flow_ref[s]
-    position_ref[...] = position
-    per_tile = nodes // tile_count
-    height = edge // PIECES
+def early_kernel(band_ref, route_ref, tile_ref, send_ref):
+    slots, rows, edge = send_ref.shape
+    height = edge // slots
+    wide = height + 2 * BAND
+    per_chunk = 128 // rows
+    offset_y, offset_x = band_ref[0, 0], band_ref[0, 1]
+    lane = lax.broadcasted_iota(jnp.int32, (slots, EXTENT), 1)
+    info = jnp.where(
+        lane == 0,
+        route_ref[:slots, :],
+        jnp.where(lane == 1, route_ref[slots : 2 * slots, :], jnp.where(lane == 2, offset_x, 0)),
+    )
+    info = info.astype(F32).astype(BF)
+    a = lax.broadcasted_iota(jnp.int32, (128, edge), 0)
+    m = lax.broadcasted_iota(jnp.int32, (128, edge), 1)
+    row = a & (rows - 1)
+    source = jnp.where(row < wide, (a // rows) * height + row + offset_y - BAND, -edge)
+    a = a[:, :slots]
+    m_slot = m[:, :slots]
+    for c in range(slots // per_chunk):
+        pick = jnp.where(m == source + c * per_chunk * height, 1.0, 0.0).astype(BF)
+        data = dot(pick, tile_ref[...])
+        named = jnp.where(((a & (rows - 1)) == wide) & (a // rows + c * per_chunk == m_slot), 1.0, 0.0)
+        left = data[:, :EXTENT] + dot(named.astype(BF), info)
+        data = jnp.concatenate([left, data[:, EXTENT:]], 1).astype(BF)
+        send_ref[c * per_chunk : (c + 1) * per_chunk] = data.reshape(per_chunk, rows, edge)
+
+
+def late_kernel(band_ref, coef_ref, flow_ref, tile_ref, position_ref, send_ref, col_ref, row_ref, pass_ref):
+    nodes = flow_ref.shape[0]
+    edge = tile_ref.shape[0]
+    slots = send_ref.shape[0]
+    height = edge // slots
+    lane = lax.broadcasted_iota(jnp.int32, flow_ref.shape, 1)
+    terms = flow_ref[...] * coef_ref[...]
+    odd = (lane & 1) == 1
+    position_y = jnp.sum(jnp.where(odd, 0.0, terms), axis=1, keepdims=True)
+    position_x = jnp.sum(jnp.where(odd, terms, 0.0), axis=1, keepdims=True)
+    position_ref[...] = jnp.where(lane == 0, position_y, jnp.where(lane == 1, position_x, 0.0))
+
+    def residuals(t):
+        result = []
+        for c, position in enumerate((position_y, position_x)):
+            half = nodes // 2
+            mean = jnp.sum(position[t * half : (t + 1) * half], axis=0, keepdims=True)
+            result.append((MIP_SCALE / half) * mean - band_ref[t, c].astype(F32))
+        return result
+
+    residual_y, residual_x = residuals(1)
+    fill_band(col_ref, residual_x, band_ref[1, 1], 1)
+    fill_band(row_ref, residual_y, band_ref[1, 0], -1)
     chunk = 128
-    for t in range(tile_count):
-        mean = jnp.sum(position[t * per_tile : (t + 1) * per_tile], axis=0, keepdims=True)
-        shift = (MIP_SCALE / per_tile) * mean
-        offset_y, offset_x = band_ref[t, 0], band_ref[t, 1]
-        fill_band(col_ref, shift[:, 1:2] - offset_x.astype(F32), offset_x, 1)
-        fill_band(row_ref, shift[:, 0:1] - offset_y.astype(F32), offset_y, -1)
-        for c in range(edge // chunk):
-            rows = slice(c * chunk, (c + 1) * chunk)
-            pass_ref[rows, :] = dot(tile_ref[t, rows, :], col_ref[...]).astype(BF)
-        for c in range(edge // chunk):
-            rows = slice(c * chunk, (c + 1) * chunk)
-            done = dot(row_ref[rows, :], pass_ref[...]).astype(BF)
-            send_ref[c * chunk // height : (c + 1) * chunk // height, t * height : (t + 1) * height, :] = (
-                done.reshape(chunk // height, height, edge)
-            )
-
-
-def gather_kernel(label_ref, inverse_ref, piece_ref, out_ref, total_ref):
-    owners, rows, _ = piece_ref.shape
+    for c in range(edge // chunk):
+        rows = slice(c * chunk, (c + 1) * chunk)
+        pass_ref[rows, :] = dot(tile_ref[rows, :], col_ref[...]).astype(BF)
+    for c in range(edge // chunk):
+        rows = slice(c * chunk, (c + 1) * chunk)
+        first, last = c * chunk // height, (c + 1) * chunk // height
+        done = dot(row_ref[rows, :], pass_ref[...]).astype(BF).reshape(last - first, height, edge)
+        for j in range(edge // EXTENT):
+            send_ref[first:last, j * height : (j + 1) * height, :] = done[
+                :, :, j * EXTENT : (j + 1) * EXTENT
+            ]
+    residual_y, residual_x = residuals(0)
+    sub = lax.broadcasted_iota(jnp.int32, (8, EXTENT), 0)
+    tail = jnp.where(sub == 0, taps(residual_x)[0], jnp.where(sub == 1, taps(residual_y)[0], 0.0))
+    first = height * edge // EXTENT
+    send_ref[:, first : first + 8, :] = jnp.broadcast_to(tail.astype(BF)[None], (slots, 8, EXTENT))
+
+
+def gather_kernel(info_ref, inverse_ref, raw_ref, late_ref, out_ref, total_ref):
+    owners, rows, edge = raw_ref.shape
     groups, height, _ = total_ref.shape
     total_ref[...] = jnp.zeros(total_ref.shape, F32)
-    per_owner = rows // height
-
-    def add(owner, carry):
-        for t in range(per_owner):
-            group = label_ref[owner, t]
-            piece = piece_ref[owner, t * height : (t + 1) * height, :].astype(F32)
-            total_ref[group] = total_ref[group] + piece
-        return carry
-
-    lax.fori_loop(0, owners, add, 0)
+    blocks = edge // EXTENT
+    tail = height * blocks
+    batch = 2 * EXTENT // rows
+    for start in range(0, owners, batch):
+        bands, columns = [], []
+        for d in range(start, start + batch):
+            info = late_ref[d, tail : tail + 8, :].astype(F32)
+            columns.append(info[0:1])
+            place = d - start
+            band = pltpu.roll(
+                jnp.broadcast_to(info[1:2], (height, EXTENT)),
+                place % (batch // 2) * rows,
+                1,
+                stride=1,
+                stride_axis=0,
+            )
+            empty = jnp.zeros_like(band)
+            bands.append(
+                jnp.concatenate([band, empty] if place < batch // 2 else [empty, band], 1)
+            )
+        raw = raw_ref[start : start + batch].reshape(batch * rows, edge)
+        lines = dot(jnp.concatenate(bands, 0).astype(BF), raw).astype(BF).astype(F32)
+        for d in range(start, start + batch):
+            line = lines[(d - start) * height : (d - start + 1) * height]
+            line = jnp.concatenate([line, jnp.zeros((height, EXTENT), F32)], 1)
+            length = edge + EXTENT
+            line = pltpu.roll(line, (length + BAND - info_ref[d, 2]) % length, 1)
+            total = None
+            for k in range(2 * BAND + 1):
+                moved = line if k == 0 else pltpu.roll(line, length - k, 1)
+                term = moved[:, :edge] * columns[d - start][:, k : k + 1]
+                total = term if total is None else total + term
+            group = info_ref[d, 0]
+            total_ref[group] = total_ref[group] + total.astype(BF).astype(F32)
+            group = info_ref[d, 1]
+            for j in range(blocks):
+                piece = late_ref[d, j * height : (j + 1) * height, :].astype(F32)
+                lanes = slice(j * EXTENT, (j + 1) * EXTENT)
+                total_ref[group, :, lanes] = total_ref[group, :, lanes] + piece
     share = groups // owners
 
     def finish(owner, carry):
@@ -248,54 +332,64 @@
     sections = lax.axis_size("gz")
     owners = lax.axis_size("xy")
     section = lax.axis_index("gz")
-    tile_count, edge = tiles.shape[1], tiles.shape[-1]
+    edge = tiles.shape[-1]
     height = edge // PIECES
     groups = 2 * owners
-
-    below = lax.ppermute(patches, "gz", [(i, i + 1) for i in range(sections - 1)])
-    label = routes[0, :, 0].reshape(tile_count, PIECES).T.astype(F32)
-    label = jnp.pad(label, ((0, 0), (0, EXTENT - tile_count)))[:, None, :]
-    label = exchange(label, "xy")[:, 0, :tile_count].astype(jnp.int32)
-    match = label.reshape(-1)[:, None] == jnp.arange(groups, dtype=jnp.int32)[None, :]
+    count = patches.shape[1]
+
+    raw = pl.pallas_call(
+        early_kernel,
+        out_shape=jax.ShapeDtypeStruct((PIECES, 2 * height, edge), BF),
+        in_specs=[in_smem(), in_vmem(), in_vmem()],
+        out_specs=in_vmem(),
+        compiler_params=params(),
+        name="early",
+    )(band_offsets[0], routes[0], tiles[0, 0])
+    raw = exchange(raw, "xy")
+    info = raw[:, height + 2 * BAND, :3].astype(jnp.int32)
+    match = info[:, :2].reshape(-1)[:, None] == jnp.arange(groups, dtype=jnp.int32)[None, :]
     inverse = 1.0 / jnp.maximum(jnp.sum(match.astype(F32), axis=0), 1.0)
     inverse = inverse.reshape(owners, groups // owners)
 
-    tables = [jnp.asarray(t) for t in dft_constants()]
-    count = patches.shape[1]
+    below = lax.ppermute(patches, "gz", [(i, i + 1) for i in range(sections - 1)])
     flow = pl.pallas_call(
         flow_kernel,
-        out_shape=jax.ShapeDtypeStruct((sections, count, EXTENT), F32),
-        in_specs=[in_smem()] + [in_vmem()] * 6,
+        out_shape=jax.ShapeDtypeStruct((count, EXTENT), F32),
+        in_specs=[in_smem()] + [in_vmem()] * 3,
         out_specs=in_vmem(),
         compiler_params=params(),
         name="flow",
-    )(peak_offsets[0], patches[0], below[0], *tables)
-    flow = exchange(flow, "gz")
-
-    linear = lax.dynamic_slice_in_dim(jnp.asarray(relaxation_map(sections)), section, 1, 0)
-    position, pieces = pl.pallas_call(
-        render_kernel,
+    )(peak_offsets[0], patches[0], below[0], jnp.asarray(dft_constants()))
+    distance = 1
+    while distance < sections:
+        other = lax.ppermute(flow, "gz", [(i, i ^ distance) for i in range(sections)])
+        flow = flow + jnp.pad(other[:, : EXTENT - 2 * distance], ((0, 0), (2 * distance, 0)))
+        distance *= 2
+
+    coef = lax.dynamic_slice_in_dim(jnp.asarray(relaxation_map(sections)), section, 1, 0)
+    position, late = pl.pallas_call(
+        late_kernel,
         out_shape=(
             jax.ShapeDtypeStruct((count, EXTENT), F32),
-            jax.ShapeDtypeStruct((PIECES, tile_count * height, edge), BF),
+            jax.ShapeDtypeStruct((PIECES, height * edge // EXTENT + 8, EXTENT), BF),
         ),
-        in_specs=[in_smem(), in_smem(), in_vmem(), in_vmem()],
+        in_specs=[in_smem()] + [in_vmem()] * 3,
         out_specs=(in_vmem(), in_vmem()),
         scratch_shapes=[pltpu.VMEM((edge, edge), BF)] * 3,
         compiler_params=params(),
-        name="render",
-    )(linear, band_offsets[0], flow, tiles[0])
-    pieces = exchange(pieces, "xy")
+        name="late",
+    )(band_offsets[0], coef, flow, tiles[0, 1])
+    late = exchange(late, "xy")
 
     cells = pl.pallas_call(
         gather_kernel,
         out_shape=jax.ShapeDtypeStruct((owners, groups // owners * height, edge), BF),
-        in_specs=[in_smem(), in_smem(), in_vmem()],
+        in_specs=[in_smem(), in_smem(), in_vmem(), in_vmem()],
         out_specs=in_vmem(),
         scratch_shapes=[pltpu.VMEM((groups, height, edge), F32)],
         compiler_params=params(),
         name="gather",
-    )(label, inverse, pieces)
+    )(info, inverse, raw, late)
     cells = exchange(cells, "xy")
     rendered = cells.reshape(PIECES, groups // owners, height, edge).transpose(1, 0, 2, 3)
     rendered = rendered.reshape(1, groups // owners, edge, edge)

time: 128 us -> 126 us (0.984)
  waiting for transfers between devices: 65.4 us -> 45.3 us
  starting transfers between devices: 40.2 us -> 55.4 us
  Pallas kernels: 11.2 us -> 17.6 us
  local copies, waits for them, and re-layouts: 9.44 us -> 5.64 us
    all_to_all x4 -> x3, waiting for transfers between devices: 64.8 us -> 39.4 us  [exchange(): return lax.all_to_all(value, axis, split_axis=0, concat_axis=0, tiled=True)]
    ppermute x0 -> x4, starting transfers between devices: none -> 25.1 us  [body(): lax.ppermute(flow, 'gz', [(i, i ^ distance) for i in range(sections)])]
    all_to_all x4 -> x3, starting transfers between devices: 38.3 us -> 28.9 us  [exchange(): return lax.all_to_all(value, axis, split_axis=0, concat_axis=0, tiled=True)]
    pallas_call x1, Pallas kernels: 2.91 us -> 8.42 us  [body(): pl.pallas_call(gather_kernel, out_shape=jax.ShapeDtypeStruct((owners, gro...]
    ppermute x0 -> x4, waiting for transfers between devices: none -> 4.81 us  [body(): lax.ppermute(flow, 'gz', [(i, i ^ distance) for i in range(sections)])]
    unnamed x16 -> x10, local copies, waits for them, and re-layouts: 5.32 us -> 1.34 us
    squeeze x0 -> x2, local copies, waits for them, and re-layouts: none -> 1.36 us  [the longest x1 1.27 us: body(): tiles[0, 0]]
    pallas_call x2 -> x3, Pallas kernels: 8.27 us -> 9.13 us  [the longest x1 4.3 us: body(): pl.pallas_call(flow_kernel, out_shape=jax.ShapeDtypeStruct((count, EXTENT...]
  transfers between devices with their start and end apart: 5 -> 8, of which waited for: 5 -> 7; matrix products, arithmetic and copies ran while one was open for 3% -> 2% of each run, Pallas kernels for 3% -> 5%
where the time goes in v2:
time: 126 us; the launch traced here: 125 us
  starting transfers between devices  55.4 us (44%)
  waiting for transfers between devices  45.3 us (36%)
  Pallas kernels  17.6 us (14%)
  local copies, waits for them, and re-layouts  5.64 us (4%)
    all_to_all x3, waiting for transfers between devices, exchange(): return lax.all_to_all(value, axis, split_axis=0, concat_axis=0, tiled=True)  39.4 us
    all_to_all x3, starting transfers between devices, exchange(): return lax.all_to_all(value, axis, split_axis=0, concat_axis=0, tiled=True)  28.9 us
    ppermute x4, starting transfers between devices, body(): lax.ppermute(flow, 'gz', [(i, i ^ distance) for i in range(sections)])  25.1 us
    pallas_call x1, Pallas kernels, body(): pl.pallas_call(gather_kernel, out_shape=jax.ShapeDtypeStruct((owners, gro...  8.42 us
    ppermute x4, waiting for transfers between devices, body(): lax.ppermute(flow, 'gz', [(i, i ^ distance) for i in range(sections)])  4.81 us
    pallas_call x1, Pallas kernels, body(): pl.pallas_call(flow_kernel, out_shape=jax.ShapeDtypeStruct((count, EXTENT...  4.3 us
  transfers between devices with their start and end apart: 8, of which 7 were waited for; matrix products, arithmetic and copies ran while one was open for 2% of the time, Pallas kernels for 5%

profile of v2, /device:TPU:2, one launch (start us, length us, event | category | flops | bytes accessed | tf_op | source)
XLA Modules:
  0.0 125.1 jit_solution(1921470401296563672)
XLA Ops:
  0.6 0.6 copy-done.4
  1.3 0.1 copy.32.route_ref
  1.4 1.3 %slice_bitcast_fusion = (bf16[512,512]{1,0:T(8,128)(2,1)S(1)}, bf16[512,512]{1,0:T(8,128)(2,1)S(1)}) fusion(bf16[1,2,512,512]{3,2,1,0:T(8,128)(2,1)} %param.9), kind=kLoop, calls=%fused_computation | loop fusion | bytes 2097152 | tf_op jit(solution)/shard_map/squeeze | solution.py:347
  2.7 0.7 copy-done.2
  3.3 2.4 %early.1 = bf16[32,32,512]{2,1,0:T(8,128)(2,1)} custom-call(s32[2,2]{1,0:T(2,128)S(1)} %bitcast.23, s32[64,1]{1,0:T(8,128)S(1)} %copy.32.route_ref, bf16[512,512]{1,0:T(8,128)(2,1)S(1)} %get-tuple-element.6.tile_ref), custom_call_target="tpu_custom_call" | custom-call | tf_op jit(solution)/shard_map/early/pallas_call | solution.py:340
  5.8 13.6 %all-to-all-start = ((bf16[32,32,512]{2,1,0:T(8,128)(2,1)}), bf16[32,32,512]{2,1,0:T(8,128)(2,1)S(1)}, u32[]{:S(2)}, u32[]{:S(2)}) async-start(bf16[32,32,512]{2,1,0:T(8,128)(2,1)} %early.1), calls=%async_computation | async-start | bytes 2097152 | tf_op jit(solution)/shard_map/all_to_all | solution.py:328
  19.4 1.3 %collective-permute-start = (bf16[1,8,128,128]{3,2,1,0:T(8,128)(2,1)S(1)}, bf16[1,8,128,128]{3,2,1,0:T(8,128)(2,1)S(1)}, u32[]{:S(2)}, u32[]{:S(2)}) collective-permute-start(bf16[1,8,128,128]{3,2,1,0:T(8,128)(2,1)S(1)} %copy-done.1), channel_id=1, source_target_pairs={{0,32},{32,64},{64,96},{96,128},{128,160},{160,192},{192,224},{224... | collective-permute-start | bytes 786440 | tf_op jit(solution)/shard_map/ppermute | solution.py:354
  20.7 0.1 copy.30.peak_ref
  20.8 1.0 collective-permute-done
  21.9 4.3 %flow.1 = f32[8,128]{1,0:T(8,128)S(1)} custom-call(s32[8,2]{1,0:T(8,128)S(1)} %copy.30.peak_ref, bf16[8,128,128]{2,1,0:T(8,128)(2,1)S(1)} %bitcast.21, bf16[8,128,128]{2,1,0:T(8,128)(2,1)S(1)} %bitcast.22, bf16[1456,256]{1,0:T(8,128)(2,1)S(1)} %copy-done), custom_call_target="tpu_custom_call" | custom-call | tf_op jit(solution)/shard_map/flow/pallas_call | solution.py:355
  26.2 6.4 %collective-permute-start.1 = (f32[8,128]{1,0:T(8,128)S(1)}, f32[8,128]{1,0:T(8,128)S(1)}, u32[]{:S(2)}, u32[]{:S(2)}) collective-permute-start(f32[8,128]{1,0:T(8,128)S(1)} %flow.1), channel_id=1, source_target_pairs={{0,32},{32,0},{64,96},{96,64},{128,160},{160,128},{192,224},{224,1... | collective-permute-start | bytes 12296 | tf_op jit(solution)/shard_map/ppermute | solution.py:365
  32.5 0.8 collective-permute-done.1
  33.4 4.6 %collective-permute-start.2 = (f32[8,128]{1,0:T(8,128)S(1)}, f32[8,128]{1,0:T(8,128)S(1)}, u32[]{:S(2)}, u32[]{:S(2)}) collective-permute-start(f32[8,128]{1,0:T(8,128)S(1)} %pad_add_fusion.3), channel_id=1, source_target_pairs={{0,64},{32,96},{64,0},{96,32},{128,192},{160,224},{192,128},{224,1... | collective-permute-start | bytes 12296 | tf_op jit(solution)/shard_map/ppermute | solution.py:365
  38.0 1.6 %collective-permute-done.2 = f32[8,128]{1,0:T(8,128)S(1)} collective-permute-done((f32[8,128]{1,0:T(8,128)S(1)}, f32[8,128]{1,0:T(8,128)S(1)}, u32[]{:S(2)}, u32[]{:S(2)}) %collective-permute-start.2) | collective-permute-done | bytes 4128 | tf_op jit(solution)/shard_map/ppermute | solution.py:365
  39.7 4.9 %collective-permute-start.3 = (f32[8,128]{1,0:T(8,128)S(1)}, f32[8,128]{1,0:T(8,128)S(1)}, u32[]{:S(2)}, u32[]{:S(2)}) collective-permute-start(f32[8,128]{1,0:T(8,128)S(1)} %pad_add_fusion.2), channel_id=1, source_target_pairs={{0,128},{32,160},{64,192},{96,224},{128,0},{160,32},{192,64},{224,... | collective-permute-start | bytes 12296 | tf_op jit(solution)/shard_map/ppermute | solution.py:365
  44.6 1.6 %collective-permute-done.3 = f32[8,128]{1,0:T(8,128)S(1)} collective-permute-done((f32[8,128]{1,0:T(8,128)S(1)}, f32[8,128]{1,0:T(8,128)S(1)}, u32[]{:S(2)}, u32[]{:S(2)}) %collective-permute-start.3) | collective-permute-done | bytes 4128 | tf_op jit(solution)/shard_map/ppermute | solution.py:365
  46.2 9.3 %collective-permute-start.4 = (f32[8,128]{1,0:T(8,128)S(1)}, f32[8,128]{1,0:T(8,128)S(1)}, u32[]{:S(2)}, u32[]{:S(2)}) collective-permute-start(f32[8,128]{1,0:T(8,128)S(1)} %pad_add_fusion.1), channel_id=1, source_target_pairs={{0,256},{32,288},{64,320},{96,352},{128,384},{160,416},{192,448},{... | collective-permute-start | bytes 12296 | tf_op jit(solution)/shard_map/ppermute | solution.py:365
  55.5 0.7 constant_dynamic-slice_fusion.coef_ref
  56.2 0.9 collective-permute-done.4
  57.1 2.4 %late.1 = (f32[8,128]{1,0:T(8,128)S(1)}, bf16[32,72,128]{2,1,0:T(8,128)(2,1)}) custom-call(s32[2,2]{1,0:T(2,128)S(1)} %bitcast.24, f32[1,128]{1,0:T(1,128)S(1)} %constant_dynamic-slice_fusion.coef_ref, f32[8,128]{1,0:T(8,128)S(1)} %pad_add_fusion.flow_ref, bf16[512,512]{1,0:T(8,128)(2,1)S(1)} %get-tuple-element.7.tile_ref), custom_call_target="tpu_custom_call" | custom-call | tf_op jit(solution)/shard_map/late/pallas_call | solution.py:370
  59.5 9.8 %all-to-all-start.1 = ((bf16[32,72,128]{2,1,0:T(8,128)(2,1)}), bf16[32,72,128]{2,1,0:T(8,128)(2,1)S(1)}, u32[]{:S(2)}, u32[]{:S(2)}) async-start(bf16[32,72,128]{2,1,0:T(8,128)(2,1)} %get-tuple-element.5), calls=%async_computation.1 | async-start | bytes 1179648 | tf_op jit(solution)/shard_map/all_to_all | solution.py:328
  69.4 0.1 copy.35.info_ref
  69.5 0.1 copy.34
  69.6 0.1 eq.15
  69.7 0.1 convert_reduce_fusion
  69.8 0.1 div.8.inverse_ref
  69.9 15.1 %all-to-all-done.1.late_ref = bf16[32,72,128]{2,1,0:T(8,128)(2,1)S(1)} async-done(((bf16[32,72,128]{2,1,0:T(8,128)(2,1)}), bf16[32,72,128]{2,1,0:T(8,128)(2,1)S(1)}, u32[]{:S(2)}, u32[]{:S(2)}) %all-to-all-start.1) | async-done | bytes 589856 | tf_op jit(solution)/shard_map/all_to_all | solution.py:328
  85.0 8.4 %gather.1 = bf16[32,32,512]{2,1,0:T(8,128)(2,1)} custom-call(s32[32,3]{1,0:T(8,128)S(1)} %copy.35.info_ref, f32[32,2]{1,0:T(8,128)S(1)} %div.8.inverse_ref, bf16[32,32,512]{2,1,0:T(8,128)(2,1)S(1)} %all-to-all-done.raw_ref, bf16[32,72,128]{2,1,0:T(8,128)(2,1)S(1)} %all-to-all-done.1.late_ref), custom_call_target="tpu_custom_call" | custom-call | tf_op jit(solution)/shard_map/gather/pallas_call | solution.py:384
  93.4 5.6 %all-to-all-start.2 = ((bf16[32,32,512]{2,1,0:T(8,128)(2,1)}), bf16[32,32,512]{2,1,0:T(8,128)(2,1)S(1)}, u32[]{:S(2)}, u32[]{:S(2)}) async-start(bf16[32,32,512]{2,1,0:T(8,128)(2,1)} %gather.1), calls=%async_computation.2 | async-start | bytes 2097152 | tf_op jit(solution)/shard_map/all_to_all | solution.py:328
  99.0 0.6 copy.31
  99.7 24.3 %all-to-all-done.2 = bf16[32,32,512]{2,1,0:T(8,128)(2,1)S(1)} async-done(((bf16[32,32,512]{2,1,0:T(8,128)(2,1)}), bf16[32,32,512]{2,1,0:T(8,128)(2,1)S(1)}, u32[]{:S(2)}, u32[]{:S(2)}) %all-to-all-start.2) | async-done | bytes 1048608 | tf_op jit(solution)/shard_map/all_to_all | solution.py:328
  124.0 1.1 copy.36
  (18 shorter events, 0.4 us)
Async XLA Ops:
  0.6 0.7 copy-start.4
  2.7 0.7 copy-start.2
  5.8 13.6 %copy-start.1 = (bf16[1,8,128,128]{3,2,1,0:T(8,128)(2,1)S(1)}, bf16[1,8,128,128]{3,2,1,0:T(8,128)(2,1)}, u32[]{:S(2)}) copy-start(bf16[1,8,128,128]{3,2,1,0:T(8,128)(2,1)} %param.7) | copy-start | bytes 786436
  5.8 16.1 %copy-start = (bf16[1456,256]{1,0:T(8,128)(2,1)S(1)}, bf16[1456,256]{1,0:T(8,128)(2,1)}, u32[]{:S(2)}) copy-start(bf16[1456,256]{1,0:T(8,128)(2,1)} %constant.19.clone.table_ref) | copy-start | bytes 2236420
  5.8 53.7 %all-to-all-start = ((bf16[32,32,512]{2,1,0:T(8,128)(2,1)}), bf16[32,32,512]{2,1,0:T(8,128)(2,1)S(1)}, u32[]{:S(2)}, u32[]{:S(2)}) async-start(bf16[32,32,512]{2,1,0:T(8,128)(2,1)} %early.1), calls=%async_computation | async-start | bytes 2097152 | tf_op jit(solution)/shard_map/all_to_all | solution.py:328
  19.4 1.3 %copy-start.3 = (s32[1,8,2]{1,2,0:T(2,128)S(1)}, s32[1,8,2]{1,2,0:T(2,128)}, u32[]{:S(2)}) copy-start(s32[1,8,2]{1,2,0:T(2,128)} %param.8) | copy-start | bytes 196
  19.4 2.4 %collective-permute-start = (bf16[1,8,128,128]{3,2,1,0:T(8,128)(2,1)S(1)}, bf16[1,8,128,128]{3,2,1,0:T(8,128)(2,1)S(1)}, u32[]{:S(2)}, u32[]{:S(2)}) collective-permute-start(bf16[1,8,128,128]{3,2,1,0:T(8,128)(2,1)S(1)} %copy-done.1), channel_id=1, source_target_pairs={{0,32},{32,64},{64,96},{96,128},{128,160},{160,192},{192,224},{224... | collective-permute-start | bytes 786440 | tf_op jit(solution)/shard_map/ppermute | solution.py:354
  26.2 7.2 %collective-permute-start.1 = (f32[8,128]{1,0:T(8,128)S(1)}, f32[8,128]{1,0:T(8,128)S(1)}, u32[]{:S(2)}, u32[]{:S(2)}) collective-permute-start(f32[8,128]{1,0:T(8,128)S(1)} %flow.1), channel_id=1, source_target_pairs={{0,32},{32,0},{64,96},{96,64},{128,160},{160,128},{192,224},{224,1... | collective-permute-start | bytes 12296 | tf_op jit(solution)/shard_map/ppermute | solution.py:365
  33.4 6.2 %collective-permute-start.2 = (f32[8,128]{1,0:T(8,128)S(1)}, f32[8,128]{1,0:T(8,128)S(1)}, u32[]{:S(2)}, u32[]{:S(2)}) collective-permute-start(f32[8,128]{1,0:T(8,128)S(1)} %pad_add_fusion.3), channel_id=1, source_target_pairs={{0,64},{32,96},{64,0},{96,32},{128,192},{160,224},{192,128},{224,1... | collective-permute-start | bytes 12296 | tf_op jit(solution)/shard_map/ppermute | solution.py:365
  39.7 6.5 %collective-permute-start.3 = (f32[8,128]{1,0:T(8,128)S(1)}, f32[8,128]{1,0:T(8,128)S(1)}, u32[]{:S(2)}, u32[]{:S(2)}) collective-permute-start(f32[8,128]{1,0:T(8,128)S(1)} %pad_add_fusion.2), channel_id=1, source_target_pairs={{0,128},{32,160},{64,192},{96,224},{128,0},{160,32},{192,64},{224,... | collective-permute-start | bytes 12296 | tf_op jit(solution)/shard_map/ppermute | solution.py:365
  46.2 10.8 %collective-permute-start.4 = (f32[8,128]{1,0:T(8,128)S(1)}, f32[8,128]{1,0:T(8,128)S(1)}, u32[]{:S(2)}, u32[]{:S(2)}) collective-permute-start(f32[8,128]{1,0:T(8,128)S(1)} %pad_add_fusion.1), channel_id=1, source_target_pairs={{0,256},{32,288},{64,320},{96,352},{128,384},{160,416},{192,448},{... | collective-permute-start | bytes 12296 | tf_op jit(solution)/shard_map/ppermute | solution.py:365
  59.5 25.5 %all-to-all-start.1 = ((bf16[32,72,128]{2,1,0:T(8,128)(2,1)}), bf16[32,72,128]{2,1,0:T(8,128)(2,1)S(1)}, u32[]{:S(2)}, u32[]{:S(2)}) async-start(bf16[32,72,128]{2,1,0:T(8,128)(2,1)} %get-tuple-element.5), calls=%async_computation.1 | async-start | bytes 1179648 | tf_op jit(solution)/shard_map/all_to_all | solution.py:328
  93.4 30.6 %all-to-all-start.2 = ((bf16[32,32,512]{2,1,0:T(8,128)(2,1)}), bf16[32,32,512]{2,1,0:T(8,128)(2,1)S(1)}, u32[]{:S(2)}, u32[]{:S(2)}) async-start(bf16[32,32,512]{2,1,0:T(8,128)(2,1)} %gather.1), calls=%async_computation.2 | async-start | bytes 2097152 | tf_op jit(solution)/shard_map/all_to_all | solution.py:328

commit v3 on v1

--- a/solution.py
+++ b/solution.py
@@ -1,6 +1,3 @@
-import functools
-import math
-
 import jax
 import jax.numpy as jnp
 import numpy as np
@@ -48,7 +45,9 @@
     fourth = np.concatenate([weight * np.cos(angle), -weight * np.sin(angle)], 1)
     fourth_high, fourth_low = high_low(fourth / float(EXTENT * EXTENT))
     fourth = np.concatenate([fourth_high, fourth_high, fourth_low], 1)
-    return first, second, third, fourth
+    fourth = np.pad(fourth, ((0, 0), (0, 4 * EXTENT - fourth.shape[1])))
+    parts = [first, second, third, fourth[:, : 2 * EXTENT], fourth[:, 2 * EXTENT :]]
+    return np.concatenate(parts, 0)
 
 
 def relaxation_map(sections):
@@ -72,8 +71,13 @@
     return jnp.dot(a, b, preferred_element_type=F32)
 
 
-def flow_kernel(peak_ref, now_ref, low_ref, first_ref, second_ref, third_ref, fourth_ref, out_ref):
+def flow_kernel(peak_ref, now_ref, low_ref, table_ref, out_ref):
     count = now_ref.shape[0]
+    ends = np.cumsum([0, 2 * HALF, 3 * EXTENT, 6 * EXTENT, 2 * REACH, 2 * REACH])
+    first_ref, second_ref, third_ref, left_ref, right_ref = (
+        table_ref.at[int(a) : int(b)] for a, b in zip(ends[:-1], ends[1:])
+    )
+    fourth = jnp.concatenate([left_ref[...], right_ref[:, : 6 * HALF - 2 * EXTENT]], 1)
     correlations = []
     for pair in range(count // 2):
         halves = []
@@ -101,7 +105,7 @@
             block = outer[HALF * k : HALF * (k + 1)]
             columns.append(jnp.concatenate([block[:, :EXTENT], block[:, EXTENT:]], 0))
         high, low = split(jnp.concatenate(columns, 1))
-        result = dot(fourth_ref[...], jnp.concatenate([high, low, high], 0))
+        result = dot(fourth, jnp.concatenate([high, low, high], 0))
         correlations += [result[:, :EXTENT], result[:, EXTENT:]]
 
     def energy(ref):
@@ -118,8 +122,8 @@
     column = lax.broadcasted_iota(jnp.int32, shape, 1)
     scores, relatives, tops = [], [], []
     for n in range(count):
-        rel_y = row - peak_ref[n, 0]
-        rel_x = ((column - peak_ref[n, 1] + EXTENT // 2) & (EXTENT - 1)) - EXTENT // 2
+        rel_y = row - peak_ref[0, n]
+        rel_x = ((column - peak_ref[1, n] + EXTENT // 2) & (EXTENT - 1)) - EXTENT // 2
         quarter = EXTENT // 4
         inside = (rel_y >= -quarter) & (rel_y < quarter) & (rel_x >= -quarter) & (rel_x < quarter)
         score = jnp.where(inside, correlations[n] * scale[n : n + 1], -1e30)
@@ -143,8 +147,8 @@
     peak_y = jnp.zeros((count, EXTENT), jnp.int32)
     peak_x = jnp.zeros((count, EXTENT), jnp.int32)
     for n in range(count):
-        peak_y = jnp.where(node == n, peak_ref[n, 0], peak_y)
-        peak_x = jnp.where(node == n, peak_ref[n, 1], peak_x)
+        peak_y = jnp.where(node == n, peak_ref[0, n], peak_y)
+        peak_x = jnp.where(node == n, peak_ref[1, n], peak_x)
     flow_y = peak_y.astype(F32) + total_y / total
     flow_x = peak_x.astype(F32) + total_x / total
     flow = jnp.where(lane == 0, flow_y, jnp.where(lane == 1, flow_x, 0.0))
@@ -152,7 +156,7 @@
 
 
 def fill_band(target_ref, residual, offset, sub_sign):
-    block = 128
+    block = EXTENT
     lane = lax.broadcasted_iota(jnp.int32, (1, block), 1)
     tap = (lane - BAND).astype(F32) - residual
     raw = jnp.where(lane <= 2 * BAND, 1.0 / (1.0 + tap * tap), 0.0)
@@ -176,16 +180,19 @@
             )
 
 
-def render_kernel(map_ref, band_ref, flow_ref, tile_ref, position_ref, send_ref, col_ref, row_ref, pass_ref):
+def render_kernel(map_ref, band_ref, flow_ref, route_ref, tile_ref, position_ref, send_ref, col_ref, row_ref, pass_ref):
     sections, nodes, _ = flow_ref.shape
     tile_count, edge, _ = tile_ref.shape
+    slots = send_ref.shape[0]
+    section, owner = lax.axis_index("gz"), lax.axis_index("xy")
     position = jnp.zeros(flow_ref.shape[1:], F32)
     for s in range(sections):
-        position = position + map_ref[0, s] * flow_ref[s]
+        position = position + map_ref[section, s] * flow_ref[s]
     position_ref[...] = position
     per_tile = nodes // tile_count
-    height = edge // PIECES
-    chunk = 128
+    height = edge // slots
+    columns = edge // EXTENT
+    chunk = EXTENT
     for t in range(tile_count):
         mean = jnp.sum(position[t * per_tile : (t + 1) * per_tile], axis=0, keepdims=True)
         shift = (MIP_SCALE / per_tile) * mean
@@ -197,35 +204,63 @@
             pass_ref[rows, :] = dot(tile_ref[t, rows, :], col_ref[...]).astype(BF)
         for c in range(edge // chunk):
             rows = slice(c * chunk, (c + 1) * chunk)
+            first, last = c * chunk // height, (c + 1) * chunk // height
             done = dot(row_ref[rows, :], pass_ref[...]).astype(BF)
-            send_ref[c * chunk // height : (c + 1) * chunk // height, t * height : (t + 1) * height, :] = (
-                done.reshape(chunk // height, height, edge)
-            )
-
-
-def gather_kernel(label_ref, inverse_ref, piece_ref, out_ref, total_ref):
+            done = done.reshape(last - first, height, edge)
+            for j in range(columns):
+                at = (t * columns + j) * height
+                send_ref[first:last, at : at + height, :] = done[:, :, j * EXTENT : (j + 1) * EXTENT]
+    lane = lax.broadcasted_iota(jnp.int32, (slots, tile_count * slots), 1)
+    slot = lax.broadcasted_iota(jnp.int32, (slots, tile_count * slots), 0)
+    names = jnp.broadcast_to(route_ref[...], lane.shape).astype(F32)
+    place = lax.broadcasted_iota(jnp.int32, (slots, EXTENT), 1)
+    share = EXTENT // (tile_count * height)
+    here = place // (tile_count * height) == owner % share
+    info = jnp.zeros((slots, EXTENT), F32)
+    for t in range(tile_count):
+        own = jnp.sum(jnp.where(lane == slot + t * slots, names, 0.0), axis=1, keepdims=True)
+        info = jnp.where(here & (place // height % tile_count == t), own, info)
+    tail = tile_count * columns * height
+    for p in range(slots):
+        send_ref[p, tail:, :] = jnp.broadcast_to(info[p : p + 1], (8, EXTENT)).astype(BF)
+
+
+def gather_kernel(piece_ref, out_ref, data_ref, name_ref):
     owners, rows, _ = piece_ref.shape
-    groups, height, _ = total_ref.shape
-    total_ref[...] = jnp.zeros(total_ref.shape, F32)
-    per_owner = rows // height
-
-    def add(owner, carry):
-        for t in range(per_owner):
-            group = label_ref[owner, t]
-            piece = piece_ref[owner, t * height : (t + 1) * height, :].astype(F32)
-            total_ref[group] = total_ref[group] + piece
-        return carry
-
-    lax.fori_loop(0, owners, add, 0)
-    share = groups // owners
-
-    def finish(owner, carry):
-        for t in range(share):
-            value = total_ref[owner * share + t] * inverse_ref[owner, t]
-            out_ref[owner, t * height : (t + 1) * height, :] = value.astype(BF)
-        return carry
-
-    lax.fori_loop(0, owners, finish, 0)
+    _, out_rows, edge = out_ref.shape
+    height = edge // owners
+    columns = edge // EXTENT
+    tile_count = (rows - 8) // (columns * height)
+    tail = rows - 8
+    share = EXTENT // (tile_count * height)
+    lane_row = lax.broadcasted_iota(jnp.int32, (EXTENT, EXTENT), 1) % height
+    sub = lax.broadcasted_iota(jnp.int32, (EXTENT, EXTENT), 0)
+    same = lane_row == sub % height
+    for d in range(owners):
+        for t in range(tile_count):
+            at = (d * tile_count + t) * height
+            for j in range(columns):
+                source = (t * columns + j) * height
+                data_ref[at : at + height, j * EXTENT : (j + 1) * EXTENT] = piece_ref[
+                    d, source : source + height, :
+                ]
+    for start in range(0, owners, share):
+        names = sum(piece_ref[d, tail : tail + 8, :].astype(F32) for d in range(start, start + share))
+        names = jnp.where(same, jnp.broadcast_to(names[0:1], same.shape), -1.0)
+        at = start * tile_count * height
+        for c in range(owners * out_rows // EXTENT):
+            group = (sub // height + c * (EXTENT // height)).astype(F32)
+            name_ref[c * EXTENT : (c + 1) * EXTENT, at : at + EXTENT] = jnp.where(
+                names == group, 1.0, 0.0
+            ).astype(BF)
+    ones = jnp.ones((data_ref.shape[0], EXTENT), BF)
+    for c in range(owners * out_rows // EXTENT):
+        pick = name_ref[c * EXTENT : (c + 1) * EXTENT, :]
+        total = dot(pick, data_ref[...])
+        share_of = 1.0 / jnp.maximum(dot(pick, ones), 1.0)
+        total = total * jnp.concatenate([share_of] * columns, 1)
+        first, last = c * EXTENT // out_rows, (c + 1) * EXTENT // out_rows
+        out_ref[first:last] = total.astype(BF).reshape(last - first, out_rows, edge)
 
 
 def in_vmem():
@@ -247,58 +282,51 @@
 def body(patches, peak_offsets, tiles, band_offsets, routes):
     sections = lax.axis_size("gz")
     owners = lax.axis_size("xy")
-    section = lax.axis_index("gz")
     tile_count, edge = tiles.shape[1], tiles.shape[-1]
     height = edge // PIECES
-    groups = 2 * owners
+    share = 2
+    count = patches.shape[1]
 
     below = lax.ppermute(patches, "gz", [(i, i + 1) for i in range(sections - 1)])
-    label = routes[0, :, 0].reshape(tile_count, PIECES).T.astype(F32)
-    label = jnp.pad(label, ((0, 0), (0, EXTENT - tile_count)))[:, None, :]
-    label = exchange(label, "xy")[:, 0, :tile_count].astype(jnp.int32)
-    match = label.reshape(-1)[:, None] == jnp.arange(groups, dtype=jnp.int32)[None, :]
-    inverse = 1.0 / jnp.maximum(jnp.sum(match.astype(F32), axis=0), 1.0)
-    inverse = inverse.reshape(owners, groups // owners)
-
-    tables = [jnp.asarray(t) for t in dft_constants()]
-    count = patches.shape[1]
     flow = pl.pallas_call(
         flow_kernel,
         out_shape=jax.ShapeDtypeStruct((sections, count, EXTENT), F32),
-        in_specs=[in_smem()] + [in_vmem()] * 6,
+        in_specs=[in_smem()] + [in_vmem()] * 3,
         out_specs=in_vmem(),
         compiler_params=params(),
         name="flow",
-    )(peak_offsets[0], patches[0], below[0], *tables)
+    )(peak_offsets[0].T, patches[0], below[0], jnp.asarray(dft_constants()))
     flow = exchange(flow, "gz")
 
-    linear = lax.dynamic_slice_in_dim(jnp.asarray(relaxation_map(sections)), section, 1, 0)
     position, pieces = pl.pallas_call(
         render_kernel,
         out_shape=(
             jax.ShapeDtypeStruct((count, EXTENT), F32),
-            jax.ShapeDtypeStruct((PIECES, tile_count * height, edge), BF),
+            jax.ShapeDtypeStruct((PIECES, tile_count * height * edge // EXTENT + 8, EXTENT), BF),
         ),
-        in_specs=[in_smem(), in_smem(), in_vmem(), in_vmem()],
+        in_specs=[in_smem(), in_smem()] + [in_vmem()] * 3,
         out_specs=(in_vmem(), in_vmem()),
         scratch_shapes=[pltpu.VMEM((edge, edge), BF)] * 3,
         compiler_params=params(),
         name="render",
-    )(linear, band_offsets[0], flow, tiles[0])
+    )(jnp.asarray(relaxation_map(sections)), band_offsets[0], flow, routes[0].T, tiles[0])
     pieces = exchange(pieces, "xy")
 
     cells = pl.pallas_call(
         gather_kernel,
-        out_shape=jax.ShapeDtypeStruct((owners, groups // owners * height, edge), BF),
-        in_specs=[in_smem(), in_smem(), in_vmem()],
+        out_shape=jax.ShapeDtypeStruct((owners, share * height, edge), BF),
+        in_specs=[in_vmem()],
         out_specs=in_vmem(),
-        scratch_shapes=[pltpu.VMEM((groups, height, edge), F32)],
+        scratch_shapes=[
+            pltpu.VMEM((owners * tile_count * height, edge), BF),
+            pltpu.VMEM((owners * share * height, owners * tile_count * height), BF),
+        ],
         compiler_params=params(),
         name="gather",
-    )(label, inverse, pieces)
+    )(pieces)
     cells = exchange(cells, "xy")
-    rendered = cells.reshape(PIECES, groups // owners, height, edge).transpose(1, 0, 2, 3)
-    rendered = rendered.reshape(1, groups // owners, edge, edge)
+    rendered = cells.reshape(PIECES, share, height, edge).transpose(1, 0, 2, 3)
+    rendered = rendered.reshape(1, share, edge, edge)
     return position[:, :2].T[None], rendered
 
 

time: 128 us -> 116 us (0.906)
  blocking collectives: 0 us -> 64.6 us
  waiting for transfers between devices: 65.4 us -> 28.3 us
  starting transfers between devices: 40.2 us -> 7.48 us
  local copies, waits for them, and re-layouts: 9.44 us -> 4.44 us
  Pallas kernels: 11.2 us -> 9.78 us
    all_to_all x0 -> x2, blocking collectives: none -> 64.6 us  [exchange(): return lax.all_to_all(value, axis, split_axis=0, concat_axis=0, tiled=True)]
    all_to_all x4 -> x1, waiting for transfers between devices: 64.8 us -> 27 us  [exchange(): return lax.all_to_all(value, axis, split_axis=0, concat_axis=0, tiled=True)]
    all_to_all x4 -> x1, starting transfers between devices: 38.3 us -> 5.6 us  [exchange(): return lax.all_to_all(value, axis, split_axis=0, concat_axis=0, tiled=True)]
    unnamed x16 -> x14, local copies, waits for them, and re-layouts: 5.32 us -> 2.76 us
  transfers between devices with their start and end apart: 5 -> 2, of which waited for: 5 -> 2; matrix products, arithmetic and copies ran while one was open for 3% -> 1% of each run, Pallas kernels for 3% -> 0%
where the time goes in v3:
time: 116 us; the launch traced here: 115 us
  blocking collectives  64.6 us (56%)
  waiting for transfers between devices  28.3 us (24%)
  Pallas kernels  9.78 us (8%)
  starting transfers between devices  7.48 us (6%)
  local copies, waits for them, and re-layouts  4.44 us (4%)
    all_to_all x2, blocking collectives, exchange(): return lax.all_to_all(value, axis, split_axis=0, concat_axis=0, tiled=True)  64.6 us
    all_to_all x1, waiting for transfers between devices, exchange(): return lax.all_to_all(value, axis, split_axis=0, concat_axis=0, tiled=True)  27 us
    all_to_all x1, starting transfers between devices, exchange(): return lax.all_to_all(value, axis, split_axis=0, concat_axis=0, tiled=True)  5.6 us
    pallas_call x1, Pallas kernels, body(): pl.pallas_call(flow_kernel, out_shape=jax.ShapeDtypeStruct((sections, cou...  4.26 us
    pallas_call x1, Pallas kernels, body(): pl.pallas_call(gather_kernel, out_shape=jax.ShapeDtypeStruct((owners, sha...  3.01 us
    unnamed x14, local copies, waits for them, and re-layouts  2.76 us
    pallas_call x1, Pallas kernels, body(): pl.pallas_call(render_kernel, out_shape=(jax.ShapeDtypeStruct((count, EXT...  2.51 us
  transfers between devices with their start and end apart: 2, of which 2 were waited for; matrix products, arithmetic and copies ran while one was open for 1% of the time, Pallas kernels for 0%

profile of v3, /device:TPU:2, one launch (start us, length us, event | category | flops | bytes accessed | tf_op | source)
XLA Modules:
  0.0 115.3 jit_solution(12627934871107861811)
XLA Ops:
  0.6 0.0 copy-start
  0.6 1.9 %collective-permute-start = (bf16[1,8,128,128]{3,2,1,0:T(8,128)(2,1)}, bf16[1,8,128,128]{3,2,1,0:T(8,128)(2,1)S(1)}, u32[]{:S(2)}, u32[]{:S(2)}) collective-permute-start(bf16[1,8,128,128]{3,2,1,0:T(8,128)(2,1)} %param.7), channel_id=1, source_target_pairs={{0,32},{32,64},{64,96},{96,128},{128,160},{160,192},{192,224},{224... | collective-permute-start | bytes 786440 | tf_op jit(solution)/shard_map/ppermute | solution.py:290
  2.5 1.3 %collective-permute-done = bf16[1,8,128,128]{3,2,1,0:T(8,128)(2,1)S(1)} collective-permute-done((bf16[1,8,128,128]{3,2,1,0:T(8,128)(2,1)}, bf16[1,8,128,128]{3,2,1,0:T(8,128)(2,1)S(1)}, u32[]{:S(2)}, u32[]{:S(2)}) %collective-permute-start) | collective-permute-done | bytes 262176 | tf_op jit(solution)/shard_map/ppermute | solution.py:290
  3.9 0.0 copy-start.1
  3.9 1.1 copy-done.1
  5.0 0.0 copy-start.2
  5.0 0.9 copy-done.2
  5.9 0.0 copy-start.4
  5.9 0.7 copy-done.4
  6.6 0.0 copy-start.3
  6.6 0.0 copy-start.5
  6.6 0.0 copy-start.6
  6.6 4.3 %flow.1 = f32[16,8,128]{2,1,0:T(8,128)S(1)} custom-call(s32[2,8]{1,0:T(2,128)S(1)} %bitcast.18, bf16[8,128,128]{2,1,0:T(8,128)(2,1)S(1)} %bitcast.16, bf16[8,128,128]{2,1,0:T(8,128)(2,1)S(1)} %bitcast.17, bf16[1456,256]{1,0:T(8,128)(2,1)S(1)} %copy-done.1), custom_call_target="tpu_custom_call" | custom-call | tf_op jit(solution)/shard_map/flow/pallas_call | solution.py:291
  10.9 20.9 %all_to_all.15.flow_ref = f32[16,8,128]{2,1,0:T(8,128)S(1)} all-to-all(f32[16,8,128]{2,1,0:T(8,128)S(1)} %flow.1), channel_id=1, replica_groups=mesh['gz'=16,'xy'=32] {'gz'}, dimensions={0} | all-to-all | bytes 131072 | tf_op jit(solution)/shard_map/all_to_all | solution.py:279
  31.8 0.0 copy-done
  31.8 0.0 copy-done.3
  31.8 0.0 copy-done.5
  31.8 0.0 copy-done.6
  31.8 2.5 %render.1 = (f32[8,128]{1,0:T(8,128)S(1)}, bf16[32,136,128]{2,1,0:T(8,128)(2,1)S(1)}) custom-call(f32[16,16]{1,0:T(8,128)S(1)} %copy-done.3, s32[2,2]{1,0:T(2,128)S(1)} %bitcast.19, f32[16,8,128]{2,1,0:T(8,128)S(1)} %all_to_all.15.flow_ref, s32[1,64]{1,0:T(1,128)S(1)} %bitcast.20, bf16[2,512,512]{2,1,0:T(8,128)(2,1)S(1)} %bitcast.15), custom_call_target="tpu_custom_call" | custom-call | tf_op jit(solution)/shard_map/render/pallas_call | solution.py:301
  34.3 43.7 %all_to_all.16.piece_ref = bf16[32,136,128]{2,1,0:T(8,128)(2,1)S(1)} all-to-all(bf16[32,136,128]{2,1,0:T(8,128)(2,1)S(1)} %get-tuple-element.5), channel_id=1, replica_groups=mesh['gz'=16,'xy'=32] {'xy'}, dimensions={0} | all-to-all | bytes 2228224 | tf_op jit(solution)/shard_map/all_to_all | solution.py:279
  78.0 3.0 %gather.1 = bf16[32,32,512]{2,1,0:T(8,128)(2,1)} custom-call(bf16[32,136,128]{2,1,0:T(8,128)(2,1)S(1)} %all_to_all.16.piece_ref), custom_call_target="tpu_custom_call" | custom-call | tf_op jit(solution)/shard_map/gather/pallas_call | solution.py:315
  81.1 5.6 %all-to-all-start.2 = ((bf16[32,32,512]{2,1,0:T(8,128)(2,1)}), bf16[32,32,512]{2,1,0:T(8,128)(2,1)S(1)}, u32[]{:S(2)}, u32[]{:S(2)}) async-start(bf16[32,32,512]{2,1,0:T(8,128)(2,1)} %gather.1), calls=%async_computation.2 | async-start | bytes 2097152 | tf_op jit(solution)/shard_map/all_to_all | solution.py:279
  86.7 0.6 copy.9
  87.3 27.0 %all-to-all-done.2 = bf16[32,32,512]{2,1,0:T(8,128)(2,1)S(1)} async-done(((bf16[32,32,512]{2,1,0:T(8,128)(2,1)}), bf16[32,32,512]{2,1,0:T(8,128)(2,1)S(1)}, u32[]{:S(2)}, u32[]{:S(2)}) %all-to-all-start.2) | async-done | bytes 1048608 | tf_op jit(solution)/shard_map/all_to_all | solution.py:279
  114.3 1.0 copy.10
  (1 shorter events, 0.0 us)
Async XLA Ops:
  0.6 31.1 %copy-start = (bf16[1,2,512,512]{3,2,1,0:T(8,128)(2,1)S(1)}, bf16[1,2,512,512]{3,2,1,0:T(8,128)(2,1)}, u32[]{:S(2)}) copy-start(bf16[1,2,512,512]{3,2,1,0:T(8,128)(2,1)} %param.9) | copy-start | bytes 3145732
  0.6 3.2 %collective-permute-start = (bf16[1,8,128,128]{3,2,1,0:T(8,128)(2,1)}, bf16[1,8,128,128]{3,2,1,0:T(8,128)(2,1)S(1)}, u32[]{:S(2)}, u32[]{:S(2)}) collective-permute-start(bf16[1,8,128,128]{3,2,1,0:T(8,128)(2,1)} %param.7), channel_id=1, source_target_pairs={{0,32},{32,64},{64,96},{96,128},{128,160},{160,192},{192,224},{224... | collective-permute-start | bytes 786440 | tf_op jit(solution)/shard_map/ppermute | solution.py:290
  3.9 1.1 copy-start.1
  5.0 0.9 copy-start.2
  5.9 0.7 copy-start.4
  6.6 25.1 %copy-start.3 = (f32[16,16]{1,0:T(8,128)S(1)}, f32[16,16]{1,0:T(8,128)}, u32[]{:S(2)}) copy-start(f32[16,16]{1,0:T(8,128)} %constant.5.clone.map_ref) | copy-start | bytes 3076
  6.6 25.1 %copy-start.5 = (s32[1,2,2]{2,1,0:T(2,128)S(1)}, s32[1,2,2]{2,1,0:T(2,128)}, u32[]{:S(2)}) copy-start(s32[1,2,2]{2,1,0:T(2,128)} %param.10) | copy-start | bytes 52
  6.6 25.2 %copy-start.6 = (s32[1,64,1]{1,2,0:T(1,128)S(1)}, s32[1,64,1]{1,2,0:T(1,128)}, u32[]{:S(2)}) copy-start(s32[1,64,1]{1,2,0:T(1,128)} %param.11) | copy-start | bytes 772
  81.1 33.2 %all-to-all-start.2 = ((bf16[32,32,512]{2,1,0:T(8,128)(2,1)}), bf16[32,32,512]{2,1,0:T(8,128)(2,1)S(1)}, u32[]{:S(2)}, u32[]{:S(2)}) async-start(bf16[32,32,512]{2,1,0:T(8,128)(2,1)} %gather.1), calls=%async_computation.2 | async-start | bytes 2097152 | tf_op jit(solution)/shard_map/all_to_all | solution.py:279

commit v4 on v3

--- a/solution.py
+++ b/solution.py
@@ -7,6 +7,7 @@
 from jax.sharding import PartitionSpec as P
 
 PIECES = 32
+NODES = 8
 BAND = 6
 RELAX = 3
 EPSILON = 1e-06
@@ -46,8 +47,9 @@
     fourth_high, fourth_low = high_low(fourth / float(EXTENT * EXTENT))
     fourth = np.concatenate([fourth_high, fourth_high, fourth_low], 1)
     fourth = np.pad(fourth, ((0, 0), (0, 4 * EXTENT - fourth.shape[1])))
-    parts = [first, second, third, fourth[:, : 2 * EXTENT], fourth[:, 2 * EXTENT :]]
-    return np.concatenate(parts, 0)
+    early = np.concatenate([first, second], 0)
+    late = np.concatenate([third, fourth[:, : 2 * EXTENT], fourth[:, 2 * EXTENT :]], 0)
+    return early, late
 
 
 def relaxation_map(sections):
@@ -71,35 +73,64 @@
     return jnp.dot(a, b, preferred_element_type=F32)
 
 
-def flow_kernel(peak_ref, now_ref, low_ref, table_ref, out_ref):
-    count = now_ref.shape[0]
-    ends = np.cumsum([0, 2 * HALF, 3 * EXTENT, 6 * EXTENT, 2 * REACH, 2 * REACH])
-    first_ref, second_ref, third_ref, left_ref, right_ref = (
-        table_ref.at[int(a) : int(b)] for a, b in zip(ends[:-1], ends[1:])
+def spectra(patches, table_ref):
+    lines = []
+    for pair in range(0, len(patches), 2):
+        both = jnp.concatenate(patches[pair : pair + 2], 1)
+        line = dot(table_ref[: 2 * HALF], jnp.concatenate([both, both], 0))
+        lines += [line[:, :EXTENT], line[:, EXTENT:]]
+    high, low = split(jnp.concatenate(lines, 0))
+    product = dot(jnp.concatenate([high, low, high], 1), table_ref[2 * HALF :])
+    result = []
+    for k in range(len(patches)):
+        a = product[2 * HALF * k : 2 * HALF * k + HALF]
+        b = product[2 * HALF * k + HALF : 2 * HALF * (k + 1)]
+        result.append((a[:, :EXTENT] - b[:, EXTENT:], -(a[:, EXTENT:] + b[:, :EXTENT])))
+    return result
+
+
+def energy(ref):
+    rows = []
+    for n in range(ref.shape[0]):
+        value = ref[n].astype(F32)
+        rows.append(jnp.sum(value * value, axis=0, keepdims=True))
+    total = jnp.sum(jnp.concatenate(rows, 0), axis=1, keepdims=True)
+    return total * (1.0 / (EXTENT * EXTENT))
+
+
+def own_kernel(now_ref, table_ref, spectrum_ref, energy_ref):
+    for pair in range(0, now_ref.shape[0], 2):
+        for k, (real, imag) in enumerate(spectra([now_ref[pair], now_ref[pair + 1]], table_ref)):
+            spectrum_ref[pair + k, :, :EXTENT] = real
+            spectrum_ref[pair + k, :, EXTENT:] = imag
+    energy_ref[...] = jnp.broadcast_to(energy(now_ref), energy_ref.shape)
+
+
+def flow_kernel(peak_ref, low_ref, spectrum_ref, energy_ref, table_ref, last_ref, out_ref, inverse_ref, arrived):
+    count = low_ref.shape[0]
+    copy = pltpu.make_async_copy(last_ref, inverse_ref, arrived)
+    copy.start()
+    crosses = []
+    for pair in range(0, count, 2):
+        block = []
+        for k, (lr, li) in enumerate(spectra([low_ref[pair], low_ref[pair + 1]], table_ref)):
+            nr = spectrum_ref[pair + k, :, :EXTENT]
+            ni = spectrum_ref[pair + k, :, EXTENT:]
+            block.append(jnp.concatenate([nr * lr + ni * li, ni * lr - nr * li], 1))
+        crosses.append(jnp.concatenate(block, 0))
+    copy.wait()
+    third = 6 * EXTENT
+    fourth = jnp.concatenate(
+        [
+            inverse_ref[third : third + 2 * REACH],
+            inverse_ref[third + 2 * REACH :, : 6 * HALF - 2 * EXTENT],
+        ],
+        1,
     )
-    fourth = jnp.concatenate([left_ref[...], right_ref[:, : 6 * HALF - 2 * EXTENT]], 1)
     correlations = []
-    for pair in range(count // 2):
-        halves = []
-        for ref in (now_ref, low_ref):
-            both = jnp.concatenate([ref[2 * pair], ref[2 * pair + 1]], 1)
-            lines = dot(first_ref[...], jnp.concatenate([both, both], 0))
-            halves += [lines[:, :EXTENT], lines[:, EXTENT:]]
-        high, low = split(jnp.concatenate(halves, 0))
-        spectra = dot(jnp.concatenate([high, low, high], 1), second_ref[...])
-        parts = []
-        for k in range(4):
-            a = spectra[2 * HALF * k : 2 * HALF * k + HALF]
-            b = spectra[2 * HALF * k + HALF : 2 * HALF * (k + 1)]
-            parts.append(
-                (a[:, :EXTENT] - b[:, EXTENT:], -(a[:, EXTENT:] + b[:, :EXTENT]))
-            )
-        crosses = []
-        for k in range(2):
-            (nr, ni), (lr, li) = parts[k], parts[k + 2]
-            crosses.append(jnp.concatenate([nr * lr + ni * li, ni * lr - nr * li], 1))
-        high, low = split(jnp.concatenate(crosses, 0))
-        outer = dot(jnp.concatenate([high, low, high], 1), third_ref[...])
+    for cross in crosses:
+        high, low = split(cross)
+        outer = dot(jnp.concatenate([high, low, high], 1), inverse_ref[:third])
         columns = []
         for k in range(2):
             block = outer[HALF * k : HALF * (k + 1)]
@@ -108,15 +139,7 @@
         result = dot(fourth, jnp.concatenate([high, low, high], 0))
         correlations += [result[:, :EXTENT], result[:, EXTENT:]]
 
-    def energy(ref):
-        rows = []
-        for n in range(count):
-            value = ref[n].astype(F32)
-            rows.append(jnp.sum(value * value, axis=0, keepdims=True))
-        total = jnp.sum(jnp.concatenate(rows, 0), axis=1, keepdims=True)
-        return total * (1.0 / (EXTENT * EXTENT))
-
-    scale = (SCORE_GAIN / EXTENT) / jnp.sqrt(energy(now_ref) * energy(low_ref) + EPSILON)
+    scale = (SCORE_GAIN / EXTENT) / jnp.sqrt(energy_ref[:, :1] * energy(low_ref) + EPSILON)
     shape = (2 * REACH, EXTENT)
     row = lax.broadcasted_iota(jnp.int32, shape, 0) - REACH
     column = lax.broadcasted_iota(jnp.int32, shape, 1)
@@ -151,7 +174,8 @@
         peak_x = jnp.where(node == n, peak_ref[1, n], peak_x)
     flow_y = peak_y.astype(F32) + total_y / total
     flow_x = peak_x.astype(F32) + total_x / total
-    flow = jnp.where(lane == 0, flow_y, jnp.where(lane == 1, flow_x, 0.0))
+    flow = jnp.where(lane == node, flow_y, jnp.where(lane == node + count, flow_x, 0.0))
+    flow = jnp.sum(flow, axis=0, keepdims=True)
     out_ref[...] = jnp.broadcast_to(flow[None], out_ref.shape)
 
 
@@ -181,7 +205,7 @@
 
 
 def render_kernel(map_ref, band_ref, flow_ref, route_ref, tile_ref, position_ref, send_ref, col_ref, row_ref, pass_ref):
-    sections, nodes, _ = flow_ref.shape
+    sections = flow_ref.shape[0]
     tile_count, edge, _ = tile_ref.shape
     slots = send_ref.shape[0]
     section, owner = lax.axis_index("gz"), lax.axis_index("xy")
@@ -189,16 +213,20 @@
     for s in range(sections):
         position = position + map_ref[section, s] * flow_ref[s]
     position_ref[...] = position
-    per_tile = nodes // tile_count
+    per_tile = NODES // tile_count
+    lanes = lax.broadcasted_iota(jnp.int32, position.shape, 1)
     height = edge // slots
     columns = edge // EXTENT
     chunk = EXTENT
     for t in range(tile_count):
-        mean = jnp.sum(position[t * per_tile : (t + 1) * per_tile], axis=0, keepdims=True)
-        shift = (MIP_SCALE / per_tile) * mean
         offset_y, offset_x = band_ref[t, 0], band_ref[t, 1]
-        fill_band(col_ref, shift[:, 1:2] - offset_x.astype(F32), offset_x, 1)
-        fill_band(row_ref, shift[:, 0:1] - offset_y.astype(F32), offset_y, -1)
+        shift_y, shift_x = (
+            jnp.sum(jnp.where(lanes // per_tile == c * tile_count + t, position, 0.0), axis=1, keepdims=True)
+            * (MIP_SCALE / per_tile)
+            for c in range(2)
+        )
+        fill_band(col_ref, shift_x - offset_x.astype(F32), offset_x, 1)
+        fill_band(row_ref, shift_y - offset_y.astype(F32), offset_y, -1)
         for c in range(edge // chunk):
             rows = slice(c * chunk, (c + 1) * chunk)
             pass_ref[rows, :] = dot(tile_ref[t, rows, :], col_ref[...]).astype(BF)
@@ -225,7 +253,7 @@
         send_ref[p, tail:, :] = jnp.broadcast_to(info[p : p + 1], (8, EXTENT)).astype(BF)
 
 
-def gather_kernel(piece_ref, out_ref, data_ref, name_ref):
+def gather_kernel(piece_ref, out_ref, data_ref):
     owners, rows, _ = piece_ref.shape
     _, out_rows, edge = out_ref.shape
     height = edge // owners
@@ -244,21 +272,16 @@
                 data_ref[at : at + height, j * EXTENT : (j + 1) * EXTENT] = piece_ref[
                     d, source : source + height, :
                 ]
-    for start in range(0, owners, share):
-        names = sum(piece_ref[d, tail : tail + 8, :].astype(F32) for d in range(start, start + share))
-        names = jnp.where(same, jnp.broadcast_to(names[0:1], same.shape), -1.0)
-        at = start * tile_count * height
-        for c in range(owners * out_rows // EXTENT):
-            group = (sub // height + c * (EXTENT // height)).astype(F32)
-            name_ref[c * EXTENT : (c + 1) * EXTENT, at : at + EXTENT] = jnp.where(
-                names == group, 1.0, 0.0
-            ).astype(BF)
-    ones = jnp.ones((data_ref.shape[0], EXTENT), BF)
+    names = [
+        sum(piece_ref[d, tail : tail + 8, :].astype(F32) for d in range(start, start + share))[0:1]
+        for start in range(0, owners, share)
+    ]
     for c in range(owners * out_rows // EXTENT):
-        pick = name_ref[c * EXTENT : (c + 1) * EXTENT, :]
-        total = dot(pick, data_ref[...])
-        share_of = 1.0 / jnp.maximum(dot(pick, ones), 1.0)
-        total = total * jnp.concatenate([share_of] * columns, 1)
+        group = (sub // height + c * (EXTENT // height)).astype(F32)
+        hits = [jnp.where(same & (name == group), 1.0, 0.0) for name in names]
+        count = jnp.sum(sum(hits), axis=1, keepdims=True)
+        total = dot(jnp.concatenate([hit.astype(BF) for hit in hits], 1), data_ref[...])
+        total = total * (1.0 / jnp.maximum(count, 1.0))
         first, last = c * EXTENT // out_rows, (c + 1) * EXTENT // out_rows
         out_ref[first:last] = total.astype(BF).reshape(last - first, out_rows, edge)
 
@@ -288,20 +311,34 @@
     count = patches.shape[1]
 
     below = lax.ppermute(patches, "gz", [(i, i + 1) for i in range(sections - 1)])
+    early_table, late_table = (jnp.asarray(t) for t in dft_constants())
+    spectrum, power = pl.pallas_call(
+        own_kernel,
+        out_shape=(
+            jax.ShapeDtypeStruct((count, HALF, 2 * EXTENT), F32),
+            jax.ShapeDtypeStruct((count, EXTENT), F32),
+        ),
+        in_specs=[in_vmem()] * 2,
+        out_specs=(in_vmem(), in_vmem()),
+        compiler_params=params(),
+        cost_estimate=pl.CostEstimate(flops=10**9, bytes_accessed=2**20, transcendentals=0),
+        name="own",
+    )(patches[0], early_table)
     flow = pl.pallas_call(
         flow_kernel,
-        out_shape=jax.ShapeDtypeStruct((sections, count, EXTENT), F32),
-        in_specs=[in_smem()] + [in_vmem()] * 3,
+        out_shape=jax.ShapeDtypeStruct((sections, 1, EXTENT), F32),
+        in_specs=[in_smem()] + [in_vmem()] * 4 + [pl.BlockSpec(memory_space=pl.ANY)],
         out_specs=in_vmem(),
+        scratch_shapes=[pltpu.VMEM(late_table.shape, BF), pltpu.SemaphoreType.DMA],
         compiler_params=params(),
         name="flow",
-    )(peak_offsets[0].T, patches[0], below[0], jnp.asarray(dft_constants()))
+    )(peak_offsets[0].T, below[0], spectrum, power, early_table, late_table)
     flow = exchange(flow, "gz")
 
     position, pieces = pl.pallas_call(
         render_kernel,
         out_shape=(
-            jax.ShapeDtypeStruct((count, EXTENT), F32),
+            jax.ShapeDtypeStruct((1, EXTENT), F32),
             jax.ShapeDtypeStruct((PIECES, tile_count * height * edge // EXTENT + 8, EXTENT), BF),
         ),
         in_specs=[in_smem(), in_smem()] + [in_vmem()] * 3,
@@ -317,17 +354,14 @@
         out_shape=jax.ShapeDtypeStruct((owners, share * height, edge), BF),
         in_specs=[in_vmem()],
         out_specs=in_vmem(),
-        scratch_shapes=[
-            pltpu.VMEM((owners * tile_count * height, edge), BF),
-            pltpu.VMEM((owners * share * height, owners * tile_count * height), BF),
-        ],
+        scratch_shapes=[pltpu.VMEM((owners * tile_count * height, edge), BF)],
         compiler_params=params(),
         name="gather",
     )(pieces)
     cells = exchange(cells, "xy")
     rendered = cells.reshape(PIECES, share, height, edge).transpose(1, 0, 2, 3)
     rendered = rendered.reshape(1, share, edge, edge)
-    return position[:, :2].T[None], rendered
+    return position[:, : 2 * count].reshape(1, 2, count), rendered
 
 
 def solution(mesh):

time: 116 us -> 110 us (0.948)
  blocking collectives: 64.6 us -> 62.2 us
  waiting for transfers between devices: 28.3 us -> 26.4 us
    all_to_all x2, blocking collectives: 64.6 us -> 62.2 us  [exchange(): return lax.all_to_all(value, axis, split_axis=0, concat_axis=0, tiled=True)]
    ppermute x1, waiting for transfers between devices: 1.34 us -> 0.01 us  [body(): lax.ppermute(patches, 'gz', [(i, i + 1) for i in range(sections - 1)])]
    unnamed x14 -> x16, local copies, waits for them, and re-layouts: 2.76 us -> 2.14 us
    pallas_call x2 -> x3, Pallas kernels: 6.77 us -> 6.22 us  [the longest x1 3.07 us: body(): pl.pallas_call(flow_kernel, out_shape=jax.ShapeDtypeStruct((sections, 1,...]
  transfers between devices with their start and end apart: 2 -> 2, of which waited for: 2 -> 1; matrix products, arithmetic and copies ran while one was open for 1% -> 1% of each run, Pallas kernels for 0% -> 1%
where the time goes in v4:
time: 110 us; the launch traced here: 109 us
  blocking collectives  62.2 us (57%)
  waiting for transfers between devices  26.4 us (24%)
  Pallas kernels  8.72 us (8%)
  starting transfers between devices  7.42 us (7%)
  local copies, waits for them, and re-layouts  3.84 us (3%)
    all_to_all x2, blocking collectives, exchange(): return lax.all_to_all(value, axis, split_axis=0, concat_axis=0, tiled=True)  62.2 us
    all_to_all x1, waiting for transfers between devices, exchange(): return lax.all_to_all(value, axis, split_axis=0, concat_axis=0, tiled=True)  26.4 us
    all_to_all x1, starting transfers between devices, exchange(): return lax.all_to_all(value, axis, split_axis=0, concat_axis=0, tiled=True)  5.66 us
    pallas_call x1, Pallas kernels, body(): pl.pallas_call(flow_kernel, out_shape=jax.ShapeDtypeStruct((sections, 1,...  3.07 us
    pallas_call x1, Pallas kernels, body(): pl.pallas_call(gather_kernel, out_shape=jax.ShapeDtypeStruct((owners, sha...  2.5 us
    pallas_call x1, Pallas kernels, body(): pl.pallas_call(render_kernel, out_shape=(jax.ShapeDtypeStruct((1, EXTENT)...  2.41 us
  transfers between devices with their start and end apart: 2, of which 1 were waited for; matrix products, arithmetic and copies ran while one was open for 1% of the time, Pallas kernels for 1%

profile of v4, /device:TPU:2, one launch (start us, length us, event | category | flops | bytes accessed | tf_op | source)
XLA Modules:
  0.0 109.3 jit_solution(15937636465581162691)
XLA Ops:
  0.6 1.8 %collective-permute-start = (bf16[1,8,128,128]{3,2,1,0:T(8,128)(2,1)}, bf16[1,8,128,128]{3,2,1,0:T(8,128)(2,1)S(1)}, u32[]{:S(2)}, u32[]{:S(2)}) collective-permute-start(bf16[1,8,128,128]{3,2,1,0:T(8,128)(2,1)} %param.8), channel_id=1, source_target_pairs={{0,32},{32,64},{64,96},{96,128},{128,160},{160,192},{192,224},{224... | collective-permute-start | bytes 786440 | tf_op jit(solution)/shard_map/ppermute | solution.py:313
  2.4 0.0 copy-start.2
  2.4 0.9 copy-done.2
  3.3 0.0 copy-start.7
  3.4 0.9 copy-done.7
  4.3 0.0 copy-start.1
  4.3 0.0 copy-start.5
  4.3 0.7 own.1
  5.1 0.0 copy-start
  5.1 0.0 copy-start.3
  5.1 0.0 copy-start.4
  5.1 0.0 copy-start.6
  5.1 0.0 collective-permute-done
  5.1 0.2 copy-done.1
  5.3 0.0 copy-done.5
  5.3 3.1 %flow.1 = f32[16,1,128]{2,1,0:T(1,128)S(1)} custom-call(s32[2,8]{1,0:T(2,128)S(1)} %bitcast.15, bf16[8,128,128]{2,1,0:T(8,128)(2,1)S(1)} %bitcast.13, f32[8,72,256]{2,1,0:T(8,128)S(1)} %get-tuple-element.6.spectrum_ref, f32[8,128]{1,0:T(8,128)S(1)} %get-tuple-element.7.energy_ref, bf16[528,256]{1,0:T(8,128)(2,1)S(1)} %copy-done.2, bf16[928,256]{1,0:T(8,128)(2,1)S(1)} %copy-done.1), custom_call_target="tpu_custom_call" | custom-call | tf_op jit(solution)/shard_map/flow/pallas_call | solution.py:327
  8.4 19.0 %all_to_all.15.flow_ref = f32[16,1,128]{2,1,0:T(1,128)S(1)} all-to-all(f32[16,1,128]{2,1,0:T(1,128)S(1)} %flow.1), channel_id=1, replica_groups=mesh['gz'=16,'xy'=32] {'gz'}, dimensions={0} | all-to-all | bytes 16384 | tf_op jit(solution)/shard_map/all_to_all | solution.py:302
  27.4 0.0 copy-done
  27.4 0.0 copy-done.3
  27.4 0.0 copy-done.4
  27.4 0.0 copy-done.6
  27.4 2.4 %render.1 = (f32[1,128]{1,0:T(1,128)S(1)}, bf16[32,136,128]{2,1,0:T(8,128)(2,1)S(1)}) custom-call(f32[16,16]{1,0:T(8,128)S(1)} %copy-done.3, s32[2,2]{1,0:T(2,128)S(1)} %bitcast.14, f32[16,1,128]{2,1,0:T(1,128)S(1)} %all_to_all.15.flow_ref, s32[1,64]{1,0:T(1,128)S(1)} %bitcast.16, bf16[2,512,512]{2,1,0:T(8,128)(2,1)S(1)} %bitcast.12), custom_call_target="tpu_custom_call" | custom-call | tf_op jit(solution)/shard_map/render/pallas_call | solution.py:338
  29.8 43.2 %all_to_all.16.piece_ref = bf16[32,136,128]{2,1,0:T(8,128)(2,1)S(1)} all-to-all(bf16[32,136,128]{2,1,0:T(8,128)(2,1)S(1)} %get-tuple-element.9), channel_id=1, replica_groups=mesh['gz'=16,'xy'=32] {'xy'}, dimensions={0} | all-to-all | bytes 2228224 | tf_op jit(solution)/shard_map/all_to_all | solution.py:302
  73.0 2.5 %gather.1 = bf16[32,32,512]{2,1,0:T(8,128)(2,1)} custom-call(bf16[32,136,128]{2,1,0:T(8,128)(2,1)S(1)} %all_to_all.16.piece_ref), custom_call_target="tpu_custom_call" | custom-call | tf_op jit(solution)/shard_map/gather/pallas_call | solution.py:352
  75.5 5.7 %all-to-all-start.2 = ((bf16[32,32,512]{2,1,0:T(8,128)(2,1)}), bf16[32,32,512]{2,1,0:T(8,128)(2,1)S(1)}, u32[]{:S(2)}, u32[]{:S(2)}) async-start(bf16[32,32,512]{2,1,0:T(8,128)(2,1)} %gather.1), calls=%async_computation.2 | async-start | bytes 2097152 | tf_op jit(solution)/shard_map/all_to_all | solution.py:302
  81.2 0.6 reshape.13
  81.8 26.4 %all-to-all-done.2 = bf16[32,32,512]{2,1,0:T(8,128)(2,1)S(1)} async-done(((bf16[32,32,512]{2,1,0:T(8,128)(2,1)}), bf16[32,32,512]{2,1,0:T(8,128)(2,1)S(1)}, u32[]{:S(2)}, u32[]{:S(2)}) %all-to-all-start.2) | async-done | bytes 1048608 | tf_op jit(solution)/shard_map/all_to_all | solution.py:302
  108.3 1.0 copy.10
  (1 shorter events, 0.0 us)
Async XLA Ops:
  0.6 4.5 %collective-permute-start = (bf16[1,8,128,128]{3,2,1,0:T(8,128)(2,1)}, bf16[1,8,128,128]{3,2,1,0:T(8,128)(2,1)S(1)}, u32[]{:S(2)}, u32[]{:S(2)}) collective-permute-start(bf16[1,8,128,128]{3,2,1,0:T(8,128)(2,1)} %param.8), channel_id=1, source_target_pairs={{0,32},{32,64},{64,96},{96,128},{128,160},{160,192},{192,224},{224... | collective-permute-start | bytes 786440 | tf_op jit(solution)/shard_map/ppermute | solution.py:313
  2.4 1.0 copy-start.2
  3.3 0.9 copy-start.7
  4.3 1.0 copy-start.1
  4.3 1.0 copy-start.5
  5.1 22.4 %copy-start = (bf16[1,2,512,512]{3,2,1,0:T(8,128)(2,1)S(1)}, bf16[1,2,512,512]{3,2,1,0:T(8,128)(2,1)}, u32[]{:S(2)}) copy-start(bf16[1,2,512,512]{3,2,1,0:T(8,128)(2,1)} %param.10) | copy-start | bytes 3145732
  5.1 22.4 %copy-start.3 = (f32[16,16]{1,0:T(8,128)S(1)}, f32[16,16]{1,0:T(8,128)}, u32[]{:S(2)}) copy-start(f32[16,16]{1,0:T(8,128)} %constant.8.clone.map_ref) | copy-start | bytes 3076
  5.1 22.3 %copy-start.4 = (s32[1,2,2]{2,1,0:T(2,128)S(1)}, s32[1,2,2]{2,1,0:T(2,128)}, u32[]{:S(2)}) copy-start(s32[1,2,2]{2,1,0:T(2,128)} %param.11) | copy-start | bytes 52
  5.1 22.3 %copy-start.6 = (s32[1,64,1]{1,2,0:T(1,128)S(1)}, s32[1,64,1]{1,2,0:T(1,128)}, u32[]{:S(2)}) copy-start(s32[1,64,1]{1,2,0:T(1,128)} %param.12) | copy-start | bytes 772
  75.5 32.8 %all-to-all-start.2 = ((bf16[32,32,512]{2,1,0:T(8,128)(2,1)}), bf16[32,32,512]{2,1,0:T(8,128)(2,1)S(1)}, u32[]{:S(2)}, u32[]{:S(2)}) async-start(bf16[32,32,512]{2,1,0:T(8,128)(2,1)} %gather.1), calls=%async_computation.2 | async-start | bytes 2097152 | tf_op jit(solution)/shard_map/all_to_all | solution.py:302

commit v5 on v4

--- a/solution.py
+++ b/solution.py
@@ -8,6 +8,7 @@
 
 PIECES = 32
 NODES = 8
+WIDE = 4
 BAND = 6
 RELAX = 3
 EPSILON = 1e-06
@@ -209,6 +210,11 @@
     tile_count, edge, _ = tile_ref.shape
     slots = send_ref.shape[0]
     section, owner = lax.axis_index("gz"), lax.axis_index("xy")
+    second_core = section % 2 == 1
+
+    def slot_of(p):
+        return jnp.where(second_core, p % WIDE * (slots // WIDE) + p // WIDE, p)
+
     position = jnp.zeros(flow_ref.shape[1:], F32)
     for s in range(sections):
         position = position + map_ref[section, s] * flow_ref[s]
@@ -235,9 +241,12 @@
             first, last = c * chunk // height, (c + 1) * chunk // height
             done = dot(row_ref[rows, :], pass_ref[...]).astype(BF)
             done = done.reshape(last - first, height, edge)
-            for j in range(columns):
-                at = (t * columns + j) * height
-                send_ref[first:last, at : at + height, :] = done[:, :, j * EXTENT : (j + 1) * EXTENT]
+            for p in range(first, last):
+                for j in range(columns):
+                    at = (t * columns + j) * height
+                    send_ref[slot_of(p), at : at + height, :] = done[
+                        p - first, :, j * EXTENT : (j + 1) * EXTENT
+                    ]
     lane = lax.broadcasted_iota(jnp.int32, (slots, tile_count * slots), 1)
     slot = lax.broadcasted_iota(jnp.int32, (slots, tile_count * slots), 0)
     names = jnp.broadcast_to(route_ref[...], lane.shape).astype(F32)
@@ -250,7 +259,7 @@
         info = jnp.where(here & (place // height % tile_count == t), own, info)
     tail = tile_count * columns * height
     for p in range(slots):
-        send_ref[p, tail:, :] = jnp.broadcast_to(info[p : p + 1], (8, EXTENT)).astype(BF)
+        send_ref[slot_of(p), tail:, :] = jnp.broadcast_to(info[p : p + 1], (8, EXTENT)).astype(BF)
 
 
 def gather_kernel(piece_ref, out_ref, data_ref):
@@ -298,8 +307,21 @@
     return pltpu.CompilerParams(vmem_limit_bytes=40 * 1024 * 1024)
 
 
-def exchange(value, axis):
-    return lax.all_to_all(value, axis, split_axis=0, concat_axis=0, tiled=True)
+def exchange(value, axis, groups=None):
+    return lax.all_to_all(
+        value, axis, split_axis=0, concat_axis=0, tiled=True, axis_index_groups=groups
+    )
+
+
+def exchange_x_then_z(value):
+    owners, rows, lanes = value.shape
+    high = owners // WIDE
+    along_x = [[z * WIDE + x for x in range(WIDE)] for z in range(high)]
+    along_z = [[z * WIDE + x for z in range(high)] for x in range(WIDE)]
+    value = exchange(value.reshape(WIDE, high * rows, lanes), "xy", along_x)
+    value = value.reshape(WIDE, high, rows, lanes).transpose(1, 0, 2, 3)
+    value = exchange(value.reshape(high, WIDE * rows, lanes), "xy", along_z)
+    return value.reshape(owners, rows, lanes)
 
 
 def body(patches, peak_offsets, tiles, band_offsets, routes):
@@ -347,7 +369,12 @@
         compiler_params=params(),
         name="render",
     )(jnp.asarray(relaxation_map(sections)), band_offsets[0], flow, routes[0].T, tiles[0])
-    pieces = exchange(pieces, "xy")
+    pieces = lax.cond(
+        lax.axis_index("gz") % 2 == 1,
+        exchange_x_then_z,
+        lambda value: exchange(value, "xy"),
+        pieces,
+    )
 
     cells = pl.pallas_call(
         gather_kernel,

time: 110 us -> 104 us (0.945)
  the two profiles are of different devices: /device:TPU:2 before, /device:TPU:1 now
where the time goes in v5:
time: 104 us
  blocking collectives  45.3 us (44%)
  waiting for transfers between devices  27.6 us (27%)
  starting transfers between devices  16.9 us (16%)
  Pallas kernels  9.36 us (9%)
  local copies, waits for them, and re-layouts  3.73 us (4%)
    all_to_all x2, blocking collectives, exchange(): lax.all_to_all(value, axis, split_axis=0, concat_axis=0, tiled=True, axis...  45.3 us
    all_to_all x2, waiting for transfers between devices, exchange(): lax.all_to_all(value, axis, split_axis=0, concat_axis=0, tiled=True, axis...  25.5 us
    all_to_all x2, starting transfers between devices, exchange(): lax.all_to_all(value, axis, split_axis=0, concat_axis=0, tiled=True, axis...  12.3 us
    ppermute x1, starting transfers between devices, body(): lax.ppermute(patches, 'gz', [(i, i + 1) for i in range(sections - 1)])  4.59 us
    pallas_call x1, Pallas kernels, body(): pl.pallas_call(flow_kernel, out_shape=jax.ShapeDtypeStruct((sections, 1,...  3.67 us
    pallas_call x1, Pallas kernels, body(): pl.pallas_call(gather_kernel, out_shape=jax.ShapeDtypeStruct((owners, sha...  2.53 us
    pallas_call x1, Pallas kernels, body(): pl.pallas_call(render_kernel, out_shape=(jax.ShapeDtypeStruct((1, EXTENT)...  2.41 us
    ppermute x1, waiting for transfers between devices, body(): lax.ppermute(patches, 'gz', [(i, i + 1) for i in range(sections - 1)])  2.08 us
  transfers between devices with their start and end apart: 3, of which 3 were waited for; matrix products, arithmetic and copies ran while one was open for 1% of the time, Pallas kernels for 1%

profile of v5, /device:TPU:1, one launch (start us, length us, event | category | flops | bytes accessed | tf_op | source)
XLA Modules:
  0.0 103.6 jit_solution(16446339839833325911)
XLA Ops:
  0.6 4.6 %collective-permute-start = (bf16[1,8,128,128]{3,2,1,0:T(8,128)(2,1)}, bf16[1,8,128,128]{3,2,1,0:T(8,128)(2,1)S(1)}, u32[]{:S(2)}, u32[]{:S(2)}) collective-permute-start(bf16[1,8,128,128]{3,2,1,0:T(8,128)(2,1)} %param.10), channel_id=1, source_target_pairs={{0,32},{32,64},{64,96},{96,128},{128,160},{160,192},{192,224},{224... | collective-permute-start | bytes 786440 | tf_op jit(solution)/shard_map/ppermute | solution.py:335
  5.2 0.0 copy-start.2
  5.2 0.9 copy-done.2
  6.2 0.0 copy-start.7
  6.2 0.9 copy-done.7
  7.1 0.0 copy-start.1
  7.1 0.0 copy-start.5
  7.1 0.7 own.1
  7.9 0.0 copy-start
  7.9 0.0 copy-start.3
  7.9 0.0 copy-start.4
  7.9 0.0 copy-start.6
  7.9 2.1 %collective-permute-done = bf16[1,8,128,128]{3,2,1,0:T(8,128)(2,1)S(1)} collective-permute-done((bf16[1,8,128,128]{3,2,1,0:T(8,128)(2,1)}, bf16[1,8,128,128]{3,2,1,0:T(8,128)(2,1)S(1)}, u32[]{:S(2)}, u32[]{:S(2)}) %collective-permute-start) | collective-permute-done | bytes 262176 | tf_op jit(solution)/shard_map/ppermute | solution.py:335
  10.0 0.0 copy-done.1
  10.0 0.0 copy-done.5
  10.0 3.7 %flow.1 = f32[16,1,128]{2,1,0:T(1,128)} custom-call(s32[2,8]{1,0:T(2,128)S(1)} %bitcast.21, bf16[8,128,128]{2,1,0:T(8,128)(2,1)S(1)} %bitcast.19, f32[8,72,256]{2,1,0:T(8,128)S(1)} %get-tuple-element.11.spectrum_ref, f32[8,128]{1,0:T(8,128)S(1)} %get-tuple-element.12.energy_ref, bf16[528,256]{1,0:T(8,128)(2,1)S(1)} %copy-done.2, bf16[928,256]{1,0:T(8,128)(2,1)S(1)} %copy-done.1), custom_call_target="tpu_custom_call" | custom-call | tf_op jit(solution)/shard_map/flow/pallas_call | solution.py:349
  13.7 8.3 %all-to-all-start.3 = ((f32[16,1,128]{2,1,0:T(1,128)}), f32[16,1,128]{2,1,0:T(1,128)S(1)}, u32[]{:S(2)}, u32[]{:S(2)}) async-start(f32[16,1,128]{2,1,0:T(1,128)} %flow.1), calls=%async_computation.3 | async-start | bytes 16384 | tf_op jit(solution)/shard_map/all_to_all | solution.py:311
  22.1 6.9 %all-to-all-done.3.flow_ref = f32[16,1,128]{2,1,0:T(1,128)S(1)} async-done(((f32[16,1,128]{2,1,0:T(1,128)}), f32[16,1,128]{2,1,0:T(1,128)S(1)}, u32[]{:S(2)}, u32[]{:S(2)}) %all-to-all-start.3) | async-done | bytes 8224 | tf_op jit(solution)/shard_map/all_to_all | solution.py:311
  29.0 0.0 copy-done
  29.0 0.0 copy-done.3
  29.0 0.0 copy-done.4
  29.0 0.0 copy-done.6
  29.0 2.4 %render.1 = (f32[1,128]{1,0:T(1,128)S(1)}, bf16[32,136,128]{2,1,0:T(8,128)(2,1)S(1)}) custom-call(f32[16,16]{1,0:T(8,128)S(1)} %copy-done.3, s32[2,2]{1,0:T(2,128)S(1)} %bitcast.20, f32[16,1,128]{2,1,0:T(1,128)S(1)} %all-to-all-done.3.flow_ref, s32[1,64]{1,0:T(1,128)S(1)} %bitcast.22, bf16[2,512,512]{2,1,0:T(8,128)(2,1)S(1)} %bitcast.18), custom_call_target="tpu_custom_call" | custom-call | tf_op jit(solution)/shard_map/render/pallas_call | solution.py:360
  31.4 45.4 %conditional.1 = (bf16[32,136,128]{2,1,0:T(8,128)(2,1)S(1)}) conditional(s32[]{:T(128)} %convert_element_type.3, bf16[32,136,128]{2,1,0:T(8,128)(2,1)S(1)} %get-tuple-element.14, bf16[32,136,128]{2,1,0:T(8,128)(2,1)S(1)} %get-tuple-element.14), branch_computations={%region_0.1_spmd, %region_1.2_spmd} | conditional | bytes 6684680 | solution.py:372
  31.5 13.9 %all_to_all.23 = bf16[4,1088,128]{2,1,0:T(8,128)(2,1)S(1)} all-to-all(bf16[4,1088,128]{2,1,0:T(8,128)(2,1)S(1)} %bitcast.24), channel_id=1, replica_groups={{0,1,2,3},{4,5,6,7},{8,9,10,11},{12,13,14,15},{16,17,18,19},{20,21,22,2..., dimensions={0} | all-to-all | bytes 2228224 | tf_op jit(solution)/shard_map/cond/branch_1_fun/all_to_all | solution.py:311
  45.4 0.1 copy.10
  45.4 31.4 %all_to_all.24 = bf16[8,544,128]{2,1,0:T(8,128)(2,1)S(1)} all-to-all(bf16[8,544,128]{2,1,0:T(8,128)(2,1)S(1)} %bitcast.25), channel_id=1, replica_groups={{0,4,8,12,16,20,24,28},{1,5,9,13,17,21,25,29},{2,6,10,14,18,22,26,30},{..., dimensions={0} | all-to-all | bytes 2228224 | tf_op jit(solution)/shard_map/cond/branch_1_fun/all_to_all | solution.py:311
  76.9 2.5 %gather.1 = bf16[32,32,512]{2,1,0:T(8,128)(2,1)} custom-call(bf16[32,136,128]{2,1,0:T(8,128)(2,1)S(1)} %get-tuple-element.15.piece_ref), custom_call_target="tpu_custom_call" | custom-call | tf_op jit(solution)/shard_map/gather/pallas_call | solution.py:379
  79.4 3.9 %all-to-all-start.4 = ((bf16[32,32,512]{2,1,0:T(8,128)(2,1)}), bf16[32,32,512]{2,1,0:T(8,128)(2,1)S(1)}, u32[]{:S(2)}, u32[]{:S(2)}) async-start(bf16[32,32,512]{2,1,0:T(8,128)(2,1)} %gather.1), calls=%async_computation.4 | async-start | bytes 2097152 | tf_op jit(solution)/shard_map/all_to_all | solution.py:311
  83.3 0.6 reshape.25
  84.0 18.6 %all-to-all-done.4 = bf16[32,32,512]{2,1,0:T(8,128)(2,1)S(1)} async-done(((bf16[32,32,512]{2,1,0:T(8,128)(2,1)}), bf16[32,32,512]{2,1,0:T(8,128)(2,1)S(1)}, u32[]{:S(2)}, u32[]{:S(2)}) %all-to-all-start.4) | async-done | bytes 1048608 | tf_op jit(solution)/shard_map/all_to_all | solution.py:311
  102.6 1.1 %copy.11 = bf16[2,32,16,512]{3,2,1,0:T(8,128)(2,1)} copy(bf16[2,32,16,512]{3,2,0,1:T(8,128)(2,1)S(1)} %bitcast.28) | data formatting | bytes 2097152 | tf_op jit(solution)/shard_map/transpose | solution.py:389
  (1 shorter events, 0.0 us)
Async XLA Ops:
  0.6 9.4 %collective-permute-start = (bf16[1,8,128,128]{3,2,1,0:T(8,128)(2,1)}, bf16[1,8,128,128]{3,2,1,0:T(8,128)(2,1)S(1)}, u32[]{:S(2)}, u32[]{:S(2)}) collective-permute-start(bf16[1,8,128,128]{3,2,1,0:T(8,128)(2,1)} %param.10), channel_id=1, source_target_pairs={{0,32},{32,64},{64,96},{96,128},{128,160},{160,192},{192,224},{224... | collective-permute-start | bytes 786440 | tf_op jit(solution)/shard_map/ppermute | solution.py:335
  5.2 1.0 copy-start.2
  6.2 0.9 copy-start.7
  7.1 2.9 %copy-start.1 = (bf16[928,256]{1,0:T(8,128)(2,1)S(1)}, bf16[928,256]{1,0:T(8,128)(2,1)}, u32[]{:S(2)}) copy-start(bf16[928,256]{1,0:T(8,128)(2,1)} %constant.27.clone.last_ref) | copy-start | bytes 1425412
  7.1 2.9 %copy-start.5 = (s32[1,8,2]{1,2,0:T(2,128)S(1)}, s32[1,8,2]{1,2,0:T(2,128)}, u32[]{:S(2)}) copy-start(s32[1,8,2]{1,2,0:T(2,128)} %param.11) | copy-start | bytes 196
  7.9 21.1 %copy-start = (bf16[1,2,512,512]{3,2,1,0:T(8,128)(2,1)S(1)}, bf16[1,2,512,512]{3,2,1,0:T(8,128)(2,1)}, u32[]{:S(2)}) copy-start(bf16[1,2,512,512]{3,2,1,0:T(8,128)(2,1)} %param.12) | copy-start | bytes 3145732
  7.9 21.1 %copy-start.3 = (f32[16,16]{1,0:T(8,128)S(1)}, f32[16,16]{1,0:T(8,128)}, u32[]{:S(2)}) copy-start(f32[16,16]{1,0:T(8,128)} %constant.28.clone.map_ref) | copy-start | bytes 3076
  7.9 21.1 %copy-start.4 = (s32[1,2,2]{2,1,0:T(2,128)S(1)}, s32[1,2,2]{2,1,0:T(2,128)}, u32[]{:S(2)}) copy-start(s32[1,2,2]{2,1,0:T(2,128)} %param.13) | copy-start | bytes 52
  7.9 21.1 %copy-start.6 = (s32[1,64,1]{1,2,0:T(1,128)S(1)}, s32[1,64,1]{1,2,0:T(1,128)}, u32[]{:S(2)}) copy-start(s32[1,64,1]{1,2,0:T(1,128)} %param.14) | copy-start | bytes 772
  13.7 15.3 %all-to-all-start.3 = ((f32[16,1,128]{2,1,0:T(1,128)}), f32[16,1,128]{2,1,0:T(1,128)S(1)}, u32[]{:S(2)}, u32[]{:S(2)}) async-start(f32[16,1,128]{2,1,0:T(1,128)} %flow.1), calls=%async_computation.3 | async-start | bytes 16384 | tf_op jit(solution)/shard_map/all_to_all | solution.py:311
  79.4 23.2 %all-to-all-start.4 = ((bf16[32,32,512]{2,1,0:T(8,128)(2,1)}), bf16[32,32,512]{2,1,0:T(8,128)(2,1)S(1)}, u32[]{:S(2)}, u32[]{:S(2)}) async-start(bf16[32,32,512]{2,1,0:T(8,128)(2,1)} %gather.1), calls=%async_computation.4 | async-start | bytes 2097152 | tf_op jit(solution)/shard_map/all_to_all | solution.py:311

commit v6 on v4

--- a/solution.py
+++ b/solution.py
@@ -8,6 +8,7 @@
 
 PIECES = 32
 NODES = 8
+WIDE = 4
 BAND = 6
 RELAX = 3
 EPSILON = 1e-06
@@ -98,7 +99,22 @@
     return total * (1.0 / (EXTENT * EXTENT))
 
 
-def own_kernel(now_ref, table_ref, spectrum_ref, energy_ref):
+def own_kernel(route_ref, now_ref, table_ref, spectrum_ref, energy_ref, name_ref):
+    slots = name_ref.shape[0]
+    tile_count = route_ref.shape[1] // slots
+    height = EXTENT // WIDE // tile_count
+    owner = lax.axis_index("xy")
+    lane = lax.broadcasted_iota(jnp.int32, (slots, tile_count * slots), 1)
+    slot = lax.broadcasted_iota(jnp.int32, (slots, tile_count * slots), 0)
+    names = jnp.broadcast_to(route_ref[...], lane.shape).astype(F32)
+    place = lax.broadcasted_iota(jnp.int32, (slots, EXTENT), 1)
+    here = place // (tile_count * height) == owner % WIDE
+    row = jnp.zeros((slots, EXTENT), F32)
+    for t in range(tile_count):
+        own = jnp.sum(jnp.where(lane == slot + t * slots, names, 0.0), axis=1, keepdims=True)
+        row = jnp.where(here & (place // height % tile_count == t), own, row)
+    for p in range(slots):
+        name_ref[p] = jnp.broadcast_to(row[p : p + 1], (8, EXTENT)).astype(BF)
     for pair in range(0, now_ref.shape[0], 2):
         for k, (real, imag) in enumerate(spectra([now_ref[pair], now_ref[pair + 1]], table_ref)):
             spectrum_ref[pair + k, :, :EXTENT] = real
@@ -204,11 +220,12 @@
             )
 
 
-def render_kernel(map_ref, band_ref, flow_ref, route_ref, tile_ref, position_ref, send_ref, col_ref, row_ref, pass_ref):
+def render_kernel(map_ref, band_ref, flow_ref, tile_ref, *refs):
+    *name_refs, position_ref, send_ref, col_ref, row_ref, pass_ref = refs
     sections = flow_ref.shape[0]
     tile_count, edge, _ = tile_ref.shape
     slots = send_ref.shape[0]
-    section, owner = lax.axis_index("gz"), lax.axis_index("xy")
+    section = lax.axis_index("gz")
     position = jnp.zeros(flow_ref.shape[1:], F32)
     for s in range(sections):
         position = position + map_ref[section, s] * flow_ref[s]
@@ -238,29 +255,19 @@
             for j in range(columns):
                 at = (t * columns + j) * height
                 send_ref[first:last, at : at + height, :] = done[:, :, j * EXTENT : (j + 1) * EXTENT]
-    lane = lax.broadcasted_iota(jnp.int32, (slots, tile_count * slots), 1)
-    slot = lax.broadcasted_iota(jnp.int32, (slots, tile_count * slots), 0)
-    names = jnp.broadcast_to(route_ref[...], lane.shape).astype(F32)
-    place = lax.broadcasted_iota(jnp.int32, (slots, EXTENT), 1)
-    share = EXTENT // (tile_count * height)
-    here = place // (tile_count * height) == owner % share
-    info = jnp.zeros((slots, EXTENT), F32)
-    for t in range(tile_count):
-        own = jnp.sum(jnp.where(lane == slot + t * slots, names, 0.0), axis=1, keepdims=True)
-        info = jnp.where(here & (place // height % tile_count == t), own, info)
-    tail = tile_count * columns * height
-    for p in range(slots):
-        send_ref[p, tail:, :] = jnp.broadcast_to(info[p : p + 1], (8, EXTENT)).astype(BF)
-
-
-def gather_kernel(piece_ref, out_ref, data_ref):
-    owners, rows, _ = piece_ref.shape
+    for name_ref in name_refs:
+        send_ref[:, tile_count * columns * height :, :] = name_ref[...]
+
+
+def gather_kernel(piece_ref, *refs):
+    *name_refs, out_ref, data_ref = refs
+    owners = piece_ref.shape[0]
     _, out_rows, edge = out_ref.shape
     height = edge // owners
     columns = edge // EXTENT
-    tile_count = (rows - 8) // (columns * height)
-    tail = rows - 8
-    share = EXTENT // (tile_count * height)
+    tile_count = EXTENT // WIDE // height
+    tail = tile_count * columns * height
+    name_ref = name_refs[0] if name_refs else piece_ref.at[:, tail:]
     lane_row = lax.broadcasted_iota(jnp.int32, (EXTENT, EXTENT), 1) % height
     sub = lax.broadcasted_iota(jnp.int32, (EXTENT, EXTENT), 0)
     same = lane_row == sub % height
@@ -273,8 +280,8 @@
                     d, source : source + height, :
                 ]
     names = [
-        sum(piece_ref[d, tail : tail + 8, :].astype(F32) for d in range(start, start + share))[0:1]
-        for start in range(0, owners, share)
+        sum(name_ref[d].astype(F32) for d in range(start, start + WIDE))[0:1]
+        for start in range(0, owners, WIDE)
     ]
     for c in range(owners * out_rows // EXTENT):
         group = (sub // height + c * (EXTENT // height)).astype(F32)
@@ -312,18 +319,19 @@
 
     below = lax.ppermute(patches, "gz", [(i, i + 1) for i in range(sections - 1)])
     early_table, late_table = (jnp.asarray(t) for t in dft_constants())
-    spectrum, power = pl.pallas_call(
+    spectrum, power, names = pl.pallas_call(
         own_kernel,
         out_shape=(
             jax.ShapeDtypeStruct((count, HALF, 2 * EXTENT), F32),
             jax.ShapeDtypeStruct((count, EXTENT), F32),
+            jax.ShapeDtypeStruct((PIECES, 8, EXTENT), BF),
         ),
-        in_specs=[in_vmem()] * 2,
-        out_specs=(in_vmem(), in_vmem()),
+        in_specs=[in_vmem()] * 3,
+        out_specs=(in_vmem(),) * 3,
         compiler_params=params(),
         cost_estimate=pl.CostEstimate(flops=10**9, bytes_accessed=2**20, transcendentals=0),
         name="own",
-    )(patches[0], early_table)
+    )(routes[0].T, patches[0], early_table)
     flow = pl.pallas_call(
         flow_kernel,
         out_shape=jax.ShapeDtypeStruct((sections, 1, EXTENT), F32),
@@ -335,29 +343,46 @@
     )(peak_offsets[0].T, below[0], spectrum, power, early_table, late_table)
     flow = exchange(flow, "gz")
 
-    position, pieces = pl.pallas_call(
-        render_kernel,
-        out_shape=(
-            jax.ShapeDtypeStruct((1, EXTENT), F32),
-            jax.ShapeDtypeStruct((PIECES, tile_count * height * edge // EXTENT + 8, EXTENT), BF),
-        ),
-        in_specs=[in_smem(), in_smem()] + [in_vmem()] * 3,
-        out_specs=(in_vmem(), in_vmem()),
-        scratch_shapes=[pltpu.VMEM((edge, edge), BF)] * 3,
-        compiler_params=params(),
-        name="render",
-    )(jnp.asarray(relaxation_map(sections)), band_offsets[0], flow, routes[0].T, tiles[0])
-    pieces = exchange(pieces, "xy")
-
-    cells = pl.pallas_call(
-        gather_kernel,
-        out_shape=jax.ShapeDtypeStruct((owners, share * height, edge), BF),
-        in_specs=[in_vmem()],
-        out_specs=in_vmem(),
-        scratch_shapes=[pltpu.VMEM((owners * tile_count * height, edge), BF)],
-        compiler_params=params(),
-        name="gather",
-    )(pieces)
+    linear = jnp.asarray(relaxation_map(sections))
+    piece_rows = tile_count * height * edge // EXTENT
+
+    def render(flow, image, *names):
+        return pl.pallas_call(
+            render_kernel,
+            out_shape=(
+                jax.ShapeDtypeStruct((1, EXTENT), F32),
+                jax.ShapeDtypeStruct((PIECES, piece_rows + 8 * len(names), EXTENT), BF),
+            ),
+            in_specs=[in_smem(), in_smem()] + [in_vmem()] * (2 + len(names)),
+            out_specs=(in_vmem(), in_vmem()),
+            scratch_shapes=[pltpu.VMEM((edge, edge), BF)] * 3,
+            compiler_params=params(),
+            cost_estimate=pl.CostEstimate(flops=4 * 10**9, bytes_accessed=2**21, transcendentals=0),
+            name="render",
+        )(linear, band_offsets[0], flow, image, *names)
+
+    def gather(*received):
+        return pl.pallas_call(
+            gather_kernel,
+            out_shape=jax.ShapeDtypeStruct((owners, share * height, edge), BF),
+            in_specs=[in_vmem()] * len(received),
+            out_specs=in_vmem(),
+            scratch_shapes=[pltpu.VMEM((owners * tile_count * height, edge), BF)],
+            compiler_params=params(),
+            name="gather",
+        )(*received)
+
+    def together(flow, image, names):
+        position, whole = render(flow, image, names)
+        return position, gather(exchange(whole, "xy"))
+
+    def names_ahead(flow, image, names):
+        names = exchange(names, "xy")
+        position, pieces = render(flow, image)
+        return position, gather(exchange(pieces, "xy"), names)
+
+    second_core = lax.axis_index("gz") % 2 == 1
+    position, cells = lax.cond(second_core, names_ahead, together, flow, tiles[0], names)
     cells = exchange(cells, "xy")
     rendered = cells.reshape(PIECES, share, height, edge).transpose(1, 0, 2, 3)
     rendered = rendered.reshape(1, share, edge, edge)

time: 110 us -> 108 us (0.982)
  the two profiles are of different devices: /device:TPU:2 before, /device:TPU:1 now
where the time goes in v6:
time: 108 us; the launch traced here: 107 us
  waiting for transfers between devices  37.4 us (35%)
  starting transfers between devices  31.1 us (29%)
  blocking collectives  24 us (22%)
  Pallas kernels  9.83 us (9%)
  local copies, waits for them, and re-layouts  4.29 us (4%)
    all_to_all x3, waiting for transfers between devices, exchange(): return lax.all_to_all(value, axis, split_axis=0, concat_axis=0, tiled=True)  36.4 us
    all_to_all x3, starting transfers between devices, exchange(): return lax.all_to_all(value, axis, split_axis=0, concat_axis=0, tiled=True)  26.5 us
    all_to_all x1, blocking collectives, exchange(): return lax.all_to_all(value, axis, split_axis=0, concat_axis=0, tiled=True)  24 us
    ppermute x1, starting transfers between devices, body(): lax.ppermute(patches, 'gz', [(i, i + 1) for i in range(sections - 1)])  4.59 us
    pallas_call x1, Pallas kernels, body(): pl.pallas_call(flow_kernel, out_shape=jax.ShapeDtypeStruct((sections, 1,...  3.67 us
    unnamed x16, local copies, waits for them, and re-layouts  2.57 us
    pallas_call x1, Pallas kernels, gather(): pl.pallas_call(gather_kernel, out_shape=jax.ShapeDtypeStruct((owners, sha...  2.48 us
    pallas_call x1, Pallas kernels, render(): pl.pallas_call(render_kernel, out_shape=(jax.ShapeDtypeStruct((1, EXTENT)...  2.4 us
  transfers between devices with their start and end apart: 4, of which 4 were waited for; matrix products, arithmetic and copies ran while one was open for 1% of the time, Pallas kernels for 3%

profile of v6, /device:TPU:1, one launch (start us, length us, event | category | flops | bytes accessed | tf_op | source)
XLA Modules:
  0.0 107.3 jit_solution(4006748864619850046)
XLA Ops:
  0.6 4.6 %collective-permute-start = (bf16[1,8,128,128]{3,2,1,0:T(8,128)(2,1)}, bf16[1,8,128,128]{3,2,1,0:T(8,128)(2,1)S(1)}, u32[]{:S(2)}, u32[]{:S(2)}) collective-permute-start(bf16[1,8,128,128]{3,2,1,0:T(8,128)(2,1)} %param.10), channel_id=1, source_target_pairs={{0,32},{32,64},{64,96},{96,128},{128,160},{160,192},{192,224},{224... | collective-permute-start | bytes 786440 | tf_op jit(solution)/shard_map/ppermute | solution.py:320
  5.2 0.0 copy-start.1
  5.2 0.9 copy-done.1
  6.2 0.0 copy-start.3
  6.2 0.9 copy-done.3
  7.1 0.0 copy-start.4
  7.1 0.7 copy-done.4
  7.8 0.0 copy-start
  7.8 0.0 copy-start.2
  7.8 1.3 %own.1 = (f32[8,72,256]{2,1,0:T(8,128)S(1)}, f32[8,128]{1,0:T(8,128)S(1)}, bf16[32,8,128]{2,1,0:T(8,128)(2,1)}) custom-call(s32[1,64]{1,0:T(1,128)S(1)} %bitcast.16, bf16[8,128,128]{2,1,0:T(8,128)(2,1)S(1)} %bitcast.15, bf16[528,256]{1,0:T(8,128)(2,1)S(1)} %copy-done.1), custom_call_target="tpu_custom_call" | custom-call | flops 1000000000 | bytes 1048576 | tf_op jit(solution)/shard_map/own/pallas_call | solution.py:322
  9.1 0.0 copy-start.5
  9.1 0.0 copy-start.6
  9.1 0.0 copy-start.7
  9.1 0.9 collective-permute-done
  10.0 0.0 copy-done
  10.0 0.0 copy-done.2
  10.0 3.7 %flow.1 = f32[16,1,128]{2,1,0:T(1,128)} custom-call(s32[2,8]{1,0:T(2,128)S(1)} %bitcast.14, bf16[8,128,128]{2,1,0:T(8,128)(2,1)S(1)} %bitcast.13, f32[8,72,256]{2,1,0:T(8,128)S(1)} %get-tuple-element.41.spectrum_ref, f32[8,128]{1,0:T(8,128)S(1)} %get-tuple-element.42.energy_ref, bf16[528,256]{1,0:T(8,128)(2,1)S(1)} %copy-done.1, bf16[928,256]{1,0:T(8,128)(2,1)S(1)} %copy-done), custom_call_target="tpu_custom_call" | custom-call | tf_op jit(solution)/shard_map/flow/pallas_call | solution.py:335
  13.7 8.3 %all-to-all-start.3 = ((f32[16,1,128]{2,1,0:T(1,128)}), f32[16,1,128]{2,1,0:T(1,128)S(1)}, u32[]{:S(2)}, u32[]{:S(2)}) async-start(f32[16,1,128]{2,1,0:T(1,128)} %flow.1), calls=%async_computation.3 | async-start | bytes 16384 | tf_op jit(solution)/shard_map/all_to_all | solution.py:309
  22.1 6.9 %all-to-all-done.3 = f32[16,1,128]{2,1,0:T(1,128)S(1)} async-done(((f32[16,1,128]{2,1,0:T(1,128)}), f32[16,1,128]{2,1,0:T(1,128)S(1)}, u32[]{:S(2)}, u32[]{:S(2)}) %all-to-all-start.3) | async-done | bytes 8224 | tf_op jit(solution)/shard_map/all_to_all | solution.py:309
  29.0 0.0 copy-done.5
  29.0 0.0 copy-done.6
  29.0 0.0 copy-done.7
  29.0 48.3 %conditional.1 = (f32[1,128]{1,0:T(1,128)S(1)}, bf16[32,32,512]{2,1,0:T(8,128)(2,1)}) conditional(s32[]{:T(128)} %convert_element_type.3, (s32[1,2,2]{2,1,0:T(2,128)S(1)}, f32[16,16]{1,0:T(8,128)S(1)}, f32[16,1,128]{2,1,0:T(1,128)S(1)}, bf16[2,512,512]{2,1,0:T(8,128)(2,1)S(1)}, bf16[32,8,128]{2,1,0:T(8,128)(2,1)}) %tuple.24, ...), branch_computations={%region_0.1_spmd, %region_1.2_spmd} | conditional | flops 4000000000 | bytes 4390960 | solution.py:385
  29.0 12.9 %all-to-all-start.2 = ((bf16[32,8,128]{2,1,0:T(8,128)(2,1)}), bf16[32,8,128]{2,1,0:T(8,128)(2,1)S(1)}, u32[]{:S(2)}, u32[]{:S(2)}) async-start(bf16[32,8,128]{2,1,0:T(8,128)(2,1)} %get-tuple-element.33), calls=%async_computation.2 | async-start | bytes 131072 | tf_op jit(solution)/shard_map/cond/branch_1_fun/all_to_all | solution.py:309
  41.9 2.4 %render.3 = (f32[1,128]{1,0:T(1,128)S(1)}, bf16[32,128,128]{2,1,0:T(8,128)(2,1)S(1)}) custom-call(f32[16,16]{1,0:T(8,128)S(1)} %get-tuple-element.27.map_ref, s32[2,2]{1,0:T(2,128)S(1)} %bitcast.22, f32[16,1,128]{2,1,0:T(1,128)S(1)} %get-tuple-element.29.flow_ref, bf16[2,512,512]{2,1,0:T(8,128)(2,1)S(1)} %get-tuple-element.30.tile_ref), custom_call_target="tpu_custom_call" | custom-call | flops 4000000000 | bytes 2097152 | tf_op jit(solution)/shard_map/cond/branch_1_fun/render/pallas_call | solution.py:350
  44.3 6.4 %all-to-all-done.2.refs_0_ = bf16[32,8,128]{2,1,0:T(8,128)(2,1)S(1)} async-done(((bf16[32,8,128]{2,1,0:T(8,128)(2,1)}), bf16[32,8,128]{2,1,0:T(8,128)(2,1)S(1)}, u32[]{:S(2)}, u32[]{:S(2)}) %all-to-all-start.2) | async-done | bytes 65568 | tf_op jit(solution)/shard_map/cond/branch_1_fun/all_to_all | solution.py:309
  50.8 24.0 %all_to_all.23.piece_ref = bf16[32,128,128]{2,1,0:T(8,128)(2,1)S(1)} all-to-all(bf16[32,128,128]{2,1,0:T(8,128)(2,1)S(1)} %get-tuple-element.32), channel_id=1, replica_groups=mesh['gz'=16,'xy'=32] {'xy'}, dimensions={0} | all-to-all | bytes 2097152 | tf_op jit(solution)/shard_map/cond/branch_1_fun/all_to_all | solution.py:309
  74.8 2.5 %gather.3 = bf16[32,32,512]{2,1,0:T(8,128)(2,1)} custom-call(bf16[32,128,128]{2,1,0:T(8,128)(2,1)S(1)} %all_to_all.23.piece_ref, bf16[32,8,128]{2,1,0:T(8,128)(2,1)S(1)} %all-to-all-done.2.refs_0_), custom_call_target="tpu_custom_call" | custom-call | tf_op jit(solution)/shard_map/cond/branch_1_fun/gather/pallas_call | solution.py:365
  77.3 5.2 %all-to-all-start.4 = ((bf16[32,32,512]{2,1,0:T(8,128)(2,1)}), bf16[32,32,512]{2,1,0:T(8,128)(2,1)S(1)}, u32[]{:S(2)}, u32[]{:S(2)}) async-start(bf16[32,32,512]{2,1,0:T(8,128)(2,1)} %get-tuple-element.45), calls=%async_computation.4 | async-start | bytes 2097152 | tf_op jit(solution)/shard_map/all_to_all | solution.py:309
  82.5 0.6 reshape.13
  83.2 23.1 %all-to-all-done.4 = bf16[32,32,512]{2,1,0:T(8,128)(2,1)S(1)} async-done(((bf16[32,32,512]{2,1,0:T(8,128)(2,1)}), bf16[32,32,512]{2,1,0:T(8,128)(2,1)S(1)}, u32[]{:S(2)}, u32[]{:S(2)}) %all-to-all-start.4) | async-done | bytes 1048608 | tf_op jit(solution)/shard_map/all_to_all | solution.py:309
  106.3 1.1 copy.10
  (1 shorter events, 0.0 us)
Async XLA Ops:
  0.6 9.4 %collective-permute-start = (bf16[1,8,128,128]{3,2,1,0:T(8,128)(2,1)}, bf16[1,8,128,128]{3,2,1,0:T(8,128)(2,1)S(1)}, u32[]{:S(2)}, u32[]{:S(2)}) collective-permute-start(bf16[1,8,128,128]{3,2,1,0:T(8,128)(2,1)} %param.10), channel_id=1, source_target_pairs={{0,32},{32,64},{64,96},{96,128},{128,160},{160,192},{192,224},{224... | collective-permute-start | bytes 786440 | tf_op jit(solution)/shard_map/ppermute | solution.py:320
  5.2 1.0 copy-start.1
  6.2 0.9 copy-start.3
  7.1 0.7 copy-start.4
  7.8 2.2 %copy-start = (bf16[928,256]{1,0:T(8,128)(2,1)S(1)}, bf16[928,256]{1,0:T(8,128)(2,1)}, u32[]{:S(2)}) copy-start(bf16[928,256]{1,0:T(8,128)(2,1)} %constant.27.clone.last_ref) | copy-start | bytes 1425412
  7.8 2.2 %copy-start.2 = (s32[1,8,2]{1,2,0:T(2,128)S(1)}, s32[1,8,2]{1,2,0:T(2,128)}, u32[]{:S(2)}) copy-start(s32[1,8,2]{1,2,0:T(2,128)} %param.11) | copy-start | bytes 196
  9.1 19.9 %copy-start.5 = (bf16[1,2,512,512]{3,2,1,0:T(8,128)(2,1)S(1)}, bf16[1,2,512,512]{3,2,1,0:T(8,128)(2,1)}, u32[]{:S(2)}) copy-start(bf16[1,2,512,512]{3,2,1,0:T(8,128)(2,1)} %param.12) | copy-start | bytes 3145732
  9.1 19.9 %copy-start.6 = (s32[1,2,2]{2,1,0:T(2,128)S(1)}, s32[1,2,2]{2,1,0:T(2,128)}, u32[]{:S(2)}) copy-start(s32[1,2,2]{2,1,0:T(2,128)} %param.13) | copy-start | bytes 52
  9.1 19.9 %copy-start.7 = (f32[16,16]{1,0:T(8,128)S(1)}, f32[16,16]{1,0:T(8,128)}, u32[]{:S(2)}) copy-start(f32[16,16]{1,0:T(8,128)} %constant.28.clone) | copy-start | bytes 3076
  13.7 15.3 %all-to-all-start.3 = ((f32[16,1,128]{2,1,0:T(1,128)}), f32[16,1,128]{2,1,0:T(1,128)S(1)}, u32[]{:S(2)}, u32[]{:S(2)}) async-start(f32[16,1,128]{2,1,0:T(1,128)} %flow.1), calls=%async_computation.3 | async-start | bytes 16384 | tf_op jit(solution)/shard_map/all_to_all | solution.py:309
  29.0 21.7 %all-to-all-start.2 = ((bf16[32,8,128]{2,1,0:T(8,128)(2,1)}), bf16[32,8,128]{2,1,0:T(8,128)(2,1)S(1)}, u32[]{:S(2)}, u32[]{:S(2)}) async-start(bf16[32,8,128]{2,1,0:T(8,128)(2,1)} %get-tuple-element.33), calls=%async_computation.2 | async-start | bytes 131072 | tf_op jit(solution)/shard_map/cond/branch_1_fun/all_to_all | solution.py:309
  77.3 29.0 %all-to-all-start.4 = ((bf16[32,32,512]{2,1,0:T(8,128)(2,1)}), bf16[32,32,512]{2,1,0:T(8,128)(2,1)S(1)}, u32[]{:S(2)}, u32[]{:S(2)}) async-start(bf16[32,32,512]{2,1,0:T(8,128)(2,1)} %get-tuple-element.45), calls=%async_computation.4 | async-start | bytes 2097152 | tf_op jit(solution)/shard_map/all_to_all | solution.py:309

commit v7 on v6

--- a/solution.py
+++ b/solution.py
@@ -221,7 +221,7 @@
 
 
 def render_kernel(map_ref, band_ref, flow_ref, tile_ref, *refs):
-    *name_refs, position_ref, send_ref, col_ref, row_ref, pass_ref = refs
+    name_ref, position_ref, send_ref, *name_outs, col_ref, row_ref, pass_ref = refs
     sections = flow_ref.shape[0]
     tile_count, edge, _ = tile_ref.shape
     slots = send_ref.shape[0]
@@ -255,7 +255,9 @@
             for j in range(columns):
                 at = (t * columns + j) * height
                 send_ref[first:last, at : at + height, :] = done[:, :, j * EXTENT : (j + 1) * EXTENT]
-    for name_ref in name_refs:
+    if name_outs:
+        name_outs[0][...] = name_ref[...]
+    else:
         send_ref[:, tile_count * columns * height :, :] = name_ref[...]
 
 
@@ -346,20 +348,18 @@
     linear = jnp.asarray(relaxation_map(sections))
     piece_rows = tile_count * height * edge // EXTENT
 
-    def render(flow, image, *names):
+    def render(flow, image, names, apart):
+        rows = (piece_rows, names.shape[1]) if apart else (piece_rows + names.shape[1],)
+        shapes = tuple(jax.ShapeDtypeStruct((PIECES, r, EXTENT), BF) for r in rows)
         return pl.pallas_call(
             render_kernel,
-            out_shape=(
-                jax.ShapeDtypeStruct((1, EXTENT), F32),
-                jax.ShapeDtypeStruct((PIECES, piece_rows + 8 * len(names), EXTENT), BF),
-            ),
-            in_specs=[in_smem(), in_smem()] + [in_vmem()] * (2 + len(names)),
-            out_specs=(in_vmem(), in_vmem()),
+            out_shape=(jax.ShapeDtypeStruct((1, EXTENT), F32),) + shapes,
+            in_specs=[in_smem(), in_smem()] + [in_vmem()] * 3,
+            out_specs=(in_vmem(),) * (1 + len(rows)),
             scratch_shapes=[pltpu.VMEM((edge, edge), BF)] * 3,
             compiler_params=params(),
-            cost_estimate=pl.CostEstimate(flops=4 * 10**9, bytes_accessed=2**21, transcendentals=0),
             name="render",
-        )(linear, band_offsets[0], flow, image, *names)
+        )(linear, band_offsets[0], flow, image, names)
 
     def gather(*received):
         return pl.pallas_call(
@@ -373,12 +373,13 @@
         )(*received)
 
     def together(flow, image, names):
-        position, whole = render(flow, image, names)
+        position, whole = render(flow, image, names, False)
         return position, gather(exchange(whole, "xy"))
 
     def names_ahead(flow, image, names):
+        position, pieces, names = render(flow, image, names, True)
         names = exchange(names, "xy")
-        position, pieces = render(flow, image)
+        pieces, names = lax.optimization_barrier((pieces, names))
         return position, gather(exchange(pieces, "xy"), names)
 
     second_core = lax.axis_index("gz") % 2 == 1

time: 108 us -> 105 us (0.972)
  blocking collectives: 24 us -> 43.3 us
  starting transfers between devices: 31.1 us -> 18.1 us
  waiting for transfers between devices: 37.4 us -> 29 us
    all_to_all x1 -> x2, blocking collectives: 24 us -> 43.3 us  [exchange(): return lax.all_to_all(value, axis, split_axis=0, concat_axis=0, tiled=True)]
    all_to_all x3 -> x2, starting transfers between devices: 26.5 us -> 13.5 us  [exchange(): return lax.all_to_all(value, axis, split_axis=0, concat_axis=0, tiled=True)]
    all_to_all x3 -> x2, waiting for transfers between devices: 36.4 us -> 27.6 us  [exchange(): return lax.all_to_all(value, axis, split_axis=0, concat_axis=0, tiled=True)]
  transfers between devices with their start and end apart: 4 -> 3, of which waited for: 4 -> 3; matrix products, arithmetic and copies ran while one was open for 1% -> 1% of each run, Pallas kernels for 3% -> 1%
where the time goes in v7:
time: 105 us
  blocking collectives  43.3 us (41%)
  waiting for transfers between devices  29 us (28%)
  starting transfers between devices  18.1 us (17%)
  Pallas kernels  9.29 us (9%)
  local copies, waits for them, and re-layouts  4.3 us (4%)
    all_to_all x2, blocking collectives, exchange(): return lax.all_to_all(value, axis, split_axis=0, concat_axis=0, tiled=True)  43.3 us
    all_to_all x2, waiting for transfers between devices, exchange(): return lax.all_to_all(value, axis, split_axis=0, concat_axis=0, tiled=True)  27.6 us
    all_to_all x2, starting transfers between devices, exchange(): return lax.all_to_all(value, axis, split_axis=0, concat_axis=0, tiled=True)  13.5 us
    ppermute x1, starting transfers between devices, body(): lax.ppermute(patches, 'gz', [(i, i + 1) for i in range(sections - 1)])  4.59 us
    pallas_call x1, Pallas kernels, body(): pl.pallas_call(flow_kernel, out_shape=jax.ShapeDtypeStruct((sections, 1,...  3.67 us
    unnamed x16, local copies, waits for them, and re-layouts  2.58 us
    pallas_call x1, Pallas kernels, gather(): pl.pallas_call(gather_kernel, out_shape=jax.ShapeDtypeStruct((owners, sha...  2.47 us
    pallas_call x1, Pallas kernels, render(): pl.pallas_call(render_kernel, out_shape=(jax.ShapeDtypeStruct((1, EXTENT)...  2.4 us
  transfers between devices with their start and end apart: 3, of which 3 were waited for; matrix products, arithmetic and copies ran while one was open for 1% of the time, Pallas kernels for 1%

profile of v7, /device:TPU:1, one launch (start us, length us, event | category | flops | bytes accessed | tf_op | source)
XLA Modules:
  0.0 104.7 jit_solution(4452055953253593714)
XLA Ops:
  0.6 4.6 %collective-permute-start = (bf16[1,8,128,128]{3,2,1,0:T(8,128)(2,1)}, bf16[1,8,128,128]{3,2,1,0:T(8,128)(2,1)S(1)}, u32[]{:S(2)}, u32[]{:S(2)}) collective-permute-start(bf16[1,8,128,128]{3,2,1,0:T(8,128)(2,1)} %param.10), channel_id=1, source_target_pairs={{0,32},{32,64},{64,96},{96,128},{128,160},{160,192},{192,224},{224... | collective-permute-start | bytes 786440 | tf_op jit(solution)/shard_map/ppermute | solution.py:322
  5.2 0.0 copy-start.1
  5.2 0.9 copy-done.1
  6.2 0.0 copy-start.3
  6.2 0.9 copy-done.3
  7.1 0.0 copy-start.4
  7.1 0.7 copy-done.4
  7.8 0.0 copy-start
  7.8 0.0 copy-start.2
  7.8 0.7 own.1
  8.6 0.0 copy-start.5
  8.6 0.0 copy-start.6
  8.6 0.0 copy-start.7
  8.6 1.4 %collective-permute-done = bf16[1,8,128,128]{3,2,1,0:T(8,128)(2,1)S(1)} collective-permute-done((bf16[1,8,128,128]{3,2,1,0:T(8,128)(2,1)}, bf16[1,8,128,128]{3,2,1,0:T(8,128)(2,1)S(1)}, u32[]{:S(2)}, u32[]{:S(2)}) %collective-permute-start) | collective-permute-done | bytes 262176 | tf_op jit(solution)/shard_map/ppermute | solution.py:322
  10.0 0.0 copy-done
  10.0 0.0 copy-done.2
  10.0 3.7 %flow.1 = f32[16,1,128]{2,1,0:T(1,128)} custom-call(s32[2,8]{1,0:T(2,128)S(1)} %bitcast.14, bf16[8,128,128]{2,1,0:T(8,128)(2,1)S(1)} %bitcast.13, f32[8,72,256]{2,1,0:T(8,128)S(1)} %get-tuple-element.44.spectrum_ref, f32[8,128]{1,0:T(8,128)S(1)} %get-tuple-element.45.energy_ref, bf16[528,256]{1,0:T(8,128)(2,1)S(1)} %copy-done.1, bf16[928,256]{1,0:T(8,128)(2,1)S(1)} %copy-done), custom_call_target="tpu_custom_call" | custom-call | tf_op jit(solution)/shard_map/flow/pallas_call | solution.py:337
  13.7 8.3 %all-to-all-start.3 = ((f32[16,1,128]{2,1,0:T(1,128)}), f32[16,1,128]{2,1,0:T(1,128)S(1)}, u32[]{:S(2)}, u32[]{:S(2)}) async-start(f32[16,1,128]{2,1,0:T(1,128)} %flow.1), calls=%async_computation.3 | async-start | bytes 16384 | tf_op jit(solution)/shard_map/all_to_all | solution.py:311
  22.1 6.9 %all-to-all-done.3 = f32[16,1,128]{2,1,0:T(1,128)S(1)} async-done(((f32[16,1,128]{2,1,0:T(1,128)}), f32[16,1,128]{2,1,0:T(1,128)S(1)}, u32[]{:S(2)}, u32[]{:S(2)}) %all-to-all-start.3) | async-done | bytes 8224 | tf_op jit(solution)/shard_map/all_to_all | solution.py:311
  29.0 0.0 copy-done.5
  29.0 0.0 copy-done.6
  29.0 0.0 copy-done.7
  29.0 48.2 %conditional.1 = (f32[1,128]{1,0:T(1,128)S(1)}, bf16[32,32,512]{2,1,0:T(8,128)(2,1)}) conditional(s32[]{:T(128)} %convert_element_type.3, (s32[1,2,2]{2,1,0:T(2,128)S(1)}, f32[16,16]{1,0:T(8,128)S(1)}, f32[16,1,128]{2,1,0:T(1,128)S(1)}, bf16[2,512,512]{2,1,0:T(8,128)(2,1)S(1)}, bf16[32,8,128]{2,1,0:T(8,128)(2,1)S(1)}) %tuple.25, ...), branch_computations={%region_0.1_spmd, %region_1.2_spmd} | conditional | bytes 2228240 | solution.py:386
  29.0 2.4 %render.3 = (f32[1,128]{1,0:T(1,128)S(1)}, bf16[32,128,128]{2,1,0:T(8,128)(2,1)S(1)}, bf16[32,8,128]{2,1,0:T(8,128)(2,1)S(1)}) custom-call(f32[16,16]{1,0:T(8,128)S(1)} %get-tuple-element.27.map_ref, s32[2,2]{1,0:T(2,128)S(1)} %bitcast.22, f32[16,1,128]{2,1,0:T(1,128)S(1)} %get-tuple-element.29.flow_ref, ...), custom_call_target="tpu_custom_call" | custom-call | tf_op jit(solution)/shard_map/cond/branch_1_fun/render/pallas_call | solution.py:354
  31.4 21.6 %all_to_all.23.refs_0_ = bf16[32,8,128]{2,1,0:T(8,128)(2,1)S(1)} all-to-all(bf16[32,8,128]{2,1,0:T(8,128)(2,1)S(1)} %get-tuple-element.34), channel_id=1, replica_groups=mesh['gz'=16,'xy'=32] {'xy'}, dimensions={0} | all-to-all | bytes 131072 | tf_op jit(solution)/shard_map/cond/branch_1_fun/all_to_all | solution.py:311
  53.0 21.7 %all_to_all.24.piece_ref = bf16[32,128,128]{2,1,0:T(8,128)(2,1)S(1)} all-to-all(bf16[32,128,128]{2,1,0:T(8,128)(2,1)S(1)} %get-tuple-element.35), channel_id=1, replica_groups=mesh['gz'=16,'xy'=32] {'xy'}, dimensions={0} | all-to-all | bytes 2097152 | tf_op jit(solution)/shard_map/cond/branch_1_fun/all_to_all | solution.py:311
  74.7 2.5 %gather.3 = bf16[32,32,512]{2,1,0:T(8,128)(2,1)} custom-call(bf16[32,128,128]{2,1,0:T(8,128)(2,1)S(1)} %all_to_all.24.piece_ref, bf16[32,8,128]{2,1,0:T(8,128)(2,1)S(1)} %all_to_all.23.refs_0_), custom_call_target="tpu_custom_call" | custom-call | tf_op jit(solution)/shard_map/cond/branch_1_fun/gather/pallas_call | solution.py:365
  77.2 5.1 %all-to-all-start.4 = ((bf16[32,32,512]{2,1,0:T(8,128)(2,1)}), bf16[32,32,512]{2,1,0:T(8,128)(2,1)S(1)}, u32[]{:S(2)}, u32[]{:S(2)}) async-start(bf16[32,32,512]{2,1,0:T(8,128)(2,1)} %get-tuple-element.48), calls=%async_computation.4 | async-start | bytes 2097152 | tf_op jit(solution)/shard_map/all_to_all | solution.py:311
  82.3 0.6 reshape.13
  83.0 20.6 %all-to-all-done.4 = bf16[32,32,512]{2,1,0:T(8,128)(2,1)S(1)} async-done(((bf16[32,32,512]{2,1,0:T(8,128)(2,1)}), bf16[32,32,512]{2,1,0:T(8,128)(2,1)S(1)}, u32[]{:S(2)}, u32[]{:S(2)}) %all-to-all-start.4) | async-done | bytes 1048608 | tf_op jit(solution)/shard_map/all_to_all | solution.py:311
  103.6 1.1 %copy.10 = bf16[32,2,16,512]{3,2,0,1:T(8,128)(2,1)} copy(bf16[32,2,16,512]{3,2,1,0:T(8,128)(2,1)S(1)} %bitcast.19) | data formatting | bytes 2097152 | tf_op jit(solution)/shard_map/reshape | solution.py:388
  (1 shorter events, 0.0 us)
Async XLA Ops:
  0.6 9.4 %collective-permute-start = (bf16[1,8,128,128]{3,2,1,0:T(8,128)(2,1)}, bf16[1,8,128,128]{3,2,1,0:T(8,128)(2,1)S(1)}, u32[]{:S(2)}, u32[]{:S(2)}) collective-permute-start(bf16[1,8,128,128]{3,2,1,0:T(8,128)(2,1)} %param.10), channel_id=1, source_target_pairs={{0,32},{32,64},{64,96},{96,128},{128,160},{160,192},{192,224},{224... | collective-permute-start | bytes 786440 | tf_op jit(solution)/shard_map/ppermute | solution.py:322
  5.2 1.0 copy-start.1
  6.2 0.9 copy-start.3
  7.1 0.7 copy-start.4
  7.8 2.2 %copy-start = (bf16[928,256]{1,0:T(8,128)(2,1)S(1)}, bf16[928,256]{1,0:T(8,128)(2,1)}, u32[]{:S(2)}) copy-start(bf16[928,256]{1,0:T(8,128)(2,1)} %constant.27.clone.last_ref) | copy-start | bytes 1425412
  7.8 2.2 %copy-start.2 = (s32[1,8,2]{1,2,0:T(2,128)S(1)}, s32[1,8,2]{1,2,0:T(2,128)}, u32[]{:S(2)}) copy-start(s32[1,8,2]{1,2,0:T(2,128)} %param.11) | copy-start | bytes 196
  8.6 20.5 %copy-start.5 = (bf16[1,2,512,512]{3,2,1,0:T(8,128)(2,1)S(1)}, bf16[1,2,512,512]{3,2,1,0:T(8,128)(2,1)}, u32[]{:S(2)}) copy-start(bf16[1,2,512,512]{3,2,1,0:T(8,128)(2,1)} %param.12) | copy-start | bytes 3145732
  8.6 20.4 %copy-start.6 = (f32[16,16]{1,0:T(8,128)S(1)}, f32[16,16]{1,0:T(8,128)}, u32[]{:S(2)}) copy-start(f32[16,16]{1,0:T(8,128)} %constant.28.clone) | copy-start | bytes 3076
  8.6 20.4 %copy-start.7 = (s32[1,2,2]{2,1,0:T(2,128)S(1)}, s32[1,2,2]{2,1,0:T(2,128)}, u32[]{:S(2)}) copy-start(s32[1,2,2]{2,1,0:T(2,128)} %param.13) | copy-start | bytes 52
  13.7 15.3 %all-to-all-start.3 = ((f32[16,1,128]{2,1,0:T(1,128)}), f32[16,1,128]{2,1,0:T(1,128)S(1)}, u32[]{:S(2)}, u32[]{:S(2)}) async-start(f32[16,1,128]{2,1,0:T(1,128)} %flow.1), calls=%async_computation.3 | async-start | bytes 16384 | tf_op jit(solution)/shard_map/all_to_all | solution.py:311
  77.2 26.5 %all-to-all-start.4 = ((bf16[32,32,512]{2,1,0:T(8,128)(2,1)}), bf16[32,32,512]{2,1,0:T(8,128)(2,1)S(1)}, u32[]{:S(2)}, u32[]{:S(2)}) async-start(bf16[32,32,512]{2,1,0:T(8,128)(2,1)} %get-tuple-element.48), calls=%async_computation.4 | async-start | bytes 2097152 | tf_op jit(solution)/shard_map/all_to_all | solution.py:311

commit v8 on v5

--- a/solution.py
+++ b/solution.py
@@ -7,7 +7,6 @@
 from jax.sharding import PartitionSpec as P
 
 PIECES = 32
-NODES = 8
 WIDE = 4
 BAND = 6
 RELAX = 3
@@ -107,10 +106,26 @@
     energy_ref[...] = jnp.broadcast_to(energy(now_ref), energy_ref.shape)
 
 
-def flow_kernel(peak_ref, low_ref, spectrum_ref, energy_ref, table_ref, last_ref, out_ref, inverse_ref, arrived):
+def write_names(owner, route_ref, name_ref):
+    slots = name_ref.shape[0]
+    tile_count = route_ref.shape[1] // slots
+    height = EXTENT // WIDE // tile_count
+    lane = lax.broadcasted_iota(jnp.int32, (slots, tile_count * slots), 1)
+    slot = lax.broadcasted_iota(jnp.int32, (slots, tile_count * slots), 0)
+    names = jnp.broadcast_to(route_ref[...], lane.shape).astype(F32)
+    place = lax.broadcasted_iota(jnp.int32, (slots, EXTENT), 1)
+    here = place // (tile_count * height) == owner % WIDE
+    row = jnp.zeros((slots, EXTENT), F32)
+    for t in range(tile_count):
+        own = jnp.sum(jnp.where(lane == slot + t * slots, names, 0.0), axis=1, keepdims=True)
+        row = jnp.where(here & (place // height % tile_count == t), own, row)
+    for p in range(slots):
+        name_ref[p] = jnp.broadcast_to(row[p : p + 1], (8, EXTENT)).astype(BF)
+
+
+def flow_kernel(place_ref, peak_ref, route_ref, low_ref, spectrum_ref, energy_ref, table_ref, inverse_ref, out_ref, name_ref):
     count = low_ref.shape[0]
-    copy = pltpu.make_async_copy(last_ref, inverse_ref, arrived)
-    copy.start()
+    write_names(place_ref[0], route_ref, name_ref)
     crosses = []
     for pair in range(0, count, 2):
         block = []
@@ -119,7 +134,6 @@
             ni = spectrum_ref[pair + k, :, EXTENT:]
             block.append(jnp.concatenate([nr * lr + ni * li, ni * lr - nr * li], 1))
         crosses.append(jnp.concatenate(block, 0))
-    copy.wait()
     third = 6 * EXTENT
     fourth = jnp.concatenate(
         [
@@ -205,12 +219,12 @@
             )
 
 
-def render_kernel(map_ref, band_ref, flow_ref, route_ref, tile_ref, position_ref, send_ref, col_ref, row_ref, pass_ref):
+def render_kernel(place_ref, map_ref, band_ref, flow_ref, name_ref, tile_ref, position_ref, send_ref, *scratch):
     sections = flow_ref.shape[0]
     tile_count, edge, _ = tile_ref.shape
     slots = send_ref.shape[0]
-    section, owner = lax.axis_index("gz"), lax.axis_index("xy")
-    second_core = section % 2 == 1
+    section = place_ref[1]
+    second_core = place_ref[2] == 1
 
     def slot_of(p):
         return jnp.where(second_core, p % WIDE * (slots // WIDE) + p // WIDE, p)
@@ -218,13 +232,16 @@
     position = jnp.zeros(flow_ref.shape[1:], F32)
     for s in range(sections):
         position = position + map_ref[section, s] * flow_ref[s]
-    position_ref[...] = position
-    per_tile = NODES // tile_count
+    nodes = position_ref.shape[1]
+    for c in range(2):
+        position_ref[c : c + 1, :] = position[:, c * nodes : (c + 1) * nodes]
+    per_tile = nodes // tile_count
     lanes = lax.broadcasted_iota(jnp.int32, position.shape, 1)
     height = edge // slots
     columns = edge // EXTENT
     chunk = EXTENT
     for t in range(tile_count):
+        col_ref, row_ref, pass_ref = scratch[3 * t : 3 * t + 3]
         offset_y, offset_x = band_ref[t, 0], band_ref[t, 1]
         shift_y, shift_x = (
             jnp.sum(jnp.where(lanes // per_tile == c * tile_count + t, position, 0.0), axis=1, keepdims=True)
@@ -247,19 +264,9 @@
                     send_ref[slot_of(p), at : at + height, :] = done[
                         p - first, :, j * EXTENT : (j + 1) * EXTENT
                     ]
-    lane = lax.broadcasted_iota(jnp.int32, (slots, tile_count * slots), 1)
-    slot = lax.broadcasted_iota(jnp.int32, (slots, tile_count * slots), 0)
-    names = jnp.broadcast_to(route_ref[...], lane.shape).astype(F32)
-    place = lax.broadcasted_iota(jnp.int32, (slots, EXTENT), 1)
-    share = EXTENT // (tile_count * height)
-    here = place // (tile_count * height) == owner % share
-    info = jnp.zeros((slots, EXTENT), F32)
-    for t in range(tile_count):
-        own = jnp.sum(jnp.where(lane == slot + t * slots, names, 0.0), axis=1, keepdims=True)
-        info = jnp.where(here & (place // height % tile_count == t), own, info)
     tail = tile_count * columns * height
     for p in range(slots):
-        send_ref[slot_of(p), tail:, :] = jnp.broadcast_to(info[p : p + 1], (8, EXTENT)).astype(BF)
+        send_ref[slot_of(p), tail:, :] = name_ref[p]
 
 
 def gather_kernel(piece_ref, out_ref, data_ref):
@@ -332,8 +339,11 @@
     share = 2
     count = patches.shape[1]
 
+    section = lax.axis_index("gz")
     below = lax.ppermute(patches, "gz", [(i, i + 1) for i in range(sections - 1)])
     early_table, late_table = (jnp.asarray(t) for t in dft_constants())
+    second_core = section % 2 == 1
+    place = jnp.stack([lax.axis_index("xy"), section, second_core.astype(jnp.int32)])
     spectrum, power = pl.pallas_call(
         own_kernel,
         out_shape=(
@@ -341,36 +351,38 @@
             jax.ShapeDtypeStruct((count, EXTENT), F32),
         ),
         in_specs=[in_vmem()] * 2,
-        out_specs=(in_vmem(), in_vmem()),
+        out_specs=(in_vmem(),) * 2,
         compiler_params=params(),
         cost_estimate=pl.CostEstimate(flops=10**9, bytes_accessed=2**20, transcendentals=0),
         name="own",
     )(patches[0], early_table)
-    flow = pl.pallas_call(
+    flow, names = pl.pallas_call(
         flow_kernel,
-        out_shape=jax.ShapeDtypeStruct((sections, 1, EXTENT), F32),
-        in_specs=[in_smem()] + [in_vmem()] * 4 + [pl.BlockSpec(memory_space=pl.ANY)],
-        out_specs=in_vmem(),
-        scratch_shapes=[pltpu.VMEM(late_table.shape, BF), pltpu.SemaphoreType.DMA],
+        out_shape=(
+            jax.ShapeDtypeStruct((sections, 1, EXTENT), F32),
+            jax.ShapeDtypeStruct((PIECES, 8, EXTENT), BF),
+        ),
+        in_specs=[in_smem()] * 2 + [in_vmem()] * 6,
+        out_specs=(in_vmem(),) * 2,
         compiler_params=params(),
         name="flow",
-    )(peak_offsets[0].T, below[0], spectrum, power, early_table, late_table)
+    )(place, peak_offsets[0].T, routes[0].T, below[0], spectrum, power, early_table, late_table)
     flow = exchange(flow, "gz")
 
     position, pieces = pl.pallas_call(
         render_kernel,
         out_shape=(
-            jax.ShapeDtypeStruct((1, EXTENT), F32),
+            jax.ShapeDtypeStruct((2, count), F32),
             jax.ShapeDtypeStruct((PIECES, tile_count * height * edge // EXTENT + 8, EXTENT), BF),
         ),
-        in_specs=[in_smem(), in_smem()] + [in_vmem()] * 3,
+        in_specs=[in_smem()] * 3 + [in_vmem()] * 3,
         out_specs=(in_vmem(), in_vmem()),
-        scratch_shapes=[pltpu.VMEM((edge, edge), BF)] * 3,
+        scratch_shapes=[pltpu.VMEM((edge, edge), BF)] * (3 * tile_count),
         compiler_params=params(),
         name="render",
-    )(jnp.asarray(relaxation_map(sections)), band_offsets[0], flow, routes[0].T, tiles[0])
+    )(place, jnp.asarray(relaxation_map(sections)), band_offsets[0], flow, names, tiles[0])
     pieces = lax.cond(
-        lax.axis_index("gz") % 2 == 1,
+        second_core,
         exchange_x_then_z,
         lambda value: exchange(value, "xy"),
         pieces,
@@ -388,7 +400,7 @@
     cells = exchange(cells, "xy")
     rendered = cells.reshape(PIECES, share, height, edge).transpose(1, 0, 2, 3)
     rendered = rendered.reshape(1, share, edge, edge)
-    return position[:, : 2 * count].reshape(1, 2, count), rendered
+    return position[None], rendered
 
 
 def solution(mesh):

time: 104 us -> 102 us (0.981)
  blocking collectives: 45.3 us -> 83.3 us
  waiting for transfers between devices: 27.6 us -> 2 us
  starting transfers between devices: 16.9 us -> 4.59 us
  Pallas kernels: 9.36 us -> 7.79 us
    all_to_all x2 -> x4, blocking collectives: 45.3 us -> 83.3 us  [exchange(): lax.all_to_all(value, axis, split_axis=0, concat_axis=0, tiled=True, axis...]
    all_to_all x2 -> x0, waiting for transfers between devices: 25.5 us -> none  [exchange(): lax.all_to_all(value, axis, split_axis=0, concat_axis=0, tiled=True, axis...]
    all_to_all x2 -> x0, starting transfers between devices: 12.3 us -> none  [exchange(): lax.all_to_all(value, axis, split_axis=0, concat_axis=0, tiled=True, axis...]
  transfers between devices with their start and end apart: 3 -> 1, of which waited for: 3 -> 1; matrix products, arithmetic and copies ran while one was open for 1% -> 0% of each run, Pallas kernels for 1% -> 1%
where the time goes in v8:
time: 102 us
  blocking collectives  83.3 us (82%)
  Pallas kernels  7.79 us (8%)
  starting transfers between devices  4.59 us (4%)
  local copies, waits for them, and re-layouts  3.06 us (3%)
  waiting for transfers between devices  2 us (2%)
    all_to_all x4, blocking collectives, exchange(): lax.all_to_all(value, axis, split_axis=0, concat_axis=0, tiled=True, axis...  83.3 us
    ppermute x1, starting transfers between devices, body(): lax.ppermute(patches, 'gz', [(i, i + 1) for i in range(sections - 1)])  4.59 us
    pallas_call x1, Pallas kernels, body(): pl.pallas_call(render_kernel, out_shape=(jax.ShapeDtypeStruct((2, count),...  2.91 us
    pallas_call x1, Pallas kernels, body(): pl.pallas_call(flow_kernel, out_shape=(jax.ShapeDtypeStruct((sections, 1,...  2.59 us
  transfers between devices with their start and end apart: 1, of which 1 were waited for; matrix products, arithmetic and copies ran while one was open for 0% of the time, Pallas kernels for 1%

profile of v8, /device:TPU:1, one launch (start us, length us, event | category | flops | bytes accessed | tf_op | source)
XLA Modules:
  0.0 101.6 jit_solution(10611721427413659622)
XLA Ops:
  0.6 4.6 %collective-permute-start = (bf16[1,8,128,128]{3,2,1,0:T(8,128)(2,1)}, bf16[1,8,128,128]{3,2,1,0:T(8,128)(2,1)S(1)}, u32[]{:S(2)}, u32[]{:S(2)}) collective-permute-start(bf16[1,8,128,128]{3,2,1,0:T(8,128)(2,1)} %param.10), channel_id=1, source_target_pairs={{0,32},{32,64},{64,96},{96,128},{128,160},{160,192},{192,224},{224... | collective-permute-start | bytes 786440 | tf_op jit(solution)/shard_map/ppermute | solution.py:343
  5.2 0.0 copy-start.2
  5.3 0.9 copy-done.2
  6.2 0.0 copy-start.7
  6.2 0.9 copy-done.7
  7.2 0.0 copy-start.1
  7.2 0.0 copy-start.4
  7.2 0.0 copy-start.6
  7.2 0.7 own.1
  7.9 0.0 copy-start
  7.9 0.0 copy-start.3
  7.9 0.0 copy-start.5
  7.9 0.1 pad_add_fusion.place_ref
  8.0 2.0 %collective-permute-done = bf16[1,8,128,128]{3,2,1,0:T(8,128)(2,1)S(1)} collective-permute-done((bf16[1,8,128,128]{3,2,1,0:T(8,128)(2,1)}, bf16[1,8,128,128]{3,2,1,0:T(8,128)(2,1)S(1)}, u32[]{:S(2)}, u32[]{:S(2)}) %collective-permute-start) | collective-permute-done | bytes 262176 | tf_op jit(solution)/shard_map/ppermute | solution.py:343
  10.0 0.0 copy-done.1
  10.0 0.0 copy-done.4
  10.0 0.0 copy-done.6
  10.0 2.6 %flow.1 = (f32[16,1,128]{2,1,0:T(1,128)S(1)}, bf16[32,8,128]{2,1,0:T(8,128)(2,1)S(1)}) custom-call(s32[3]{0:T(128)S(1)} %pad_add_fusion.place_ref, s32[2,8]{1,0:T(2,128)S(1)} %bitcast.24, s32[1,64]{1,0:T(1,128)S(1)} %bitcast.26, bf16[8,128,128]{2,1,0:T(8,128)(2,1)S(1)} %bitcast.23, f32[8,72,256]{2,1,0:T(8,128)S(1)} %get-tuple-element.13.spectrum_ref, ...), custom_call_target="tpu_custom_call" | custom-call | tf_op jit(solution)/shard_map/flow/pallas_call | solution.py:359
  12.6 15.1 %all_to_all.25.flow_ref = f32[16,1,128]{2,1,0:T(1,128)S(1)} all-to-all(f32[16,1,128]{2,1,0:T(1,128)S(1)} %get-tuple-element.15), channel_id=1, replica_groups=mesh['gz'=16,'xy'=32] {'gz'}, dimensions={0} | all-to-all | bytes 16384 | tf_op jit(solution)/shard_map/all_to_all | solution.py:318
  27.8 0.0 copy-done
  27.8 0.0 copy-done.3
  27.8 0.0 copy-done.5
  27.8 2.9 %render.1 = (f32[2,8]{1,0:T(2,128)}, bf16[32,136,128]{2,1,0:T(8,128)(2,1)S(1)}) custom-call(s32[3]{0:T(128)S(1)} %pad_add_fusion.place_ref, f32[16,16]{1,0:T(8,128)S(1)} %copy-done.3, s32[2,2]{1,0:T(2,128)S(1)} %bitcast.25, f32[16,1,128]{2,1,0:T(1,128)S(1)} %all_to_all.25.flow_ref, bf16[32,8,128]{2,1,0:T(8,128)(2,1)S(1)} %get-tuple-element.16.name_ref, ...), custom_call_target="tpu_custom_call" | custom-call | tf_op jit(solution)/shard_map/render/pallas_call | solution.py:372
  30.7 45.2 %conditional.1 = (bf16[32,136,128]{2,1,0:T(8,128)(2,1)S(1)}) conditional(s32[]{:T(128)} %convert_element_type.4, bf16[32,136,128]{2,1,0:T(8,128)(2,1)S(1)} %get-tuple-element.18, bf16[32,136,128]{2,1,0:T(8,128)(2,1)S(1)} %get-tuple-element.18), branch_computations={%region_0.1_spmd, %region_1.2_spmd} | conditional | bytes 6684680 | solution.py:384
  30.7 13.9 %all_to_all.23 = bf16[4,1088,128]{2,1,0:T(8,128)(2,1)S(1)} all-to-all(bf16[4,1088,128]{2,1,0:T(8,128)(2,1)S(1)} %bitcast.28), channel_id=1, replica_groups={{0,1,2,3},{4,5,6,7},{8,9,10,11},{12,13,14,15},{16,17,18,19},{20,21,22,2..., dimensions={0} | all-to-all | bytes 2228224 | tf_op jit(solution)/shard_map/cond/branch_1_fun/all_to_all | solution.py:318
  44.6 0.1 copy.10
  44.7 31.2 %all_to_all.24 = bf16[8,544,128]{2,1,0:T(8,128)(2,1)S(1)} all-to-all(bf16[8,544,128]{2,1,0:T(8,128)(2,1)S(1)} %bitcast.29), channel_id=1, replica_groups={{0,4,8,12,16,20,24,28},{1,5,9,13,17,21,25,29},{2,6,10,14,18,22,26,30},{..., dimensions={0} | all-to-all | bytes 2228224 | tf_op jit(solution)/shard_map/cond/branch_1_fun/all_to_all | solution.py:318
  75.9 1.5 %gather.1 = bf16[32,32,512]{2,1,0:T(8,128)(2,1)S(1)} custom-call(bf16[32,136,128]{2,1,0:T(8,128)(2,1)S(1)} %get-tuple-element.19.piece_ref), custom_call_target="tpu_custom_call" | custom-call | tf_op jit(solution)/shard_map/gather/pallas_call | solution.py:391
  77.4 23.1 %all_to_all.26 = bf16[32,32,512]{2,1,0:T(8,128)(2,1)S(1)} all-to-all(bf16[32,32,512]{2,1,0:T(8,128)(2,1)S(1)} %gather.1), channel_id=1, replica_groups=mesh['gz'=16,'xy'=32] {'xy'}, dimensions={0} | all-to-all | bytes 2097152 | tf_op jit(solution)/shard_map/all_to_all | solution.py:318
  100.5 1.1 %copy.11 = bf16[2,32,16,512]{3,2,1,0:T(8,128)(2,1)} copy(bf16[2,32,16,512]{3,2,0,1:T(8,128)(2,1)S(1)} %bitcast.32) | data formatting | bytes 2097152 | tf_op jit(solution)/shard_map/transpose | solution.py:401
Async XLA Ops:
  0.6 9.4 %collective-permute-start = (bf16[1,8,128,128]{3,2,1,0:T(8,128)(2,1)}, bf16[1,8,128,128]{3,2,1,0:T(8,128)(2,1)S(1)}, u32[]{:S(2)}, u32[]{:S(2)}) collective-permute-start(bf16[1,8,128,128]{3,2,1,0:T(8,128)(2,1)} %param.10), channel_id=1, source_target_pairs={{0,32},{32,64},{64,96},{96,128},{128,160},{160,192},{192,224},{224... | collective-permute-start | bytes 786440 | tf_op jit(solution)/shard_map/ppermute | solution.py:343
  5.2 1.0 copy-start.2
  6.2 0.9 copy-start.7
  7.2 2.9 %copy-start.1 = (bf16[928,256]{1,0:T(8,128)(2,1)S(1)}, bf16[928,256]{1,0:T(8,128)(2,1)}, u32[]{:S(2)}) copy-start(bf16[928,256]{1,0:T(8,128)(2,1)} %constant.30.clone.inverse_ref) | copy-start | bytes 1425412
  7.2 2.9 %copy-start.4 = (s32[1,8,2]{1,2,0:T(2,128)S(1)}, s32[1,8,2]{1,2,0:T(2,128)}, u32[]{:S(2)}) copy-start(s32[1,8,2]{1,2,0:T(2,128)} %param.11) | copy-start | bytes 196
  7.2 2.9 %copy-start.6 = (s32[1,64,1]{1,2,0:T(1,128)S(1)}, s32[1,64,1]{1,2,0:T(1,128)}, u32[]{:S(2)}) copy-start(s32[1,64,1]{1,2,0:T(1,128)} %param.14) | copy-start | bytes 772
  7.9 19.9 %copy-start = (bf16[1,2,512,512]{3,2,1,0:T(8,128)(2,1)S(1)}, bf16[1,2,512,512]{3,2,1,0:T(8,128)(2,1)}, u32[]{:S(2)}) copy-start(bf16[1,2,512,512]{3,2,1,0:T(8,128)(2,1)} %param.12) | copy-start | bytes 3145732
  7.9 19.9 %copy-start.3 = (f32[16,16]{1,0:T(8,128)S(1)}, f32[16,16]{1,0:T(8,128)}, u32[]{:S(2)}) copy-start(f32[16,16]{1,0:T(8,128)} %constant.31.clone.map_ref) | copy-start | bytes 3076
  7.9 19.9 %copy-start.5 = (s32[1,2,2]{2,1,0:T(2,128)S(1)}, s32[1,2,2]{2,1,0:T(2,128)}, u32[]{:S(2)}) copy-start(s32[1,2,2]{2,1,0:T(2,128)} %param.13) | copy-start | bytes 52

commit v9 on v8

--- a/solution.py
+++ b/solution.py
@@ -232,9 +232,12 @@
     position = jnp.zeros(flow_ref.shape[1:], F32)
     for s in range(sections):
         position = position + map_ref[section, s] * flow_ref[s]
+    *scratch, moved_ref, moved = scratch
     nodes = position_ref.shape[1]
     for c in range(2):
-        position_ref[c : c + 1, :] = position[:, c * nodes : (c + 1) * nodes]
+        moved_ref[c : c + 1, :] = position[:, c * nodes : (c + 1) * nodes]
+    leaving = pltpu.make_async_copy(moved_ref, position_ref, moved)
+    leaving.start()
     per_tile = nodes // tile_count
     lanes = lax.broadcasted_iota(jnp.int32, position.shape, 1)
     height = edge // slots
@@ -256,7 +259,10 @@
         for c in range(edge // chunk):
             rows = slice(c * chunk, (c + 1) * chunk)
             first, last = c * chunk // height, (c + 1) * chunk // height
-            done = dot(row_ref[rows, :], pass_ref[...]).astype(BF)
+            near = range(max(c - 1, 0), min(c + 2, edge // chunk))
+            from_row = near[0] * chunk // (edge // 2) * (edge // 2)
+            to_row = edge // 2 if near[-1] * chunk < edge // 2 else edge
+            done = dot(row_ref[rows, from_row:to_row], pass_ref[from_row:to_row, :]).astype(BF)
             done = done.reshape(last - first, height, edge)
             for p in range(first, last):
                 for j in range(columns):
@@ -267,6 +273,7 @@
     tail = tile_count * columns * height
     for p in range(slots):
         send_ref[slot_of(p), tail:, :] = name_ref[p]
+    leaving.wait()
 
 
 def gather_kernel(piece_ref, out_ref, data_ref):
@@ -302,6 +309,20 @@
         out_ref[first:last] = total.astype(BF).reshape(last - first, out_rows, edge)
 
 
+def place_kernel(cell_ref, out_ref, arrived):
+    height = out_ref.shape[2]
+    copies = [
+        pltpu.make_async_copy(
+            cell_ref.at[:, g * height : (g + 1) * height, :], out_ref.at[g], arrived.at[g]
+        )
+        for g in range(out_ref.shape[0])
+    ]
+    for copy in copies:
+        copy.start()
+    for copy in copies:
+        copy.wait()
+
+
 def in_vmem():
     return pl.BlockSpec(memory_space=pltpu.VMEM)
 
@@ -376,8 +397,9 @@
             jax.ShapeDtypeStruct((PIECES, tile_count * height * edge // EXTENT + 8, EXTENT), BF),
         ),
         in_specs=[in_smem()] * 3 + [in_vmem()] * 3,
-        out_specs=(in_vmem(), in_vmem()),
-        scratch_shapes=[pltpu.VMEM((edge, edge), BF)] * (3 * tile_count),
+        out_specs=(pl.BlockSpec(memory_space=pl.ANY), in_vmem()),
+        scratch_shapes=[pltpu.VMEM((edge, edge), BF)] * (3 * tile_count)
+        + [pltpu.VMEM((2, count), F32), pltpu.SemaphoreType.DMA],
         compiler_params=params(),
         name="render",
     )(place, jnp.asarray(relaxation_map(sections)), band_offsets[0], flow, names, tiles[0])
@@ -398,7 +420,15 @@
         name="gather",
     )(pieces)
     cells = exchange(cells, "xy")
-    rendered = cells.reshape(PIECES, share, height, edge).transpose(1, 0, 2, 3)
+    rendered = pl.pallas_call(
+        place_kernel,
+        out_shape=jax.ShapeDtypeStruct((share, PIECES, height, edge), BF),
+        in_specs=[in_vmem()],
+        out_specs=pl.BlockSpec(memory_space=pl.ANY),
+        scratch_shapes=[pltpu.SemaphoreType.DMA((share,))],
+        compiler_params=params(),
+        name="place",
+    )(cells)
     rendered = rendered.reshape(1, share, edge, edge)
     return position[None], rendered
 

time: 102 us -> 102 us (level)
  local copies, waits for them, and re-layouts: 3.06 us -> 2.01 us
    transpose x1 -> x0, local copies, waits for them, and re-layouts: 1.05 us -> none  [body(): rendered = cells.reshape(PIECES, share, height, edge).transpose(1, 0, 2, 3)]
where the time goes in v9:
time: 102 us; the launch traced here: 101 us
  blocking collectives  83.4 us (82%)
  Pallas kernels  8.53 us (8%)
  starting transfers between devices  4.59 us (4%)
  local copies, waits for them, and re-layouts  2.01 us (2%)
  waiting for transfers between devices  2 us (2%)
    all_to_all x4, blocking collectives, exchange(): lax.all_to_all(value, axis, split_axis=0, concat_axis=0, tiled=True, axis...  83.4 us
    ppermute x1, starting transfers between devices, body(): lax.ppermute(patches, 'gz', [(i, i + 1) for i in range(sections - 1)])  4.59 us
    pallas_call x1, Pallas kernels, body(): pl.pallas_call(render_kernel, out_shape=(jax.ShapeDtypeStruct((2, count),...  2.68 us
    pallas_call x1, Pallas kernels, body(): pl.pallas_call(flow_kernel, out_shape=(jax.ShapeDtypeStruct((sections, 1,...  2.59 us
  transfers between devices with their start and end apart: 1, of which 1 were waited for; matrix products, arithmetic and copies ran while one was open for 0% of the time, Pallas kernels for 1%

profile of v9, /device:TPU:1, one launch (start us, length us, event | category | flops | bytes accessed | tf_op | source)
XLA Modules:
  0.0 101.4 jit_solution(15871743861627441444)
XLA Ops:
  0.6 4.6 %collective-permute-start = (bf16[1,8,128,128]{3,2,1,0:T(8,128)(2,1)}, bf16[1,8,128,128]{3,2,1,0:T(8,128)(2,1)S(1)}, u32[]{:S(2)}, u32[]{:S(2)}) collective-permute-start(bf16[1,8,128,128]{3,2,1,0:T(8,128)(2,1)} %param.10), channel_id=1, source_target_pairs={{0,32},{32,64},{64,96},{96,128},{128,160},{160,192},{192,224},{224... | collective-permute-start | bytes 786440 | tf_op jit(solution)/shard_map/ppermute | solution.py:364
  5.2 0.0 copy-start.2
  5.3 0.9 copy-done.2
  6.2 0.0 copy-start.7
  6.2 0.9 copy-done.7
  7.2 0.0 copy-start.1
  7.2 0.0 copy-start.4
  7.2 0.0 copy-start.6
  7.2 0.7 own.1
  7.9 0.0 copy-start
  7.9 0.0 copy-start.3
  7.9 0.0 copy-start.5
  7.9 0.1 pad_add_fusion.place_ref
  8.0 2.0 %collective-permute-done = bf16[1,8,128,128]{3,2,1,0:T(8,128)(2,1)S(1)} collective-permute-done((bf16[1,8,128,128]{3,2,1,0:T(8,128)(2,1)}, bf16[1,8,128,128]{3,2,1,0:T(8,128)(2,1)S(1)}, u32[]{:S(2)}, u32[]{:S(2)}) %collective-permute-start) | collective-permute-done | bytes 262176 | tf_op jit(solution)/shard_map/ppermute | solution.py:364
  10.0 0.0 copy-done.1
  10.0 0.0 copy-done.4
  10.0 0.0 copy-done.6
  10.0 2.6 %flow.1 = (f32[16,1,128]{2,1,0:T(1,128)S(1)}, bf16[32,8,128]{2,1,0:T(8,128)(2,1)S(1)}) custom-call(s32[3]{0:T(128)S(1)} %pad_add_fusion.place_ref, s32[2,8]{1,0:T(2,128)S(1)} %bitcast.21, s32[1,64]{1,0:T(1,128)S(1)} %bitcast.23, bf16[8,128,128]{2,1,0:T(8,128)(2,1)S(1)} %bitcast.20, f32[8,72,256]{2,1,0:T(8,128)S(1)} %get-tuple-element.13.spectrum_ref, ...), custom_call_target="tpu_custom_call" | custom-call | tf_op jit(solution)/shard_map/flow/pallas_call | solution.py:380
  12.6 15.1 %all_to_all.25.flow_ref = f32[16,1,128]{2,1,0:T(1,128)S(1)} all-to-all(f32[16,1,128]{2,1,0:T(1,128)S(1)} %get-tuple-element.15), channel_id=1, replica_groups=mesh['gz'=16,'xy'=32] {'gz'}, dimensions={0} | all-to-all | bytes 16384 | tf_op jit(solution)/shard_map/all_to_all | solution.py:339
  27.8 0.0 copy-done
  27.8 0.0 copy-done.3
  27.8 0.0 copy-done.5
  27.8 2.7 %render.1 = (f32[2,8]{1,0:T(2,128)}, bf16[32,136,128]{2,1,0:T(8,128)(2,1)S(1)}) custom-call(s32[3]{0:T(128)S(1)} %pad_add_fusion.place_ref, f32[16,16]{1,0:T(8,128)S(1)} %copy-done.3, s32[2,2]{1,0:T(2,128)S(1)} %bitcast.22, f32[16,1,128]{2,1,0:T(1,128)S(1)} %all_to_all.25.flow_ref, bf16[32,8,128]{2,1,0:T(8,128)(2,1)S(1)} %get-tuple-element.16.name_ref, ...), custom_call_target="tpu_custom_call" | custom-call | tf_op jit(solution)/shard_map/render/pallas_call | solution.py:393
  30.5 45.4 %conditional.1 = (bf16[32,136,128]{2,1,0:T(8,128)(2,1)S(1)}) conditional(s32[]{:T(128)} %convert_element_type.4, bf16[32,136,128]{2,1,0:T(8,128)(2,1)S(1)} %get-tuple-element.18, bf16[32,136,128]{2,1,0:T(8,128)(2,1)S(1)} %get-tuple-element.18), branch_computations={%region_0.1_spmd, %region_1.2_spmd} | conditional | bytes 6684680 | solution.py:406
  30.5 13.9 %all_to_all.23 = bf16[4,1088,128]{2,1,0:T(8,128)(2,1)S(1)} all-to-all(bf16[4,1088,128]{2,1,0:T(8,128)(2,1)S(1)} %bitcast.25), channel_id=1, replica_groups={{0,1,2,3},{4,5,6,7},{8,9,10,11},{12,13,14,15},{16,17,18,19},{20,21,22,2..., dimensions={0} | all-to-all | bytes 2228224 | tf_op jit(solution)/shard_map/cond/branch_1_fun/all_to_all | solution.py:339
  44.4 0.1 copy.10
  44.5 31.4 %all_to_all.24 = bf16[8,544,128]{2,1,0:T(8,128)(2,1)S(1)} all-to-all(bf16[8,544,128]{2,1,0:T(8,128)(2,1)S(1)} %bitcast.26), channel_id=1, replica_groups={{0,4,8,12,16,20,24,28},{1,5,9,13,17,21,25,29},{2,6,10,14,18,22,26,30},{..., dimensions={0} | all-to-all | bytes 2228224 | tf_op jit(solution)/shard_map/cond/branch_1_fun/all_to_all | solution.py:339
  75.9 1.5 %gather.1 = bf16[32,32,512]{2,1,0:T(8,128)(2,1)S(1)} custom-call(bf16[32,136,128]{2,1,0:T(8,128)(2,1)S(1)} %get-tuple-element.19.piece_ref), custom_call_target="tpu_custom_call" | custom-call | tf_op jit(solution)/shard_map/gather/pallas_call | solution.py:413
  77.4 23.0 %all_to_all.26.cell_ref = bf16[32,32,512]{2,1,0:T(8,128)(2,1)S(1)} all-to-all(bf16[32,32,512]{2,1,0:T(8,128)(2,1)S(1)} %gather.1), channel_id=1, replica_groups=mesh['gz'=16,'xy'=32] {'xy'}, dimensions={0} | all-to-all | bytes 2097152 | tf_op jit(solution)/shard_map/all_to_all | solution.py:339
  100.4 1.0 place.1
Async XLA Ops:
  0.6 9.4 %collective-permute-start = (bf16[1,8,128,128]{3,2,1,0:T(8,128)(2,1)}, bf16[1,8,128,128]{3,2,1,0:T(8,128)(2,1)S(1)}, u32[]{:S(2)}, u32[]{:S(2)}) collective-permute-start(bf16[1,8,128,128]{3,2,1,0:T(8,128)(2,1)} %param.10), channel_id=1, source_target_pairs={{0,32},{32,64},{64,96},{96,128},{128,160},{160,192},{192,224},{224... | collective-permute-start | bytes 786440 | tf_op jit(solution)/shard_map/ppermute | solution.py:364
  5.2 1.0 copy-start.2
  6.2 0.9 copy-start.7
  7.2 2.9 %copy-start.1 = (bf16[928,256]{1,0:T(8,128)(2,1)S(1)}, bf16[928,256]{1,0:T(8,128)(2,1)}, u32[]{:S(2)}) copy-start(bf16[928,256]{1,0:T(8,128)(2,1)} %constant.30.clone.inverse_ref) | copy-start | bytes 1425412
  7.2 2.9 %copy-start.4 = (s32[1,8,2]{1,2,0:T(2,128)S(1)}, s32[1,8,2]{1,2,0:T(2,128)}, u32[]{:S(2)}) copy-start(s32[1,8,2]{1,2,0:T(2,128)} %param.11) | copy-start | bytes 196
  7.2 2.9 %copy-start.6 = (s32[1,64,1]{1,2,0:T(1,128)S(1)}, s32[1,64,1]{1,2,0:T(1,128)}, u32[]{:S(2)}) copy-start(s32[1,64,1]{1,2,0:T(1,128)} %param.14) | copy-start | bytes 772
  7.9 19.9 %copy-start = (bf16[1,2,512,512]{3,2,1,0:T(8,128)(2,1)S(1)}, bf16[1,2,512,512]{3,2,1,0:T(8,128)(2,1)}, u32[]{:S(2)}) copy-start(bf16[1,2,512,512]{3,2,1,0:T(8,128)(2,1)} %param.12) | copy-start | bytes 3145732
  7.9 19.9 %copy-start.3 = (f32[16,16]{1,0:T(8,128)S(1)}, f32[16,16]{1,0:T(8,128)}, u32[]{:S(2)}) copy-start(f32[16,16]{1,0:T(8,128)} %constant.31.clone.map_ref) | copy-start | bytes 3076
  7.9 19.9 %copy-start.5 = (s32[1,2,2]{2,1,0:T(2,128)S(1)}, s32[1,2,2]{2,1,0:T(2,128)}, u32[]{:S(2)}) copy-start(s32[1,2,2]{2,1,0:T(2,128)} %param.13) | copy-start | bytes 52

commit v10 on v9

--- a/solution.py
+++ b/solution.py
@@ -120,20 +120,17 @@
         own = jnp.sum(jnp.where(lane == slot + t * slots, names, 0.0), axis=1, keepdims=True)
         row = jnp.where(here & (place // height % tile_count == t), own, row)
     for p in range(slots):
-        name_ref[p] = jnp.broadcast_to(row[p : p + 1], (8, EXTENT)).astype(BF)
+        name_ref[p] = row[p : p + 1]
 
 
 def flow_kernel(place_ref, peak_ref, route_ref, low_ref, spectrum_ref, energy_ref, table_ref, inverse_ref, out_ref, name_ref):
     count = low_ref.shape[0]
     write_names(place_ref[0], route_ref, name_ref)
     crosses = []
-    for pair in range(0, count, 2):
-        block = []
-        for k, (lr, li) in enumerate(spectra([low_ref[pair], low_ref[pair + 1]], table_ref)):
-            nr = spectrum_ref[pair + k, :, :EXTENT]
-            ni = spectrum_ref[pair + k, :, EXTENT:]
-            block.append(jnp.concatenate([nr * lr + ni * li, ni * lr - nr * li], 1))
-        crosses.append(jnp.concatenate(block, 0))
+    for n, (lr, li) in enumerate(spectra([low_ref[n] for n in range(count)], table_ref)):
+        nr = spectrum_ref[n, :, :EXTENT]
+        ni = spectrum_ref[n, :, EXTENT:]
+        crosses.append(jnp.concatenate([nr * lr + ni * li, ni * lr - nr * li], 1))
     third = 6 * EXTENT
     fourth = jnp.concatenate(
         [
@@ -142,13 +139,13 @@
         ],
         1,
     )
+    high, low = split(jnp.concatenate(crosses, 0))
+    outer = dot(jnp.concatenate([high, low, high], 1), inverse_ref[:third])
     correlations = []
-    for cross in crosses:
-        high, low = split(cross)
-        outer = dot(jnp.concatenate([high, low, high], 1), inverse_ref[:third])
+    for pair in range(0, count, 2):
         columns = []
-        for k in range(2):
-            block = outer[HALF * k : HALF * (k + 1)]
+        for n in (pair, pair + 1):
+            block = outer[HALF * n : HALF * (n + 1)]
             columns.append(jnp.concatenate([block[:, :EXTENT], block[:, EXTENT:]], 0))
         high, low = split(jnp.concatenate(columns, 1))
         result = dot(fourth, jnp.concatenate([high, low, high], 0))
@@ -224,11 +221,6 @@
     tile_count, edge, _ = tile_ref.shape
     slots = send_ref.shape[0]
     section = place_ref[1]
-    second_core = place_ref[2] == 1
-
-    def slot_of(p):
-        return jnp.where(second_core, p % WIDE * (slots // WIDE) + p // WIDE, p)
-
     position = jnp.zeros(flow_ref.shape[1:], F32)
     for s in range(sections):
         position = position + map_ref[section, s] * flow_ref[s]
@@ -264,26 +256,25 @@
             to_row = edge // 2 if near[-1] * chunk < edge // 2 else edge
             done = dot(row_ref[rows, from_row:to_row], pass_ref[from_row:to_row, :]).astype(BF)
             done = done.reshape(last - first, height, edge)
-            for p in range(first, last):
-                for j in range(columns):
-                    at = (t * columns + j) * height
-                    send_ref[slot_of(p), at : at + height, :] = done[
-                        p - first, :, j * EXTENT : (j + 1) * EXTENT
-                    ]
+            for j in range(columns):
+                at = (t * columns + j) * height
+                send_ref[first:last, at : at + height, :] = done[:, :, j * EXTENT : (j + 1) * EXTENT]
     tail = tile_count * columns * height
-    for p in range(slots):
-        send_ref[slot_of(p), tail:, :] = name_ref[p]
+    if send_ref.shape[1] > tail:
+        for p in range(slots):
+            send_ref[p, tail:, :] = jnp.broadcast_to(name_ref[p], (8, EXTENT)).astype(BF)
     leaving.wait()
 
 
-def gather_kernel(piece_ref, out_ref, data_ref):
-    owners, rows, _ = piece_ref.shape
+def gather_kernel(piece_ref, *refs):
+    *name_refs, out_ref, data_ref = refs
+    owners = piece_ref.shape[0]
     _, out_rows, edge = out_ref.shape
     height = edge // owners
     columns = edge // EXTENT
-    tile_count = (rows - 8) // (columns * height)
-    tail = rows - 8
-    share = EXTENT // (tile_count * height)
+    tile_count = EXTENT // WIDE // height
+    tail = tile_count * columns * height
+    name_ref = name_refs[0] if name_refs else piece_ref.at[:, tail:]
     lane_row = lax.broadcasted_iota(jnp.int32, (EXTENT, EXTENT), 1) % height
     sub = lax.broadcasted_iota(jnp.int32, (EXTENT, EXTENT), 0)
     same = lane_row == sub % height
@@ -296,8 +287,8 @@
                     d, source : source + height, :
                 ]
     names = [
-        sum(piece_ref[d, tail : tail + 8, :].astype(F32) for d in range(start, start + share))[0:1]
-        for start in range(0, owners, share)
+        sum(name_ref[d].astype(F32) for d in range(start, start + WIDE))[0:1]
+        for start in range(0, owners, WIDE)
     ]
     for c in range(owners * out_rows // EXTENT):
         group = (sub // height + c * (EXTENT // height)).astype(F32)
@@ -335,21 +326,8 @@
     return pltpu.CompilerParams(vmem_limit_bytes=40 * 1024 * 1024)
 
 
-def exchange(value, axis, groups=None):
-    return lax.all_to_all(
-        value, axis, split_axis=0, concat_axis=0, tiled=True, axis_index_groups=groups
-    )
-
-
-def exchange_x_then_z(value):
-    owners, rows, lanes = value.shape
-    high = owners // WIDE
-    along_x = [[z * WIDE + x for x in range(WIDE)] for z in range(high)]
-    along_z = [[z * WIDE + x for z in range(high)] for x in range(WIDE)]
-    value = exchange(value.reshape(WIDE, high * rows, lanes), "xy", along_x)
-    value = value.reshape(WIDE, high, rows, lanes).transpose(1, 0, 2, 3)
-    value = exchange(value.reshape(high, WIDE * rows, lanes), "xy", along_z)
-    return value.reshape(owners, rows, lanes)
+def exchange(value, axis):
+    return lax.all_to_all(value, axis, split_axis=0, concat_axis=0, tiled=True)
 
 
 def body(patches, peak_offsets, tiles, band_offsets, routes):
@@ -381,7 +359,7 @@
         flow_kernel,
         out_shape=(
             jax.ShapeDtypeStruct((sections, 1, EXTENT), F32),
-            jax.ShapeDtypeStruct((PIECES, 8, EXTENT), BF),
+            jax.ShapeDtypeStruct((PIECES, 1, EXTENT), F32),
         ),
         in_specs=[in_smem()] * 2 + [in_vmem()] * 6,
         out_specs=(in_vmem(),) * 2,
@@ -390,35 +368,46 @@
     )(place, peak_offsets[0].T, routes[0].T, below[0], spectrum, power, early_table, late_table)
     flow = exchange(flow, "gz")
 
-    position, pieces = pl.pallas_call(
-        render_kernel,
-        out_shape=(
-            jax.ShapeDtypeStruct((2, count), F32),
-            jax.ShapeDtypeStruct((PIECES, tile_count * height * edge // EXTENT + 8, EXTENT), BF),
-        ),
-        in_specs=[in_smem()] * 3 + [in_vmem()] * 3,
-        out_specs=(pl.BlockSpec(memory_space=pl.ANY), in_vmem()),
-        scratch_shapes=[pltpu.VMEM((edge, edge), BF)] * (3 * tile_count)
-        + [pltpu.VMEM((2, count), F32), pltpu.SemaphoreType.DMA],
-        compiler_params=params(),
-        name="render",
-    )(place, jnp.asarray(relaxation_map(sections)), band_offsets[0], flow, names, tiles[0])
-    pieces = lax.cond(
-        second_core,
-        exchange_x_then_z,
-        lambda value: exchange(value, "xy"),
-        pieces,
-    )
-
-    cells = pl.pallas_call(
-        gather_kernel,
-        out_shape=jax.ShapeDtypeStruct((owners, share * height, edge), BF),
-        in_specs=[in_vmem()],
-        out_specs=in_vmem(),
-        scratch_shapes=[pltpu.VMEM((owners * tile_count * height, edge), BF)],
-        compiler_params=params(),
-        name="gather",
-    )(pieces)
+    linear = jnp.asarray(relaxation_map(sections))
+    piece_rows = tile_count * height * edge // EXTENT
+
+    def render(flow, image, names, rows):
+        return pl.pallas_call(
+            render_kernel,
+            out_shape=(
+                jax.ShapeDtypeStruct((2, count), F32),
+                jax.ShapeDtypeStruct((PIECES, rows, EXTENT), BF),
+            ),
+            in_specs=[in_smem()] * 3 + [in_vmem()] * 3,
+            out_specs=(pl.BlockSpec(memory_space=pl.ANY), in_vmem()),
+            scratch_shapes=[pltpu.VMEM((edge, edge), BF)] * (3 * tile_count)
+            + [pltpu.VMEM((2, count), F32), pltpu.SemaphoreType.DMA],
+            compiler_params=params(),
+            name="render",
+        )(place, linear, band_offsets[0], flow, names, image)
+
+    def gather(*received):
+        return pl.pallas_call(
+            gather_kernel,
+            out_shape=jax.ShapeDtypeStruct((owners, share * height, edge), BF),
+            in_specs=[in_vmem()] * len(received),
+            out_specs=in_vmem(),
+            scratch_shapes=[pltpu.VMEM((owners * tile_count * height, edge), BF)],
+            compiler_params=params(),
+            name="gather",
+        )(*received)
+
+    def together(flow, image, names):
+        position, whole = render(flow, image, names, piece_rows + 8)
+        return position, gather(exchange(whole, "xy"))
+
+    def names_ahead(flow, image, names):
+        position, pieces = render(flow, image, names, piece_rows)
+        names, pieces = lax.optimization_barrier((names, pieces))
+        names, pieces = lax.optimization_barrier((exchange(names, "xy"), pieces))
+        return position, gather(exchange(pieces, "xy"), names)
+
+    position, cells = lax.cond(second_core, names_ahead, together, flow, tiles[0], names)
     cells = exchange(cells, "xy")
     rendered = pl.pallas_call(
         place_kernel,

time: 102 us -> 103 us (level)
  blocking collectives: 83.4 us -> 85 us
    all_to_all x4, blocking collectives: 83.4 us -> 85 us  [exchange(): return lax.all_to_all(value, axis, split_axis=0, concat_axis=0, tiled=True)]
where the time goes in v10:
time: 103 us
  blocking collectives  85 us (83%)
  Pallas kernels  8.28 us (8%)
  starting transfers between devices  4.59 us (4%)
  waiting for transfers between devices  2 us (2%)
  local copies, waits for them, and re-layouts  1.93 us (2%)
    all_to_all x4, blocking collectives, exchange(): return lax.all_to_all(value, axis, split_axis=0, concat_axis=0, tiled=True)  85 us
    ppermute x1, starting transfers between devices, body(): lax.ppermute(patches, 'gz', [(i, i + 1) for i in range(sections - 1)])  4.59 us
    pallas_call x1, Pallas kernels, render(): pl.pallas_call(render_kernel, out_shape=(jax.ShapeDtypeStruct((2, count),...  2.66 us
    pallas_call x1, Pallas kernels, body(): pl.pallas_call(flow_kernel, out_shape=(jax.ShapeDtypeStruct((sections, 1,...  2.39 us
  transfers between devices with their start and end apart: 1, of which 1 were waited for; matrix products, arithmetic and copies ran while one was open for 0% of the time, Pallas kernels for 1%

profile of v10, /device:TPU:1, one launch (start us, length us, event | category | flops | bytes accessed | tf_op | source)
XLA Modules:
  0.0 102.7 jit_solution(16746639057724854029)
XLA Ops:
  0.6 4.6 %collective-permute-start = (bf16[1,8,128,128]{3,2,1,0:T(8,128)(2,1)}, bf16[1,8,128,128]{3,2,1,0:T(8,128)(2,1)S(1)}, u32[]{:S(2)}, u32[]{:S(2)}) collective-permute-start(bf16[1,8,128,128]{3,2,1,0:T(8,128)(2,1)} %param.10), channel_id=1, source_target_pairs={{0,32},{32,64},{64,96},{96,128},{128,160},{160,192},{192,224},{224... | collective-permute-start | bytes 786440 | tf_op jit(solution)/shard_map/ppermute | solution.py:342
  5.2 0.0 copy-start.1
  5.3 0.9 copy-done.1
  6.2 0.0 copy-start.4
  6.2 0.9 copy-done.4
  7.2 0.0 copy-start
  7.2 0.0 copy-start.2
  7.2 0.0 copy-start.3
  7.2 0.7 own.1
  7.9 0.0 copy-start.5
  7.9 0.0 copy-start.6
  7.9 0.0 copy-start.7
  7.9 0.1 pad_add_fusion.place_ref
  8.0 2.0 %collective-permute-done = bf16[1,8,128,128]{3,2,1,0:T(8,128)(2,1)S(1)} collective-permute-done((bf16[1,8,128,128]{3,2,1,0:T(8,128)(2,1)}, bf16[1,8,128,128]{3,2,1,0:T(8,128)(2,1)S(1)}, u32[]{:S(2)}, u32[]{:S(2)}) %collective-permute-start) | collective-permute-done | bytes 262176 | tf_op jit(solution)/shard_map/ppermute | solution.py:342
  10.0 0.0 copy-done
  10.0 0.0 copy-done.2
  10.0 0.0 copy-done.3
  10.0 2.4 %flow.1 = (f32[16,1,128]{2,1,0:T(1,128)S(1)}, f32[32,1,128]{2,1,0:T(1,128)S(1)}) custom-call(s32[3]{0:T(128)S(1)} %pad_add_fusion.place_ref, s32[2,8]{1,0:T(2,128)S(1)} %bitcast.15, s32[1,64]{1,0:T(1,128)S(1)} %bitcast.16, bf16[8,128,128]{2,1,0:T(8,128)(2,1)S(1)} %bitcast.14, f32[8,72,256]{2,1,0:T(8,128)S(1)} %get-tuple-element.52.spectrum_ref, ...), custom_call_target="tpu_custom_call" | custom-call | tf_op jit(solution)/shard_map/flow/pallas_call | solution.py:358
  12.4 15.2 %all_to_all.25 = f32[16,1,128]{2,1,0:T(1,128)S(1)} all-to-all(f32[16,1,128]{2,1,0:T(1,128)S(1)} %get-tuple-element.54), channel_id=1, replica_groups=mesh['gz'=16,'xy'=32] {'gz'}, dimensions={0} | all-to-all | bytes 16384 | tf_op jit(solution)/shard_map/all_to_all | solution.py:330
  27.6 0.0 copy-done.5
  27.6 0.0 copy-done.6
  27.6 0.0 copy-done.7
  27.6 47.4 %conditional.1 = (f32[2,8]{1,0:T(2,128)}, bf16[32,32,512]{2,1,0:T(8,128)(2,1)S(1)}) conditional(s32[]{:T(128)} %convert_element_type.4, (s32[1,2,2]{2,1,0:T(2,128)S(1)}, s32[3]{0:T(128)S(1)}, f32[16,16]{1,0:T(8,128)S(1)}, f32[16,1,128]{2,1,0:T(1,128)S(1)}, f32[32,1,128]{2,1,0:T(1,128)S(1)}, /*index=5*/bf16[2,512,512]{2,1,0:T(8,128)(2,1)S(1)}) %tuple.26, ...), branch_computations={%region_0.1_spmd, %region_1.2_spmd} | conditional | bytes 2228240 | solution.py:410
  27.6 2.7 %render.3 = (f32[2,8]{1,0:T(2,128)}, bf16[32,128,128]{2,1,0:T(8,128)(2,1)S(1)}) custom-call(s32[3]{0:T(128)S(1)} %get-tuple-element.32.place_ref, f32[16,16]{1,0:T(8,128)S(1)} %get-tuple-element.33.map_ref, s32[2,2]{1,0:T(2,128)S(1)} %bitcast.22, f32[16,1,128]{2,1,0:T(1,128)S(1)} %get-tuple-element.35.flow_ref, ...), custom_call_target="tpu_custom_call" | custom-call | tf_op jit(solution)/shard_map/cond/branch_1_fun/render/pallas_call | solution.py:375
  30.3 21.4 %all_to_all.23.refs_0_ = f32[32,1,128]{2,1,0:T(1,128)S(1)} all-to-all(f32[32,1,128]{2,1,0:T(1,128)S(1)} %get-tuple-element.40.name_ref), channel_id=1, replica_groups=mesh['gz'=16,'xy'=32] {'xy'}, dimensions={0} | all-to-all | bytes 32768 | tf_op jit(solution)/shard_map/cond/branch_1_fun/all_to_all | solution.py:330
  51.7 21.8 %all_to_all.24.piece_ref = bf16[32,128,128]{2,1,0:T(8,128)(2,1)S(1)} all-to-all(bf16[32,128,128]{2,1,0:T(8,128)(2,1)S(1)} %get-tuple-element.42), channel_id=1, replica_groups=mesh['gz'=16,'xy'=32] {'xy'}, dimensions={0} | all-to-all | bytes 2097152 | tf_op jit(solution)/shard_map/cond/branch_1_fun/all_to_all | solution.py:330
  73.5 1.5 %gather.3 = bf16[32,32,512]{2,1,0:T(8,128)(2,1)S(1)} custom-call(bf16[32,128,128]{2,1,0:T(8,128)(2,1)S(1)} %all_to_all.24.piece_ref, f32[32,1,128]{2,1,0:T(1,128)S(1)} %all_to_all.23.refs_0_), custom_call_target="tpu_custom_call" | custom-call | tf_op jit(solution)/shard_map/cond/branch_1_fun/gather/pallas_call | solution.py:390
  75.0 26.7 %all_to_all.26.cell_ref = bf16[32,32,512]{2,1,0:T(8,128)(2,1)S(1)} all-to-all(bf16[32,32,512]{2,1,0:T(8,128)(2,1)S(1)} %get-tuple-element.57), channel_id=1, replica_groups=mesh['gz'=16,'xy'=32] {'xy'}, dimensions={0} | all-to-all | bytes 2097152 | tf_op jit(solution)/shard_map/all_to_all | solution.py:330
  101.7 1.0 place.1
Async XLA Ops:
  0.6 9.4 %collective-permute-start = (bf16[1,8,128,128]{3,2,1,0:T(8,128)(2,1)}, bf16[1,8,128,128]{3,2,1,0:T(8,128)(2,1)S(1)}, u32[]{:S(2)}, u32[]{:S(2)}) collective-permute-start(bf16[1,8,128,128]{3,2,1,0:T(8,128)(2,1)} %param.10), channel_id=1, source_target_pairs={{0,32},{32,64},{64,96},{96,128},{128,160},{160,192},{192,224},{224... | collective-permute-start | bytes 786440 | tf_op jit(solution)/shard_map/ppermute | solution.py:342
  5.2 1.0 copy-start.1
  6.2 0.9 copy-start.4
  7.2 2.9 %copy-start = (bf16[928,256]{1,0:T(8,128)(2,1)S(1)}, bf16[928,256]{1,0:T(8,128)(2,1)}, u32[]{:S(2)}) copy-start(bf16[928,256]{1,0:T(8,128)(2,1)} %constant.30.clone.inverse_ref) | copy-start | bytes 1425412
  7.2 2.9 %copy-start.2 = (s32[1,8,2]{1,2,0:T(2,128)S(1)}, s32[1,8,2]{1,2,0:T(2,128)}, u32[]{:S(2)}) copy-start(s32[1,8,2]{1,2,0:T(2,128)} %param.11) | copy-start | bytes 196
  7.2 2.9 %copy-start.3 = (s32[1,64,1]{1,2,0:T(1,128)S(1)}, s32[1,64,1]{1,2,0:T(1,128)}, u32[]{:S(2)}) copy-start(s32[1,64,1]{1,2,0:T(1,128)} %param.14) | copy-start | bytes 772
  7.9 19.7 %copy-start.5 = (bf16[1,2,512,512]{3,2,1,0:T(8,128)(2,1)S(1)}, bf16[1,2,512,512]{3,2,1,0:T(8,128)(2,1)}, u32[]{:S(2)}) copy-start(bf16[1,2,512,512]{3,2,1,0:T(8,128)(2,1)} %param.12) | copy-start | bytes 3145732
  7.9 19.7 %copy-start.6 = (f32[16,16]{1,0:T(8,128)S(1)}, f32[16,16]{1,0:T(8,128)}, u32[]{:S(2)}) copy-start(f32[16,16]{1,0:T(8,128)} %constant.31.clone) | copy-start | bytes 3076
  7.9 19.7 %copy-start.7 = (s32[1,2,2]{2,1,0:T(2,128)S(1)}, s32[1,2,2]{2,1,0:T(2,128)}, u32[]{:S(2)}) copy-start(s32[1,2,2]{2,1,0:T(2,128)} %param.13) | copy-start | bytes 52

commit v11 on v8

--- a/solution.py
+++ b/solution.py
@@ -8,6 +8,7 @@
 
 PIECES = 32
 WIDE = 4
+SHARE = 8
 BAND = 6
 RELAX = 3
 EPSILON = 1e-06
@@ -109,12 +110,12 @@
 def write_names(owner, route_ref, name_ref):
     slots = name_ref.shape[0]
     tile_count = route_ref.shape[1] // slots
-    height = EXTENT // WIDE // tile_count
+    height = EXTENT // SHARE // tile_count
     lane = lax.broadcasted_iota(jnp.int32, (slots, tile_count * slots), 1)
     slot = lax.broadcasted_iota(jnp.int32, (slots, tile_count * slots), 0)
     names = jnp.broadcast_to(route_ref[...], lane.shape).astype(F32)
     place = lax.broadcasted_iota(jnp.int32, (slots, EXTENT), 1)
-    here = place // (tile_count * height) == owner % WIDE
+    here = place // (tile_count * height) == (owner & (SHARE - 1))
     row = jnp.zeros((slots, EXTENT), F32)
     for t in range(tile_count):
         own = jnp.sum(jnp.where(lane == slot + t * slots, names, 0.0), axis=1, keepdims=True)
@@ -125,15 +126,12 @@
 
 def flow_kernel(place_ref, peak_ref, route_ref, low_ref, spectrum_ref, energy_ref, table_ref, inverse_ref, out_ref, name_ref):
     count = low_ref.shape[0]
-    write_names(place_ref[0], route_ref, name_ref)
+    write_names(place_ref[:, :1], route_ref, name_ref)
     crosses = []
-    for pair in range(0, count, 2):
-        block = []
-        for k, (lr, li) in enumerate(spectra([low_ref[pair], low_ref[pair + 1]], table_ref)):
-            nr = spectrum_ref[pair + k, :, :EXTENT]
-            ni = spectrum_ref[pair + k, :, EXTENT:]
-            block.append(jnp.concatenate([nr * lr + ni * li, ni * lr - nr * li], 1))
-        crosses.append(jnp.concatenate(block, 0))
+    for n, (lr, li) in enumerate(spectra([low_ref[n] for n in range(count)], table_ref)):
+        nr = spectrum_ref[n, :, :EXTENT]
+        ni = spectrum_ref[n, :, EXTENT:]
+        crosses.append(jnp.concatenate([nr * lr + ni * li, ni * lr - nr * li], 1))
     third = 6 * EXTENT
     fourth = jnp.concatenate(
         [
@@ -142,13 +140,13 @@
         ],
         1,
     )
+    high, low = split(jnp.concatenate(crosses, 0))
+    outer = dot(jnp.concatenate([high, low, high], 1), inverse_ref[:third])
     correlations = []
-    for cross in crosses:
-        high, low = split(cross)
-        outer = dot(jnp.concatenate([high, low, high], 1), inverse_ref[:third])
+    for pair in range(0, count, 2):
         columns = []
-        for k in range(2):
-            block = outer[HALF * k : HALF * (k + 1)]
+        for n in (pair, pair + 1):
+            block = outer[HALF * n : HALF * (n + 1)]
             columns.append(jnp.concatenate([block[:, :EXTENT], block[:, EXTENT:]], 0))
         high, low = split(jnp.concatenate(columns, 1))
         result = dot(fourth, jnp.concatenate([high, low, high], 0))
@@ -160,8 +158,8 @@
     column = lax.broadcasted_iota(jnp.int32, shape, 1)
     scores, relatives, tops = [], [], []
     for n in range(count):
-        rel_y = row - peak_ref[0, n]
-        rel_x = ((column - peak_ref[1, n] + EXTENT // 2) & (EXTENT - 1)) - EXTENT // 2
+        rel_y = row - peak_ref[0:1, n : n + 1]
+        rel_x = ((column - peak_ref[1:2, n : n + 1] + EXTENT // 2) & (EXTENT - 1)) - EXTENT // 2
         quarter = EXTENT // 4
         inside = (rel_y >= -quarter) & (rel_y < quarter) & (rel_x >= -quarter) & (rel_x < quarter)
         score = jnp.where(inside, correlations[n] * scale[n : n + 1], -1e30)
@@ -185,8 +183,8 @@
     peak_y = jnp.zeros((count, EXTENT), jnp.int32)
     peak_x = jnp.zeros((count, EXTENT), jnp.int32)
     for n in range(count):
-        peak_y = jnp.where(node == n, peak_ref[0, n], peak_y)
-        peak_x = jnp.where(node == n, peak_ref[1, n], peak_x)
+        peak_y = jnp.where(node == n, peak_ref[0:1, n : n + 1], peak_y)
+        peak_x = jnp.where(node == n, peak_ref[1:2, n : n + 1], peak_x)
     flow_y = peak_y.astype(F32) + total_y / total
     flow_x = peak_x.astype(F32) + total_x / total
     flow = jnp.where(lane == node, flow_y, jnp.where(lane == node + count, flow_x, 0.0))
@@ -219,19 +217,18 @@
             )
 
 
-def render_kernel(place_ref, map_ref, band_ref, flow_ref, name_ref, tile_ref, position_ref, send_ref, *scratch):
-    sections = flow_ref.shape[0]
+def render_kernel(band_ref, map_ref, flow_ref, name_ref, tile_ref, position_ref, send_ref, *scratch):
     tile_count, edge, _ = tile_ref.shape
     slots = send_ref.shape[0]
-    section = place_ref[1]
-    second_core = place_ref[2] == 1
+    section = lax.axis_index("gz")
+    second_core = section % 2 == 1
 
     def slot_of(p):
         return jnp.where(second_core, p % WIDE * (slots // WIDE) + p // WIDE, p)
 
-    position = jnp.zeros(flow_ref.shape[1:], F32)
-    for s in range(sections):
-        position = position + map_ref[section, s] * flow_ref[s]
+    lanes = lax.broadcasted_iota(jnp.int32, map_ref.shape, 1)
+    weights = jnp.sum(jnp.where(lanes == section, map_ref[...], 0.0), axis=1, keepdims=True)
+    position = jnp.sum(weights * flow_ref[:, 0, :], axis=0, keepdims=True)
     nodes = position_ref.shape[1]
     for c in range(2):
         position_ref[c : c + 1, :] = position[:, c * nodes : (c + 1) * nodes]
@@ -240,33 +237,51 @@
     height = edge // slots
     columns = edge // EXTENT
     chunk = EXTENT
+    chunks = edge // chunk
+
+    def fill(t, c, target_ref, sub_sign):
+        offset = band_ref[t : t + 1, c : c + 1]
+        here = lanes // per_tile == c * tile_count + t
+        total = jnp.sum(jnp.where(here, position, 0.0), axis=1, keepdims=True)
+        shift = total * (MIP_SCALE / per_tile)
+        fill_band(target_ref, shift - offset.astype(F32), offset, sub_sign)
+
+    def first(t, c):
+        col_ref, _, pass_ref = scratch[3 * t : 3 * t + 3]
+        rows = slice(c * chunk, (c + 1) * chunk)
+        pass_ref[rows, :] = dot(tile_ref[t, rows, :], col_ref[...]).astype(BF)
+
+    def second(t, c):
+        _, row_ref, pass_ref = scratch[3 * t : 3 * t + 3]
+        near = range(max(c - 1, 0), min(c + 2, chunks))
+        from_row = near[0] * chunk // (edge // 2) * (edge // 2)
+        to_row = edge // 2 if near[-1] * chunk < edge // 2 else edge
+        rows = slice(c * chunk, (c + 1) * chunk)
+        done = dot(row_ref[rows, from_row:to_row], pass_ref[from_row:to_row, :]).astype(BF)
+        each = chunk // height
+        done = done.reshape(each, height, edge)
+        for p in range(each):
+            for j in range(columns):
+                at = (t * columns + j) * height
+                send_ref[slot_of(c * each + p), at : at + height, :] = done[
+                    p, :, j * EXTENT : (j + 1) * EXTENT
+                ]
+
+    tail = tile_count * columns * height
+    fill(0, 1, scratch[0], 1)
     for t in range(tile_count):
-        col_ref, row_ref, pass_ref = scratch[3 * t : 3 * t + 3]
-        offset_y, offset_x = band_ref[t, 0], band_ref[t, 1]
-        shift_y, shift_x = (
-            jnp.sum(jnp.where(lanes // per_tile == c * tile_count + t, position, 0.0), axis=1, keepdims=True)
-            * (MIP_SCALE / per_tile)
-            for c in range(2)
-        )
-        fill_band(col_ref, shift_x - offset_x.astype(F32), offset_x, 1)
-        fill_band(row_ref, shift_y - offset_y.astype(F32), offset_y, -1)
-        for c in range(edge // chunk):
-            rows = slice(c * chunk, (c + 1) * chunk)
-            pass_ref[rows, :] = dot(tile_ref[t, rows, :], col_ref[...]).astype(BF)
-        for c in range(edge // chunk):
-            rows = slice(c * chunk, (c + 1) * chunk)
-            first, last = c * chunk // height, (c + 1) * chunk // height
-            done = dot(row_ref[rows, :], pass_ref[...]).astype(BF)
-            done = done.reshape(last - first, height, edge)
-            for p in range(first, last):
-                for j in range(columns):
-                    at = (t * columns + j) * height
-                    send_ref[slot_of(p), at : at + height, :] = done[
-                        p - first, :, j * EXTENT : (j + 1) * EXTENT
-                    ]
-    tail = tile_count * columns * height
-    for p in range(slots):
-        send_ref[slot_of(p), tail:, :] = name_ref[p]
+        for c in range(chunks):
+            first(t, c)
+            if c == 0:
+                fill(t, 0, scratch[3 * t + 1], -1)
+            if c == 1 and t + 1 < tile_count:
+                fill(t + 1, 1, scratch[3 * t + 3], 1)
+            if t > 0:
+                second(t - 1, c)
+    for c in range(chunks):
+        second(tile_count - 1, c)
+        for p in range(c * slots // chunks, (c + 1) * slots // chunks):
+            send_ref[slot_of(p), tail:, :] = name_ref[p]
 
 
 def gather_kernel(piece_ref, out_ref, data_ref):
@@ -274,32 +289,58 @@
     _, out_rows, edge = out_ref.shape
     height = edge // owners
     columns = edge // EXTENT
-    tile_count = (rows - 8) // (columns * height)
     tail = rows - 8
-    share = EXTENT // (tile_count * height)
-    lane_row = lax.broadcasted_iota(jnp.int32, (EXTENT, EXTENT), 1) % height
+    tile_count = tail // (columns * height)
+    part = EXTENT // SHARE // tile_count
+    parts = height // part
+    depth = owners * tile_count * part
+    for d in range(owners):
+        for j in range(columns):
+            pieces = []
+            for t in range(tile_count):
+                at = (t * columns + j) * height
+                pieces.append(piece_ref[d, at : at + height, :].astype(F32))
+            for k in range(parts):
+                at = k * depth + d * tile_count * part
+                data_ref[at : at + tile_count * part, j * EXTENT : (j + 1) * EXTENT] = (
+                    jnp.concatenate([p[k * part : (k + 1) * part] for p in pieces], 0).astype(BF)
+                )
+    lane = lax.broadcasted_iota(jnp.int32, (EXTENT, EXTENT), 1)
     sub = lax.broadcasted_iota(jnp.int32, (EXTENT, EXTENT), 0)
-    same = lane_row == sub % height
-    for d in range(owners):
-        for t in range(tile_count):
-            at = (d * tile_count + t) * height
-            for j in range(columns):
-                source = (t * columns + j) * height
-                data_ref[at : at + height, j * EXTENT : (j + 1) * EXTENT] = piece_ref[
-                    d, source : source + height, :
-                ]
+    same = lane % part == sub % part
     names = [
-        sum(piece_ref[d, tail : tail + 8, :].astype(F32) for d in range(start, start + share))[0:1]
-        for start in range(0, owners, share)
+        sum(piece_ref[d, tail : tail + 8, :].astype(F32) for d in range(start, start + SHARE))[0:1]
+        for start in range(0, owners, SHARE)
     ]
-    for c in range(owners * out_rows // EXTENT):
-        group = (sub // height + c * (EXTENT // height)).astype(F32)
+    each = EXTENT // part
+    for c in range(owners * out_rows // height // each):
+        group = (sub // part + c * each).astype(F32)
         hits = [jnp.where(same & (name == group), 1.0, 0.0) for name in names]
         count = jnp.sum(sum(hits), axis=1, keepdims=True)
-        total = dot(jnp.concatenate([hit.astype(BF) for hit in hits], 1), data_ref[...])
-        total = total * (1.0 / jnp.maximum(count, 1.0))
-        first, last = c * EXTENT // out_rows, (c + 1) * EXTENT // out_rows
-        out_ref[first:last] = total.astype(BF).reshape(last - first, out_rows, edge)
+        scale = 1.0 / jnp.maximum(count, 1.0)
+        pick = jnp.concatenate([hit.astype(BF) for hit in hits], 1)
+        totals = [
+            (dot(pick, data_ref[k * depth : (k + 1) * depth]) * scale).reshape(each, part, edge)
+            for k in range(parts)
+        ]
+        total = jnp.concatenate(totals, 1).astype(BF)
+        first, last = c * each * height // out_rows, (c + 1) * each * height // out_rows
+        out_ref[first:last] = total.reshape(last - first, out_rows, edge)
+
+
+def place_kernel(position_ref, cell_ref, moved_ref, out_ref, arrived):
+    height = out_ref.shape[2]
+    copies = [
+        pltpu.make_async_copy(
+            cell_ref.at[:, g * height : (g + 1) * height, :], out_ref.at[g], arrived.at[g]
+        )
+        for g in range(out_ref.shape[0])
+    ]
+    copies.append(pltpu.make_async_copy(position_ref, moved_ref, arrived.at[len(copies)]))
+    for copy in copies:
+        copy.start()
+    for copy in copies:
+        copy.wait()
 
 
 def in_vmem():
@@ -343,7 +384,7 @@
     below = lax.ppermute(patches, "gz", [(i, i + 1) for i in range(sections - 1)])
     early_table, late_table = (jnp.asarray(t) for t in dft_constants())
     second_core = section % 2 == 1
-    place = jnp.stack([lax.axis_index("xy"), section, second_core.astype(jnp.int32)])
+    place = jnp.stack([lax.axis_index("xy"), second_core.astype(jnp.int32)])[None]
     spectrum, power = pl.pallas_call(
         own_kernel,
         out_shape=(
@@ -362,7 +403,7 @@
             jax.ShapeDtypeStruct((sections, 1, EXTENT), F32),
             jax.ShapeDtypeStruct((PIECES, 8, EXTENT), BF),
         ),
-        in_specs=[in_smem()] * 2 + [in_vmem()] * 6,
+        in_specs=[in_vmem()] * 8,
         out_specs=(in_vmem(),) * 2,
         compiler_params=params(),
         name="flow",
@@ -375,12 +416,12 @@
             jax.ShapeDtypeStruct((2, count), F32),
             jax.ShapeDtypeStruct((PIECES, tile_count * height * edge // EXTENT + 8, EXTENT), BF),
         ),
-        in_specs=[in_smem()] * 3 + [in_vmem()] * 3,
+        in_specs=[in_vmem()] * 5,
         out_specs=(in_vmem(), in_vmem()),
         scratch_shapes=[pltpu.VMEM((edge, edge), BF)] * (3 * tile_count),
         compiler_params=params(),
         name="render",
-    )(place, jnp.asarray(relaxation_map(sections)), band_offsets[0], flow, names, tiles[0])
+    )(band_offsets[0], jnp.asarray(relaxation_map(sections).T), flow, names, tiles[0])
     pieces = lax.cond(
         second_core,
         exchange_x_then_z,
@@ -398,7 +439,18 @@
         name="gather",
     )(pieces)
     cells = exchange(cells, "xy")
-    rendered = cells.reshape(PIECES, share, height, edge).transpose(1, 0, 2, 3)
+    position, rendered = pl.pallas_call(
+        place_kernel,
+        out_shape=(
+            jax.ShapeDtypeStruct(position.shape, F32),
+            jax.ShapeDtypeStruct((share, PIECES, height, edge), BF),
+        ),
+        in_specs=[in_vmem()] * 2,
+        out_specs=(pl.BlockSpec(memory_space=pl.ANY),) * 2,
+        scratch_shapes=[pltpu.SemaphoreType.DMA((share + 1,))],
+        compiler_params=params(),
+        name="place",
+    )(position, cells)
     rendered = rendered.reshape(1, share, edge, edge)
     return position[None], rendered
 

time: 102 us -> 99.2 us (0.973)
  Pallas kernels: 7.79 us -> 6.15 us
  local copies, waits for them, and re-layouts: 3.06 us -> 2.01 us
    pallas_call x1, Pallas kernels: 2.91 us -> 1.56 us  [body(): pl.pallas_call(render_kernel, out_shape=(jax.ShapeDtypeStruct((2, count),...]
    transpose x1 -> x0, local copies, waits for them, and re-layouts: 1.05 us -> none  [body(): rendered = cells.reshape(PIECES, share, height, edge).transpose(1, 0, 2, 3)]
where the time goes in v11:
time: 99.2 us; the launch traced here: 98.9 us
  blocking collectives  83.3 us (84%)
  Pallas kernels  6.15 us (6%)
  starting transfers between devices  4.59 us (5%)
  local copies, waits for them, and re-layouts  2.01 us (2%)
  waiting for transfers between devices  2 us (2%)
    all_to_all x4, blocking collectives, exchange(): lax.all_to_all(value, axis, split_axis=0, concat_axis=0, tiled=True, axis...  83.3 us
    ppermute x1, starting transfers between devices, body(): lax.ppermute(patches, 'gz', [(i, i + 1) for i in range(sections - 1)])  4.59 us
    ppermute x1, waiting for transfers between devices, body(): lax.ppermute(patches, 'gz', [(i, i + 1) for i in range(sections - 1)])  2 us
  transfers between devices with their start and end apart: 1, of which 1 were waited for; matrix products, arithmetic and copies ran while one was open for 0% of the time, Pallas kernels for 1%

profile of v11, /device:TPU:1, one launch (start us, length us, event | category | flops | bytes accessed | tf_op | source)
XLA Modules:
  0.0 98.9 jit_solution(16092569905674083589)
XLA Ops:
  0.6 4.6 %collective-permute-start = (bf16[1,8,128,128]{3,2,1,0:T(8,128)(2,1)}, bf16[1,8,128,128]{3,2,1,0:T(8,128)(2,1)S(1)}, u32[]{:S(2)}, u32[]{:S(2)}) collective-permute-start(bf16[1,8,128,128]{3,2,1,0:T(8,128)(2,1)} %param.10), channel_id=1, source_target_pairs={{0,32},{32,64},{64,96},{96,128},{128,160},{160,192},{192,224},{224... | collective-permute-start | bytes 786440 | tf_op jit(solution)/shard_map/ppermute | solution.py:384
  5.2 0.0 copy-start.2
  5.3 0.9 copy-done.2
  6.2 0.0 copy-start.7
  6.2 0.9 copy-done.7
  7.2 0.0 copy-start.1
  7.2 0.0 copy-start.4
  7.2 0.0 copy-start.6
  7.2 0.7 own.1
  7.9 0.0 copy-start
  7.9 0.0 copy-start.3
  7.9 0.0 copy-start.5
  7.9 0.1 add_bitcast_fusion.place_ref
  8.0 2.0 %collective-permute-done = bf16[1,8,128,128]{3,2,1,0:T(8,128)(2,1)S(1)} collective-permute-done((bf16[1,8,128,128]{3,2,1,0:T(8,128)(2,1)}, bf16[1,8,128,128]{3,2,1,0:T(8,128)(2,1)S(1)}, u32[]{:S(2)}, u32[]{:S(2)}) %collective-permute-start) | collective-permute-done | bytes 262176 | tf_op jit(solution)/shard_map/ppermute | solution.py:384
  10.0 0.0 copy-done.1
  10.0 0.0 copy-done.4
  10.0 0.0 copy-done.6
  10.0 1.9 %flow.1 = (f32[16,1,128]{2,1,0:T(1,128)S(1)}, bf16[32,8,128]{2,1,0:T(8,128)(2,1)S(1)}) custom-call(s32[1,2]{1,0:T(1,128)S(1)} %add_bitcast_fusion.place_ref, s32[2,8]{1,0:T(2,128)S(1)} %bitcast.22, s32[1,64]{1,0:T(1,128)S(1)} %bitcast.24, bf16[8,128,128]{2,1,0:T(8,128)(2,1)S(1)} %bitcast.21, f32[8,72,256]{2,1,0:T(8,128)S(1)} %get-tuple-element.15.spectrum_ref, ...), custom_call_target="tpu_custom_call" | custom-call | tf_op jit(solution)/shard_map/flow/pallas_call | solution.py:400
  11.9 15.2 %all_to_all.25.flow_ref = f32[16,1,128]{2,1,0:T(1,128)S(1)} all-to-all(f32[16,1,128]{2,1,0:T(1,128)S(1)} %get-tuple-element.17), channel_id=1, replica_groups=mesh['gz'=16,'xy'=32] {'gz'}, dimensions={0} | all-to-all | bytes 16384 | tf_op jit(solution)/shard_map/all_to_all | solution.py:359
  27.1 0.0 copy-done
  27.1 0.0 copy-done.3
  27.1 0.0 copy-done.5
  27.1 1.6 %render.1 = (f32[2,8]{1,0:T(2,128)S(1)}, bf16[32,136,128]{2,1,0:T(8,128)(2,1)S(1)}) custom-call(s32[2,2]{1,0:T(2,128)S(1)} %bitcast.23, f32[16,16]{1,0:T(8,128)S(1)} %copy-done.3, f32[16,1,128]{2,1,0:T(1,128)S(1)} %all_to_all.25.flow_ref, bf16[32,8,128]{2,1,0:T(8,128)(2,1)S(1)} %get-tuple-element.18.name_ref, bf16[2,512,512]{2,1,0:T(8,128)(2,1)S(1)} %bitcast.20), custom_call_target="tpu_custom_call" | custom-call | tf_op jit(solution)/shard_map/render/pallas_call | solution.py:413
  28.6 45.4 %conditional.1 = (bf16[32,136,128]{2,1,0:T(8,128)(2,1)S(1)}) conditional(s32[]{:T(128)} %convert_element_type.4, bf16[32,136,128]{2,1,0:T(8,128)(2,1)S(1)} %get-tuple-element.20, bf16[32,136,128]{2,1,0:T(8,128)(2,1)S(1)} %get-tuple-element.20), branch_computations={%region_0.1_spmd, %region_1.2_spmd} | conditional | bytes 6684680 | solution.py:425
  28.7 13.9 %all_to_all.23 = bf16[4,1088,128]{2,1,0:T(8,128)(2,1)S(1)} all-to-all(bf16[4,1088,128]{2,1,0:T(8,128)(2,1)S(1)} %bitcast.26), channel_id=1, replica_groups={{0,1,2,3},{4,5,6,7},{8,9,10,11},{12,13,14,15},{16,17,18,19},{20,21,22,2..., dimensions={0} | all-to-all | bytes 2228224 | tf_op jit(solution)/shard_map/cond/branch_1_fun/all_to_all | solution.py:359
  42.6 0.1 copy.10
  42.6 31.4 %all_to_all.24 = bf16[8,544,128]{2,1,0:T(8,128)(2,1)S(1)} all-to-all(bf16[8,544,128]{2,1,0:T(8,128)(2,1)S(1)} %bitcast.27), channel_id=1, replica_groups={{0,4,8,12,16,20,24,28},{1,5,9,13,17,21,25,29},{2,6,10,14,18,22,26,30},{..., dimensions={0} | all-to-all | bytes 2228224 | tf_op jit(solution)/shard_map/cond/branch_1_fun/all_to_all | solution.py:359
  74.0 1.0 %gather.1 = bf16[32,32,512]{2,1,0:T(8,128)(2,1)S(1)} custom-call(bf16[32,136,128]{2,1,0:T(8,128)(2,1)S(1)} %get-tuple-element.23.piece_ref), custom_call_target="tpu_custom_call" | custom-call | tf_op jit(solution)/shard_map/gather/pallas_call | solution.py:432
  75.0 22.9 %all_to_all.26.cell_ref = bf16[32,32,512]{2,1,0:T(8,128)(2,1)S(1)} all-to-all(bf16[32,32,512]{2,1,0:T(8,128)(2,1)S(1)} %gather.1), channel_id=1, replica_groups=mesh['gz'=16,'xy'=32] {'xy'}, dimensions={0} | all-to-all | bytes 2097152 | tf_op jit(solution)/shard_map/all_to_all | solution.py:359
  97.9 1.0 %place.1 = (f32[2,8]{1,0:T(2,128)}, bf16[2,32,16,512]{3,2,1,0:T(8,128)(2,1)}) custom-call(f32[2,8]{1,0:T(2,128)S(1)} %get-tuple-element.19.position_ref, bf16[32,32,512]{2,1,0:T(8,128)(2,1)S(1)} %all_to_all.26.cell_ref), custom_call_target="tpu_custom_call" | custom-call | tf_op jit(solution)/shard_map/place/pallas_call | solution.py:442
Async XLA Ops:
  0.6 9.4 %collective-permute-start = (bf16[1,8,128,128]{3,2,1,0:T(8,128)(2,1)}, bf16[1,8,128,128]{3,2,1,0:T(8,128)(2,1)S(1)}, u32[]{:S(2)}, u32[]{:S(2)}) collective-permute-start(bf16[1,8,128,128]{3,2,1,0:T(8,128)(2,1)} %param.10), channel_id=1, source_target_pairs={{0,32},{32,64},{64,96},{96,128},{128,160},{160,192},{192,224},{224... | collective-permute-start | bytes 786440 | tf_op jit(solution)/shard_map/ppermute | solution.py:384
  5.2 1.0 copy-start.2
  6.2 0.9 copy-start.7
  7.2 2.9 %copy-start.1 = (bf16[928,256]{1,0:T(8,128)(2,1)S(1)}, bf16[928,256]{1,0:T(8,128)(2,1)}, u32[]{:S(2)}) copy-start(bf16[928,256]{1,0:T(8,128)(2,1)} %constant.30.clone.inverse_ref) | copy-start | bytes 1425412
  7.2 2.9 %copy-start.4 = (s32[1,8,2]{1,2,0:T(2,128)S(1)}, s32[1,8,2]{1,2,0:T(2,128)}, u32[]{:S(2)}) copy-start(s32[1,8,2]{1,2,0:T(2,128)} %param.11) | copy-start | bytes 196
  7.2 2.9 %copy-start.6 = (s32[1,64,1]{1,2,0:T(1,128)S(1)}, s32[1,64,1]{1,2,0:T(1,128)}, u32[]{:S(2)}) copy-start(s32[1,64,1]{1,2,0:T(1,128)} %param.14) | copy-start | bytes 772
  7.9 19.1 %copy-start = (bf16[1,2,512,512]{3,2,1,0:T(8,128)(2,1)S(1)}, bf16[1,2,512,512]{3,2,1,0:T(8,128)(2,1)}, u32[]{:S(2)}) copy-start(bf16[1,2,512,512]{3,2,1,0:T(8,128)(2,1)} %param.12) | copy-start | bytes 3145732
  7.9 19.1 %copy-start.3 = (f32[16,16]{1,0:T(8,128)S(1)}, f32[16,16]{1,0:T(8,128)}, u32[]{:S(2)}) copy-start(f32[16,16]{1,0:T(8,128)} %constant.31.clone.map_ref) | copy-start | bytes 3076
  7.9 19.1 %copy-start.5 = (s32[1,2,2]{2,1,0:T(2,128)S(1)}, s32[1,2,2]{2,1,0:T(2,128)}, u32[]{:S(2)}) copy-start(s32[1,2,2]{2,1,0:T(2,128)} %param.13) | copy-start | bytes 52

commit v12 on v11

--- a/solution.py
+++ b/solution.py
@@ -7,7 +7,6 @@
 from jax.sharding import PartitionSpec as P
 
 PIECES = 32
-WIDE = 4
 SHARE = 8
 BAND = 6
 RELAX = 3
@@ -100,14 +99,18 @@
 
 
 def own_kernel(now_ref, table_ref, spectrum_ref, energy_ref):
+    shape = (HALF, EXTENT)
+    row = lax.broadcasted_iota(jnp.int32, shape, 0)
+    mean = (row == 0) & (lax.broadcasted_iota(jnp.int32, shape, 1) == 0)
     for pair in range(0, now_ref.shape[0], 2):
         for k, (real, imag) in enumerate(spectra([now_ref[pair], now_ref[pair + 1]], table_ref)):
+            real, imag = jnp.where(mean, 0.0, real), jnp.where(mean, 0.0, imag)
             spectrum_ref[pair + k, :, :EXTENT] = real
             spectrum_ref[pair + k, :, EXTENT:] = imag
     energy_ref[...] = jnp.broadcast_to(energy(now_ref), energy_ref.shape)
 
 
-def write_names(owner, route_ref, name_ref):
+def write_names(owner, second_core, route_ref, name_ref):
     slots = name_ref.shape[0]
     tile_count = route_ref.shape[1] // slots
     height = EXTENT // SHARE // tile_count
@@ -115,7 +118,10 @@
     slot = lax.broadcasted_iota(jnp.int32, (slots, tile_count * slots), 0)
     names = jnp.broadcast_to(route_ref[...], lane.shape).astype(F32)
     place = lax.broadcasted_iota(jnp.int32, (slots, EXTENT), 1)
-    here = place // (tile_count * height) == (owner & (SHARE - 1))
+    own_place = owner & (SHARE - 1)
+    slot_column = lax.broadcasted_iota(jnp.int32, (slots, 1), 0)
+    pair_place = (own_place & (SHARE - 2)) | ((owner ^ slot_column) & 1)
+    here = place // (tile_count * height) == jnp.where(second_core == 1, pair_place, own_place)
     row = jnp.zeros((slots, EXTENT), F32)
     for t in range(tile_count):
         own = jnp.sum(jnp.where(lane == slot + t * slots, names, 0.0), axis=1, keepdims=True)
@@ -126,7 +132,7 @@
 
 def flow_kernel(place_ref, peak_ref, route_ref, low_ref, spectrum_ref, energy_ref, table_ref, inverse_ref, out_ref, name_ref):
     count = low_ref.shape[0]
-    write_names(place_ref[:, :1], route_ref, name_ref)
+    write_names(place_ref[:, :1], place_ref[:, 1:], route_ref, name_ref)
     crosses = []
     for n, (lr, li) in enumerate(spectra([low_ref[n] for n in range(count)], table_ref)):
         nr = spectrum_ref[n, :, :EXTENT]
@@ -220,11 +226,11 @@
 def render_kernel(band_ref, map_ref, flow_ref, name_ref, tile_ref, position_ref, send_ref, *scratch):
     tile_count, edge, _ = tile_ref.shape
     slots = send_ref.shape[0]
-    section = lax.axis_index("gz")
+    section, owner = lax.axis_index("gz"), lax.axis_index("xy")
     second_core = section % 2 == 1
 
     def slot_of(p):
-        return jnp.where(second_core, p % WIDE * (slots // WIDE) + p // WIDE, p)
+        return jnp.where(second_core, ((owner + p) % 2) * (slots // 2) + p // 2, p)
 
     lanes = lax.broadcasted_iota(jnp.int32, map_ref.shape, 1)
     weights = jnp.sum(jnp.where(lanes == section, map_ref[...], 0.0), axis=1, keepdims=True)
@@ -361,15 +367,14 @@
     )
 
 
-def exchange_x_then_z(value):
+def exchange_pair_first(value):
     owners, rows, lanes = value.shape
-    high = owners // WIDE
-    along_x = [[z * WIDE + x for x in range(WIDE)] for z in range(high)]
-    along_z = [[z * WIDE + x for z in range(high)] for x in range(WIDE)]
-    value = exchange(value.reshape(WIDE, high * rows, lanes), "xy", along_x)
-    value = value.reshape(WIDE, high, rows, lanes).transpose(1, 0, 2, 3)
-    value = exchange(value.reshape(high, WIDE * rows, lanes), "xy", along_z)
-    return value.reshape(owners, rows, lanes)
+    half = owners // 2
+    kept, given = value[:half], value[half:]
+    taken = lax.ppermute(given, "xy", [(i, i ^ 1) for i in range(owners)])
+    value = jnp.concatenate([kept, taken], 1)
+    parity = [[2 * i + q for i in range(half)] for q in range(2)]
+    return exchange(value, "xy", parity).reshape(owners, rows, lanes)
 
 
 def body(patches, peak_offsets, tiles, band_offsets, routes):
@@ -424,7 +429,7 @@
     )(band_offsets[0], jnp.asarray(relaxation_map(sections).T), flow, names, tiles[0])
     pieces = lax.cond(
         second_core,
-        exchange_x_then_z,
+        exchange_pair_first,
         lambda value: exchange(value, "xy"),
         pieces,
     )

time: 99.2 us -> 101 us (1.018)
  blocking collectives: 83.3 us -> 75.1 us
  waiting for transfers between devices: 2 us -> 9.15 us
  starting transfers between devices: 4.59 us -> 7.71 us
    all_to_all x4 -> x3, blocking collectives: 83.3 us -> 75.1 us  [exchange(): lax.all_to_all(value, axis, split_axis=0, concat_axis=0, tiled=True, axis...]
    ppermute x0 -> x1, waiting for transfers between devices: none -> 7.15 us  [exchange_pair_first(): taken = lax.ppermute(given, 'xy', [(i, i ^ 1) for i in range(owners)])]
    ppermute x0 -> x1, starting transfers between devices: none -> 3.12 us  [exchange_pair_first(): taken = lax.ppermute(given, 'xy', [(i, i ^ 1) for i in range(owners)])]
  transfers between devices with their start and end apart: 1 -> 2, of which waited for: 1 -> 2; matrix products, arithmetic and copies ran while one was open for 0% -> 0% of each run, Pallas kernels for 1% -> 1%
where the time goes in v12:
time: 101 us
  blocking collectives  75.1 us (74%)
  waiting for transfers between devices  9.15 us (9%)
  starting transfers between devices  7.71 us (8%)
  Pallas kernels  6.15 us (6%)
  local copies, waits for them, and re-layouts  2.01 us (2%)
    all_to_all x3, blocking collectives, exchange(): lax.all_to_all(value, axis, split_axis=0, concat_axis=0, tiled=True, axis...  75.1 us
    ppermute x1, waiting for transfers between devices, exchange_pair_first(): taken = lax.ppermute(given, 'xy', [(i, i ^ 1) for i in range(owners)])  7.15 us
    ppermute x1, starting transfers between devices, body(): lax.ppermute(patches, 'gz', [(i, i + 1) for i in range(sections - 1)])  4.59 us
    ppermute x1, starting transfers between devices, exchange_pair_first(): taken = lax.ppermute(given, 'xy', [(i, i ^ 1) for i in range(owners)])  3.12 us
  transfers between devices with their start and end apart: 2, of which 2 were waited for; matrix products, arithmetic and copies ran while one was open for 0% of the time, Pallas kernels for 1%

profile of v12, /device:TPU:1, one launch (start us, length us, event | category | flops | bytes accessed | tf_op | source)
XLA Modules:
  0.0 101.1 jit_solution(1010712964972547113)
XLA Ops:
  0.6 4.6 %collective-permute-start.1 = (bf16[1,8,128,128]{3,2,1,0:T(8,128)(2,1)}, bf16[1,8,128,128]{3,2,1,0:T(8,128)(2,1)S(1)}, u32[]{:S(2)}, u32[]{:S(2)}) collective-permute-start(bf16[1,8,128,128]{3,2,1,0:T(8,128)(2,1)} %param.10), channel_id=1, source_target_pairs={{0,32},{32,64},{64,96},{96,128},{128,160},{160,192},{192,224},{224... | collective-permute-start | bytes 786440 | tf_op jit(solution)/shard_map/ppermute | solution.py:389
  5.2 0.0 copy-start.2
  5.3 0.9 copy-done.2
  6.2 0.0 copy-start.7
  6.2 0.9 copy-done.7
  7.2 0.0 copy-start.1
  7.2 0.0 copy-start.4
  7.2 0.0 copy-start.6
  7.2 0.7 own.1
  7.9 0.0 copy-start
  7.9 0.0 copy-start.3
  7.9 0.0 copy-start.5
  7.9 0.1 add_bitcast_fusion.place_ref
  8.0 2.0 %collective-permute-done.1 = bf16[1,8,128,128]{3,2,1,0:T(8,128)(2,1)S(1)} collective-permute-done((bf16[1,8,128,128]{3,2,1,0:T(8,128)(2,1)}, bf16[1,8,128,128]{3,2,1,0:T(8,128)(2,1)S(1)}, u32[]{:S(2)}, u32[]{:S(2)}) %collective-permute-start.1) | collective-permute-done | bytes 262176 | tf_op jit(solution)/shard_map/ppermute | solution.py:389
  10.0 0.0 copy-done.1
  10.0 0.0 copy-done.4
  10.0 0.0 copy-done.6
  10.0 1.9 %flow.1 = (f32[16,1,128]{2,1,0:T(1,128)S(1)}, bf16[32,8,128]{2,1,0:T(8,128)(2,1)S(1)}) custom-call(s32[1,2]{1,0:T(1,128)S(1)} %add_bitcast_fusion.place_ref, s32[2,8]{1,0:T(2,128)S(1)} %bitcast.17, s32[1,64]{1,0:T(1,128)S(1)} %bitcast.19, bf16[8,128,128]{2,1,0:T(8,128)(2,1)S(1)} %bitcast.16, f32[8,72,256]{2,1,0:T(8,128)S(1)} %get-tuple-element.15.spectrum_ref, ...), custom_call_target="tpu_custom_call" | custom-call | tf_op jit(solution)/shard_map/flow/pallas_call | solution.py:405
  11.9 15.2 %all_to_all.20.flow_ref = f32[16,1,128]{2,1,0:T(1,128)S(1)} all-to-all(f32[16,1,128]{2,1,0:T(1,128)S(1)} %get-tuple-element.17), channel_id=1, replica_groups=mesh['gz'=16,'xy'=32] {'gz'}, dimensions={0} | all-to-all | bytes 16384 | tf_op jit(solution)/shard_map/all_to_all | solution.py:365
  27.0 0.0 copy-done
  27.0 0.0 copy-done.3
  27.0 0.0 copy-done.5
  27.1 1.6 %render.1 = (f32[2,8]{1,0:T(2,128)S(1)}, bf16[32,136,128]{2,1,0:T(8,128)(2,1)S(1)}) custom-call(s32[2,2]{1,0:T(2,128)S(1)} %bitcast.18, f32[16,16]{1,0:T(8,128)S(1)} %copy-done.3, f32[16,1,128]{2,1,0:T(1,128)S(1)} %all_to_all.20.flow_ref, bf16[32,8,128]{2,1,0:T(8,128)(2,1)S(1)} %get-tuple-element.18.name_ref, bf16[2,512,512]{2,1,0:T(8,128)(2,1)S(1)} %bitcast.15), custom_call_target="tpu_custom_call" | custom-call | tf_op jit(solution)/shard_map/render/pallas_call | solution.py:418
  28.6 46.4 %conditional.1 = (bf16[32,136,128]{2,1,0:T(8,128)(2,1)S(1)}) conditional(s32[]{:T(128)} %convert_element_type.4, bf16[32,136,128]{2,1,0:T(8,128)(2,1)S(1)} %get-tuple-element.20, bf16[32,136,128]{2,1,0:T(8,128)(2,1)S(1)} %get-tuple-element.20), branch_computations={%region_0.1_spmd, %region_1.2_spmd} | conditional | flops 2228224 | bytes 8912944 | solution.py:430
  28.6 0.1 fusion
  28.7 3.1 %collective-permute-start = (bf16[16,136,128]{2,1,0:T(8,128)(2,1)S(1)}, bf16[16,136,128]{2,1,0:T(8,128)(2,1)S(1)}, u32[]{:S(2)}, u32[]{:S(2)}) collective-permute-start(bf16[16,136,128]{2,1,0:T(8,128)(2,1)S(1)} %get-tuple-element.24), channel_id=1, source_target_pairs={{0,1},{1,0},{2,3},{3,2},{4,5},{5,4},{6,7},{7,6},{8,9},{9,8},{10,11... | collective-permute-start | bytes 1671176 | tf_op jit(solution)/shard_map/cond/branch_1_fun/ppermute | solution.py:374
  31.9 7.2 %collective-permute-done = bf16[16,136,128]{2,1,0:T(8,128)(2,1)S(1)} collective-permute-done((bf16[16,136,128]{2,1,0:T(8,128)(2,1)S(1)}, bf16[16,136,128]{2,1,0:T(8,128)(2,1)S(1)}, u32[]{:S(2)}, u32[]{:S(2)}) %collective-permute-start) | collective-permute-done | bytes 557088 | tf_op jit(solution)/shard_map/cond/branch_1_fun/ppermute | solution.py:374
  39.0 0.1 pad_maximum_fusion
  39.1 35.9 %all_to_all.19 = bf16[16,272,128]{2,1,0:T(8,128)(2,1)S(1)} all-to-all(bf16[16,272,128]{2,1,0:T(8,128)(2,1)S(1)} %pad_maximum_fusion), channel_id=1, replica_groups={{0,2,4,6,8,10,12,14,16,18,20,22,24,26,28,30},{1,3,5,7,9,11,13,15,17,19,..., dimensions={0} | all-to-all | bytes 2228224 | tf_op jit(solution)/shard_map/cond/branch_1_fun/all_to_all | solution.py:365
  75.0 1.0 gather.1
  76.0 24.0 %all_to_all.21.cell_ref = bf16[32,32,512]{2,1,0:T(8,128)(2,1)S(1)} all-to-all(bf16[32,32,512]{2,1,0:T(8,128)(2,1)S(1)} %gather.1), channel_id=1, replica_groups=mesh['gz'=16,'xy'=32] {'xy'}, dimensions={0} | all-to-all | bytes 2097152 | tf_op jit(solution)/shard_map/all_to_all | solution.py:365
  100.1 1.0 place.1
Async XLA Ops:
  0.6 9.4 %collective-permute-start.1 = (bf16[1,8,128,128]{3,2,1,0:T(8,128)(2,1)}, bf16[1,8,128,128]{3,2,1,0:T(8,128)(2,1)S(1)}, u32[]{:S(2)}, u32[]{:S(2)}) collective-permute-start(bf16[1,8,128,128]{3,2,1,0:T(8,128)(2,1)} %param.10), channel_id=1, source_target_pairs={{0,32},{32,64},{64,96},{96,128},{128,160},{160,192},{192,224},{224... | collective-permute-start | bytes 786440 | tf_op jit(solution)/shard_map/ppermute | solution.py:389
  5.2 1.0 copy-start.2
  6.2 0.9 copy-start.7
  7.2 2.9 %copy-start.1 = (bf16[928,256]{1,0:T(8,128)(2,1)S(1)}, bf16[928,256]{1,0:T(8,128)(2,1)}, u32[]{:S(2)}) copy-start(bf16[928,256]{1,0:T(8,128)(2,1)} %constant.30.clone.inverse_ref) | copy-start | bytes 1425412
  7.2 2.9 %copy-start.4 = (s32[1,8,2]{1,2,0:T(2,128)S(1)}, s32[1,8,2]{1,2,0:T(2,128)}, u32[]{:S(2)}) copy-start(s32[1,8,2]{1,2,0:T(2,128)} %param.11) | copy-start | bytes 196
  7.2 2.9 %copy-start.6 = (s32[1,64,1]{1,2,0:T(1,128)S(1)}, s32[1,64,1]{1,2,0:T(1,128)}, u32[]{:S(2)}) copy-start(s32[1,64,1]{1,2,0:T(1,128)} %param.14) | copy-start | bytes 772
  7.9 19.1 %copy-start = (bf16[1,2,512,512]{3,2,1,0:T(8,128)(2,1)S(1)}, bf16[1,2,512,512]{3,2,1,0:T(8,128)(2,1)}, u32[]{:S(2)}) copy-start(bf16[1,2,512,512]{3,2,1,0:T(8,128)(2,1)} %param.12) | copy-start | bytes 3145732
  7.9 19.1 %copy-start.3 = (f32[16,16]{1,0:T(8,128)S(1)}, f32[16,16]{1,0:T(8,128)}, u32[]{:S(2)}) copy-start(f32[16,16]{1,0:T(8,128)} %constant.31.clone.map_ref) | copy-start | bytes 3076
  7.9 19.1 %copy-start.5 = (s32[1,2,2]{2,1,0:T(2,128)S(1)}, s32[1,2,2]{2,1,0:T(2,128)}, u32[]{:S(2)}) copy-start(s32[1,2,2]{2,1,0:T(2,128)} %param.13) | copy-start | bytes 52
  28.7 10.3 %collective-permute-start = (bf16[16,136,128]{2,1,0:T(8,128)(2,1)S(1)}, bf16[16,136,128]{2,1,0:T(8,128)(2,1)S(1)}, u32[]{:S(2)}, u32[]{:S(2)}) collective-permute-start(bf16[16,136,128]{2,1,0:T(8,128)(2,1)S(1)} %get-tuple-element.24), channel_id=1, source_target_pairs={{0,1},{1,0},{2,3},{3,2},{4,5},{5,4},{6,7},{7,6},{8,9},{9,8},{10,11... | collective-permute-start | bytes 1671176 | tf_op jit(solution)/shard_map/cond/branch_1_fun/ppermute | solution.py:374

commit v13 on v11

--- a/solution.py
+++ b/solution.py
@@ -100,8 +100,12 @@
 
 
 def own_kernel(now_ref, table_ref, spectrum_ref, energy_ref):
+    shape = (HALF, EXTENT)
+    row = lax.broadcasted_iota(jnp.int32, shape, 0)
+    mean = (row == 0) & (lax.broadcasted_iota(jnp.int32, shape, 1) == 0)
     for pair in range(0, now_ref.shape[0], 2):
         for k, (real, imag) in enumerate(spectra([now_ref[pair], now_ref[pair + 1]], table_ref)):
+            real, imag = jnp.where(mean, 0.0, real), jnp.where(mean, 0.0, imag)
             spectrum_ref[pair + k, :, :EXTENT] = real
             spectrum_ref[pair + k, :, EXTENT:] = imag
     energy_ref[...] = jnp.broadcast_to(energy(now_ref), energy_ref.shape)

time: 99.2 us -> 99.2 us (level)
  no operation moved by 1% of the time
where the time goes in v13:
time: 99.2 us; the launch traced here: 98.9 us
  blocking collectives  83.3 us (84%)
  Pallas kernels  6.15 us (6%)
  starting transfers between devices  4.59 us (5%)
  local copies, waits for them, and re-layouts  2.01 us (2%)
  waiting for transfers between devices  2 us (2%)
    all_to_all x4, blocking collectives, exchange(): lax.all_to_all(value, axis, split_axis=0, concat_axis=0, tiled=True, axis...  83.3 us
    ppermute x1, starting transfers between devices, body(): lax.ppermute(patches, 'gz', [(i, i + 1) for i in range(sections - 1)])  4.59 us
    ppermute x1, waiting for transfers between devices, body(): lax.ppermute(patches, 'gz', [(i, i + 1) for i in range(sections - 1)])  2 us
  transfers between devices with their start and end apart: 1, of which 1 were waited for; matrix products, arithmetic and copies ran while one was open for 0% of the time, Pallas kernels for 1%

profile of v13, /device:TPU:1, one launch (start us, length us, event | category | flops | bytes accessed | tf_op | source)
XLA Modules:
  0.0 98.9 jit_solution(13092706484109282278)
XLA Ops:
  0.6 4.6 %collective-permute-start = (bf16[1,8,128,128]{3,2,1,0:T(8,128)(2,1)}, bf16[1,8,128,128]{3,2,1,0:T(8,128)(2,1)S(1)}, u32[]{:S(2)}, u32[]{:S(2)}) collective-permute-start(bf16[1,8,128,128]{3,2,1,0:T(8,128)(2,1)} %param.10), channel_id=1, source_target_pairs={{0,32},{32,64},{64,96},{96,128},{128,160},{160,192},{192,224},{224... | collective-permute-start | bytes 786440 | tf_op jit(solution)/shard_map/ppermute | solution.py:388
  5.2 0.0 copy-start.2
  5.3 0.9 copy-done.2
  6.2 0.0 copy-start.7
  6.2 0.9 copy-done.7
  7.2 0.0 copy-start.1
  7.2 0.0 copy-start.4
  7.2 0.0 copy-start.6
  7.2 0.7 own.1
  7.9 0.0 copy-start
  7.9 0.0 copy-start.3
  7.9 0.0 copy-start.5
  7.9 0.1 add_bitcast_fusion.place_ref
  8.0 2.0 %collective-permute-done = bf16[1,8,128,128]{3,2,1,0:T(8,128)(2,1)S(1)} collective-permute-done((bf16[1,8,128,128]{3,2,1,0:T(8,128)(2,1)}, bf16[1,8,128,128]{3,2,1,0:T(8,128)(2,1)S(1)}, u32[]{:S(2)}, u32[]{:S(2)}) %collective-permute-start) | collective-permute-done | bytes 262176 | tf_op jit(solution)/shard_map/ppermute | solution.py:388
  10.0 0.0 copy-done.1
  10.0 0.0 copy-done.4
  10.0 0.0 copy-done.6
  10.0 1.9 %flow.1 = (f32[16,1,128]{2,1,0:T(1,128)S(1)}, bf16[32,8,128]{2,1,0:T(8,128)(2,1)S(1)}) custom-call(s32[1,2]{1,0:T(1,128)S(1)} %add_bitcast_fusion.place_ref, s32[2,8]{1,0:T(2,128)S(1)} %bitcast.22, s32[1,64]{1,0:T(1,128)S(1)} %bitcast.24, bf16[8,128,128]{2,1,0:T(8,128)(2,1)S(1)} %bitcast.21, f32[8,72,256]{2,1,0:T(8,128)S(1)} %get-tuple-element.15.spectrum_ref, ...), custom_call_target="tpu_custom_call" | custom-call | tf_op jit(solution)/shard_map/flow/pallas_call | solution.py:404
  11.9 15.2 %all_to_all.25.flow_ref = f32[16,1,128]{2,1,0:T(1,128)S(1)} all-to-all(f32[16,1,128]{2,1,0:T(1,128)S(1)} %get-tuple-element.17), channel_id=1, replica_groups=mesh['gz'=16,'xy'=32] {'gz'}, dimensions={0} | all-to-all | bytes 16384 | tf_op jit(solution)/shard_map/all_to_all | solution.py:363
  27.1 0.0 copy-done
  27.1 0.0 copy-done.3
  27.1 0.0 copy-done.5
  27.1 1.6 %render.1 = (f32[2,8]{1,0:T(2,128)S(1)}, bf16[32,136,128]{2,1,0:T(8,128)(2,1)S(1)}) custom-call(s32[2,2]{1,0:T(2,128)S(1)} %bitcast.23, f32[16,16]{1,0:T(8,128)S(1)} %copy-done.3, f32[16,1,128]{2,1,0:T(1,128)S(1)} %all_to_all.25.flow_ref, bf16[32,8,128]{2,1,0:T(8,128)(2,1)S(1)} %get-tuple-element.18.name_ref, bf16[2,512,512]{2,1,0:T(8,128)(2,1)S(1)} %bitcast.20), custom_call_target="tpu_custom_call" | custom-call | tf_op jit(solution)/shard_map/render/pallas_call | solution.py:417
  28.6 45.4 %conditional.1 = (bf16[32,136,128]{2,1,0:T(8,128)(2,1)S(1)}) conditional(s32[]{:T(128)} %convert_element_type.4, bf16[32,136,128]{2,1,0:T(8,128)(2,1)S(1)} %get-tuple-element.20, bf16[32,136,128]{2,1,0:T(8,128)(2,1)S(1)} %get-tuple-element.20), branch_computations={%region_0.1_spmd, %region_1.2_spmd} | conditional | bytes 6684680 | solution.py:429
  28.7 13.9 %all_to_all.23 = bf16[4,1088,128]{2,1,0:T(8,128)(2,1)S(1)} all-to-all(bf16[4,1088,128]{2,1,0:T(8,128)(2,1)S(1)} %bitcast.26), channel_id=1, replica_groups={{0,1,2,3},{4,5,6,7},{8,9,10,11},{12,13,14,15},{16,17,18,19},{20,21,22,2..., dimensions={0} | all-to-all | bytes 2228224 | tf_op jit(solution)/shard_map/cond/branch_1_fun/all_to_all | solution.py:363
  42.6 0.1 copy.10
  42.6 31.4 %all_to_all.24 = bf16[8,544,128]{2,1,0:T(8,128)(2,1)S(1)} all-to-all(bf16[8,544,128]{2,1,0:T(8,128)(2,1)S(1)} %bitcast.27), channel_id=1, replica_groups={{0,4,8,12,16,20,24,28},{1,5,9,13,17,21,25,29},{2,6,10,14,18,22,26,30},{..., dimensions={0} | all-to-all | bytes 2228224 | tf_op jit(solution)/shard_map/cond/branch_1_fun/all_to_all | solution.py:363
  74.0 1.0 %gather.1 = bf16[32,32,512]{2,1,0:T(8,128)(2,1)S(1)} custom-call(bf16[32,136,128]{2,1,0:T(8,128)(2,1)S(1)} %get-tuple-element.23.piece_ref), custom_call_target="tpu_custom_call" | custom-call | tf_op jit(solution)/shard_map/gather/pallas_call | solution.py:436
  75.0 22.9 %all_to_all.26.cell_ref = bf16[32,32,512]{2,1,0:T(8,128)(2,1)S(1)} all-to-all(bf16[32,32,512]{2,1,0:T(8,128)(2,1)S(1)} %gather.1), channel_id=1, replica_groups=mesh['gz'=16,'xy'=32] {'xy'}, dimensions={0} | all-to-all | bytes 2097152 | tf_op jit(solution)/shard_map/all_to_all | solution.py:363
  97.9 1.0 %place.1 = (f32[2,8]{1,0:T(2,128)}, bf16[2,32,16,512]{3,2,1,0:T(8,128)(2,1)}) custom-call(f32[2,8]{1,0:T(2,128)S(1)} %get-tuple-element.19.position_ref, bf16[32,32,512]{2,1,0:T(8,128)(2,1)S(1)} %all_to_all.26.cell_ref), custom_call_target="tpu_custom_call" | custom-call | tf_op jit(solution)/shard_map/place/pallas_call | solution.py:446
Async XLA Ops:
  0.6 9.4 %collective-permute-start = (bf16[1,8,128,128]{3,2,1,0:T(8,128)(2,1)}, bf16[1,8,128,128]{3,2,1,0:T(8,128)(2,1)S(1)}, u32[]{:S(2)}, u32[]{:S(2)}) collective-permute-start(bf16[1,8,128,128]{3,2,1,0:T(8,128)(2,1)} %param.10), channel_id=1, source_target_pairs={{0,32},{32,64},{64,96},{96,128},{128,160},{160,192},{192,224},{224... | collective-permute-start | bytes 786440 | tf_op jit(solution)/shard_map/ppermute | solution.py:388
  5.2 1.0 copy-start.2
  6.2 0.9 copy-start.7
  7.2 2.9 %copy-start.1 = (bf16[928,256]{1,0:T(8,128)(2,1)S(1)}, bf16[928,256]{1,0:T(8,128)(2,1)}, u32[]{:S(2)}) copy-start(bf16[928,256]{1,0:T(8,128)(2,1)} %constant.30.clone.inverse_ref) | copy-start | bytes 1425412
  7.2 2.9 %copy-start.4 = (s32[1,8,2]{1,2,0:T(2,128)S(1)}, s32[1,8,2]{1,2,0:T(2,128)}, u32[]{:S(2)}) copy-start(s32[1,8,2]{1,2,0:T(2,128)} %param.11) | copy-start | bytes 196
  7.2 2.9 %copy-start.6 = (s32[1,64,1]{1,2,0:T(1,128)S(1)}, s32[1,64,1]{1,2,0:T(1,128)}, u32[]{:S(2)}) copy-start(s32[1,64,1]{1,2,0:T(1,128)} %param.14) | copy-start | bytes 772
  7.9 19.1 %copy-start = (bf16[1,2,512,512]{3,2,1,0:T(8,128)(2,1)S(1)}, bf16[1,2,512,512]{3,2,1,0:T(8,128)(2,1)}, u32[]{:S(2)}) copy-start(bf16[1,2,512,512]{3,2,1,0:T(8,128)(2,1)} %param.12) | copy-start | bytes 3145732
  7.9 19.1 %copy-start.3 = (f32[16,16]{1,0:T(8,128)S(1)}, f32[16,16]{1,0:T(8,128)}, u32[]{:S(2)}) copy-start(f32[16,16]{1,0:T(8,128)} %constant.31.clone.map_ref) | copy-start | bytes 3076
  7.9 19.1 %copy-start.5 = (s32[1,2,2]{2,1,0:T(2,128)S(1)}, s32[1,2,2]{2,1,0:T(2,128)}, u32[]{:S(2)}) copy-start(s32[1,2,2]{2,1,0:T(2,128)} %param.13) | copy-start | bytes 52

commit v14 on v13

--- a/solution.py
+++ b/solution.py
@@ -225,10 +225,10 @@
     tile_count, edge, _ = tile_ref.shape
     slots = send_ref.shape[0]
     section = lax.axis_index("gz")
-    second_core = section % 2 == 1
+    later_core = section % 2 == 0
 
     def slot_of(p):
-        return jnp.where(second_core, p % WIDE * (slots // WIDE) + p // WIDE, p)
+        return jnp.where(later_core, p % WIDE * (slots // WIDE) + p // WIDE, p)
 
     lanes = lax.broadcasted_iota(jnp.int32, map_ref.shape, 1)
     weights = jnp.sum(jnp.where(lanes == section, map_ref[...], 0.0), axis=1, keepdims=True)
@@ -387,8 +387,8 @@
     section = lax.axis_index("gz")
     below = lax.ppermute(patches, "gz", [(i, i + 1) for i in range(sections - 1)])
     early_table, late_table = (jnp.asarray(t) for t in dft_constants())
-    second_core = section % 2 == 1
-    place = jnp.stack([lax.axis_index("xy"), second_core.astype(jnp.int32)])[None]
+    later_core = section % 2 == 0
+    place = jnp.stack([lax.axis_index("xy"), later_core.astype(jnp.int32)])[None]
     spectrum, power = pl.pallas_call(
         own_kernel,
         out_shape=(
@@ -427,7 +427,7 @@
         name="render",
     )(band_offsets[0], jnp.asarray(relaxation_map(sections).T), flow, names, tiles[0])
     pieces = lax.cond(
-        second_core,
+        later_core,
         exchange_x_then_z,
         lambda value: exchange(value, "xy"),
         pieces,

time: 99.2 us -> 109 us (1.099)
  the two profiles are of different devices: /device:TPU:1 before, /device:TPU:2 now
where the time goes in v14:
time: 109 us
  blocking collectives  98 us (90%)
  Pallas kernels  6.16 us (6%)
  local copies, waits for them, and re-layouts  2.16 us (2%)
  starting transfers between devices  1.75 us (2%)
    all_to_all x4, blocking collectives, exchange(): lax.all_to_all(value, axis, split_axis=0, concat_axis=0, tiled=True, axis...  98 us
  transfers between devices with their start and end apart: 1, of which 0 were waited for; matrix products, arithmetic and copies ran while one was open for 0% of the time, Pallas kernels for 1%

profile of v14, /device:TPU:2, one launch (start us, length us, event | category | flops | bytes accessed | tf_op | source)
XLA Modules:
  0.0 108.9 jit_solution(14889295639382238106)
XLA Ops:
  0.6 1.8 %collective-permute-start = (bf16[1,8,128,128]{3,2,1,0:T(8,128)(2,1)}, bf16[1,8,128,128]{3,2,1,0:T(8,128)(2,1)S(1)}, u32[]{:S(2)}, u32[]{:S(2)}) collective-permute-start(bf16[1,8,128,128]{3,2,1,0:T(8,128)(2,1)} %param.10), channel_id=1, source_target_pairs={{0,32},{32,64},{64,96},{96,128},{128,160},{160,192},{192,224},{224... | collective-permute-start | bytes 786440 | tf_op jit(solution)/shard_map/ppermute | solution.py:388
  2.4 0.0 copy-start.2
  2.4 0.9 copy-done.2
  3.4 0.0 copy-start.7
  3.4 0.9 copy-done.7
  4.3 0.0 copy-start.1
  4.3 0.0 copy-start.4
  4.3 0.0 copy-start.6
  4.3 0.7 own.1
  5.1 0.0 copy-start
  5.1 0.0 copy-start.3
  5.1 0.0 copy-start.5
  5.1 0.1 add_bitcast_fusion.place_ref
  5.2 0.0 collective-permute-done
  5.2 0.2 copy-done.1
  5.3 0.0 copy-done.4
  5.3 0.0 copy-done.6
  5.3 1.9 %flow.1 = (f32[16,1,128]{2,1,0:T(1,128)S(1)}, bf16[32,8,128]{2,1,0:T(8,128)(2,1)S(1)}) custom-call(s32[1,2]{1,0:T(1,128)S(1)} %add_bitcast_fusion.place_ref, s32[2,8]{1,0:T(2,128)S(1)} %bitcast.22, s32[1,64]{1,0:T(1,128)S(1)} %bitcast.24, bf16[8,128,128]{2,1,0:T(8,128)(2,1)S(1)} %bitcast.21, f32[8,72,256]{2,1,0:T(8,128)S(1)} %get-tuple-element.15.spectrum_ref, ...), custom_call_target="tpu_custom_call" | custom-call | tf_op jit(solution)/shard_map/flow/pallas_call | solution.py:404
  7.2 19.0 %all_to_all.25.flow_ref = f32[16,1,128]{2,1,0:T(1,128)S(1)} all-to-all(f32[16,1,128]{2,1,0:T(1,128)S(1)} %get-tuple-element.17), channel_id=1, replica_groups=mesh['gz'=16,'xy'=32] {'gz'}, dimensions={0} | all-to-all | bytes 16384 | tf_op jit(solution)/shard_map/all_to_all | solution.py:363
  26.2 0.0 copy-done
  26.2 0.0 copy-done.3
  26.2 0.0 copy-done.5
  26.2 1.6 %render.1 = (f32[2,8]{1,0:T(2,128)S(1)}, bf16[32,136,128]{2,1,0:T(8,128)(2,1)S(1)}) custom-call(s32[2,2]{1,0:T(2,128)S(1)} %bitcast.23, f32[16,16]{1,0:T(8,128)S(1)} %copy-done.3, f32[16,1,128]{2,1,0:T(1,128)S(1)} %all_to_all.25.flow_ref, bf16[32,8,128]{2,1,0:T(8,128)(2,1)S(1)} %get-tuple-element.18.name_ref, bf16[2,512,512]{2,1,0:T(8,128)(2,1)S(1)} %bitcast.20), custom_call_target="tpu_custom_call" | custom-call | tf_op jit(solution)/shard_map/render/pallas_call | solution.py:417
  27.8 55.9 %conditional.1 = (bf16[32,136,128]{2,1,0:T(8,128)(2,1)S(1)}) conditional(s32[]{:T(128)} %convert_element_type.4, bf16[32,136,128]{2,1,0:T(8,128)(2,1)S(1)} %get-tuple-element.20, bf16[32,136,128]{2,1,0:T(8,128)(2,1)S(1)} %get-tuple-element.20), branch_computations={%region_0.1_spmd, %region_1.2_spmd} | conditional | bytes 6684680 | solution.py:429
  27.8 14.4 %all_to_all.23 = bf16[4,1088,128]{2,1,0:T(8,128)(2,1)S(1)} all-to-all(bf16[4,1088,128]{2,1,0:T(8,128)(2,1)S(1)} %bitcast.26), channel_id=1, replica_groups={{0,1,2,3},{4,5,6,7},{8,9,10,11},{12,13,14,15},{16,17,18,19},{20,21,22,2..., dimensions={0} | all-to-all | bytes 2228224 | tf_op jit(solution)/shard_map/cond/branch_1_fun/all_to_all | solution.py:363
  42.2 0.1 copy.10
  42.3 41.4 %all_to_all.24 = bf16[8,544,128]{2,1,0:T(8,128)(2,1)S(1)} all-to-all(bf16[8,544,128]{2,1,0:T(8,128)(2,1)S(1)} %bitcast.27), channel_id=1, replica_groups={{0,4,8,12,16,20,24,28},{1,5,9,13,17,21,25,29},{2,6,10,14,18,22,26,30},{..., dimensions={0} | all-to-all | bytes 2228224 | tf_op jit(solution)/shard_map/cond/branch_1_fun/all_to_all | solution.py:363
  83.7 1.0 gather.1
  84.7 23.2 %all_to_all.26.cell_ref = bf16[32,32,512]{2,1,0:T(8,128)(2,1)S(1)} all-to-all(bf16[32,32,512]{2,1,0:T(8,128)(2,1)S(1)} %gather.1), channel_id=1, replica_groups=mesh['gz'=16,'xy'=32] {'xy'}, dimensions={0} | all-to-all | bytes 2097152 | tf_op jit(solution)/shard_map/all_to_all | solution.py:363
  107.9 1.0 place.1
Async XLA Ops:
  0.6 4.6 %collective-permute-start = (bf16[1,8,128,128]{3,2,1,0:T(8,128)(2,1)}, bf16[1,8,128,128]{3,2,1,0:T(8,128)(2,1)S(1)}, u32[]{:S(2)}, u32[]{:S(2)}) collective-permute-start(bf16[1,8,128,128]{3,2,1,0:T(8,128)(2,1)} %param.10), channel_id=1, source_target_pairs={{0,32},{32,64},{64,96},{96,128},{128,160},{160,192},{192,224},{224... | collective-permute-start | bytes 786440 | tf_op jit(solution)/shard_map/ppermute | solution.py:388
  2.4 1.0 copy-start.2
  3.4 0.9 copy-start.7
  4.3 1.0 copy-start.1
  4.3 1.0 copy-start.4
  4.3 1.0 copy-start.6
  5.1 21.1 %copy-start = (bf16[1,2,512,512]{3,2,1,0:T(8,128)(2,1)S(1)}, bf16[1,2,512,512]{3,2,1,0:T(8,128)(2,1)}, u32[]{:S(2)}) copy-start(bf16[1,2,512,512]{3,2,1,0:T(8,128)(2,1)} %param.12) | copy-start | bytes 3145732
  5.1 21.1 %copy-start.3 = (f32[16,16]{1,0:T(8,128)S(1)}, f32[16,16]{1,0:T(8,128)}, u32[]{:S(2)}) copy-start(f32[16,16]{1,0:T(8,128)} %constant.31.clone.map_ref) | copy-start | bytes 3076
  5.1 21.1 %copy-start.5 = (s32[1,2,2]{2,1,0:T(2,128)S(1)}, s32[1,2,2]{2,1,0:T(2,128)}, u32[]{:S(2)}) copy-start(s32[1,2,2]{2,1,0:T(2,128)} %param.13) | copy-start | bytes 52

commit v15 on v13

--- a/solution.py
+++ b/solution.py
@@ -196,21 +196,25 @@
     out_ref[...] = jnp.broadcast_to(flow[None], out_ref.shape)
 
 
-def fill_band(target_ref, residual, offset, sub_sign):
+def tap_norm(residual):
+    lane = lax.broadcasted_iota(jnp.int32, (1, EXTENT), 1)
+    away = (lane - BAND).astype(F32) - residual
+    raw = jnp.where(lane <= 2 * BAND, 1.0 / (1.0 + away * away), 0.0)
+    return jnp.sum(raw, axis=1, keepdims=True)
+
+
+def fill_columns(target_ref, residual, offset):
     block = EXTENT
-    lane = lax.broadcasted_iota(jnp.int32, (1, block), 1)
-    tap = (lane - BAND).astype(F32) - residual
-    raw = jnp.where(lane <= 2 * BAND, 1.0 / (1.0 + tap * tap), 0.0)
-    norm = jnp.sum(raw, axis=1, keepdims=True)
+    norm = tap_norm(residual)
     a = lax.broadcasted_iota(jnp.int32, (block, block), 0)
     b = lax.broadcasted_iota(jnp.int32, (block, block), 1)
-    d = sub_sign * (a - b) - offset
+    d = a - b - offset
     k = ((d + block // 2) & (block - 1)) - block // 2
     away = k.astype(F32) - residual
     value = (1.0 / (1.0 + away * away)) / norm
     blocks = {}
     for step in (-1, 0, 1):
-        near = jnp.abs(d + sub_sign * step * block) <= BAND
+        near = jnp.abs(d + step * block) <= BAND
         blocks[step] = jnp.where(near, value, 0.0).astype(BF)
     zero = jnp.zeros((block, block), BF)
     count = target_ref.shape[0] // block
@@ -219,6 +223,31 @@
             target_ref[i * block : (i + 1) * block, j * block : (j + 1) * block] = blocks.get(
                 i - j, zero
             )
+
+
+def window_start(chunk_index, chunk, edge):
+    return min(max(chunk_index * chunk - chunk // 2, 0), edge - 2 * chunk)
+
+
+def fill_rows(target_ref, residual, offset):
+    chunk = target_ref.shape[1] // 2
+    edge = target_ref.shape[0]
+    norm = tap_norm(residual)
+    a = lax.broadcasted_iota(jnp.int32, (chunk, chunk), 0)
+    b = lax.broadcasted_iota(jnp.int32, (chunk, chunk), 1)
+    made = {}
+    for c in range(edge // chunk):
+        step = window_start(c, chunk, edge) - c * chunk
+        if step not in made:
+            d = b - a - offset + step
+            k = ((d + chunk // 2) & (chunk - 1)) - chunk // 2
+            away = k.astype(F32) - residual
+            value = (1.0 / (1.0 + away * away)) / norm
+            made[step] = [
+                jnp.where(jnp.abs(d + j * chunk) <= BAND, value, 0.0).astype(BF) for j in range(2)
+            ]
+        for j in range(2):
+            target_ref[c * chunk : (c + 1) * chunk, j * chunk : (j + 1) * chunk] = made[step][j]
 
 
 def render_kernel(band_ref, map_ref, flow_ref, name_ref, tile_ref, position_ref, send_ref, *scratch):
@@ -243,12 +272,12 @@
     chunk = EXTENT
     chunks = edge // chunk
 
-    def fill(t, c, target_ref, sub_sign):
+    def fill(t, c, target_ref):
         offset = band_ref[t : t + 1, c : c + 1]
         here = lanes // per_tile == c * tile_count + t
         total = jnp.sum(jnp.where(here, position, 0.0), axis=1, keepdims=True)
         shift = total * (MIP_SCALE / per_tile)
-        fill_band(target_ref, shift - offset.astype(F32), offset, sub_sign)
+        (fill_rows, fill_columns)[c](target_ref, shift - offset.astype(F32), offset)
 
     def first(t, c):
         col_ref, _, pass_ref = scratch[3 * t : 3 * t + 3]
@@ -257,11 +286,8 @@
 
     def second(t, c):
         _, row_ref, pass_ref = scratch[3 * t : 3 * t + 3]
-        near = range(max(c - 1, 0), min(c + 2, chunks))
-        from_row = near[0] * chunk // (edge // 2) * (edge // 2)
-        to_row = edge // 2 if near[-1] * chunk < edge // 2 else edge
-        rows = slice(c * chunk, (c + 1) * chunk)
-        done = dot(row_ref[rows, from_row:to_row], pass_ref[from_row:to_row, :]).astype(BF)
+        start = window_start(c, chunk, edge)
+        done = dot(row_ref[c * chunk : (c + 1) * chunk, :], pass_ref[start : start + 2 * chunk, :]).astype(BF)
         each = chunk // height
         done = done.reshape(each, height, edge)
         for p in range(each):
@@ -272,14 +298,14 @@
                 ]
 
     tail = tile_count * columns * height
-    fill(0, 1, scratch[0], 1)
+    fill(0, 1, scratch[0])
     for t in range(tile_count):
         for c in range(chunks):
             first(t, c)
             if c == 0:
-                fill(t, 0, scratch[3 * t + 1], -1)
+                fill(t, 0, scratch[3 * t + 1])
             if c == 1 and t + 1 < tile_count:
-                fill(t + 1, 1, scratch[3 * t + 3], 1)
+                fill(t + 1, 1, scratch[3 * t + 3])
             if t > 0:
                 second(t - 1, c)
     for c in range(chunks):
@@ -422,7 +448,9 @@
         ),
         in_specs=[in_vmem()] * 5,
         out_specs=(in_vmem(), in_vmem()),
-        scratch_shapes=[pltpu.VMEM((edge, edge), BF)] * (3 * tile_count),
+        scratch_shapes=[
+            pltpu.VMEM((edge, width), BF) for width in (edge, 2 * EXTENT, edge) * tile_count
+        ],
         compiler_params=params(),
         name="render",
     )(band_offsets[0], jnp.asarray(relaxation_map(sections).T), flow, names, tiles[0])

time: 99.2 us -> 99.1 us (level)
  no operation moved by 1% of the time
where the time goes in v15:
time: 99.1 us; the launch traced here: 98.8 us
  blocking collectives  83.3 us (84%)
  Pallas kernels  6.02 us (6%)
  starting transfers between devices  4.59 us (5%)
  local copies, waits for them, and re-layouts  2.01 us (2%)
  waiting for transfers between devices  2 us (2%)
    all_to_all x4, blocking collectives, exchange(): lax.all_to_all(value, axis, split_axis=0, concat_axis=0, tiled=True, axis...  83.3 us
    ppermute x1, starting transfers between devices, body(): lax.ppermute(patches, 'gz', [(i, i + 1) for i in range(sections - 1)])  4.59 us
    ppermute x1, waiting for transfers between devices, body(): lax.ppermute(patches, 'gz', [(i, i + 1) for i in range(sections - 1)])  2 us
  transfers between devices with their start and end apart: 1, of which 1 were waited for; matrix products, arithmetic and copies ran while one was open for 0% of the time, Pallas kernels for 1%

profile of v15, /device:TPU:1, one launch (start us, length us, event | category | flops | bytes accessed | tf_op | source)
XLA Modules:
  0.0 98.8 jit_solution(1630091726235655679)
XLA Ops:
  0.6 4.6 %collective-permute-start = (bf16[1,8,128,128]{3,2,1,0:T(8,128)(2,1)}, bf16[1,8,128,128]{3,2,1,0:T(8,128)(2,1)S(1)}, u32[]{:S(2)}, u32[]{:S(2)}) collective-permute-start(bf16[1,8,128,128]{3,2,1,0:T(8,128)(2,1)} %param.10), channel_id=1, source_target_pairs={{0,32},{32,64},{64,96},{96,128},{128,160},{160,192},{192,224},{224... | collective-permute-start | bytes 786440 | tf_op jit(solution)/shard_map/ppermute | solution.py:414
  5.2 0.0 copy-start.2
  5.3 0.9 copy-done.2
  6.2 0.0 copy-start.7
  6.2 0.9 copy-done.7
  7.2 0.0 copy-start.1
  7.2 0.0 copy-start.4
  7.2 0.0 copy-start.6
  7.2 0.7 own.1
  7.9 0.0 copy-start
  7.9 0.0 copy-start.3
  7.9 0.0 copy-start.5
  7.9 0.1 add_bitcast_fusion.place_ref
  8.0 2.0 %collective-permute-done = bf16[1,8,128,128]{3,2,1,0:T(8,128)(2,1)S(1)} collective-permute-done((bf16[1,8,128,128]{3,2,1,0:T(8,128)(2,1)}, bf16[1,8,128,128]{3,2,1,0:T(8,128)(2,1)S(1)}, u32[]{:S(2)}, u32[]{:S(2)}) %collective-permute-start) | collective-permute-done | bytes 262176 | tf_op jit(solution)/shard_map/ppermute | solution.py:414
  10.0 0.0 copy-done.1
  10.0 0.0 copy-done.4
  10.0 0.0 copy-done.6
  10.0 1.9 %flow.1 = (f32[16,1,128]{2,1,0:T(1,128)S(1)}, bf16[32,8,128]{2,1,0:T(8,128)(2,1)S(1)}) custom-call(s32[1,2]{1,0:T(1,128)S(1)} %add_bitcast_fusion.place_ref, s32[2,8]{1,0:T(2,128)S(1)} %bitcast.22, s32[1,64]{1,0:T(1,128)S(1)} %bitcast.24, bf16[8,128,128]{2,1,0:T(8,128)(2,1)S(1)} %bitcast.21, f32[8,72,256]{2,1,0:T(8,128)S(1)} %get-tuple-element.15.spectrum_ref, ...), custom_call_target="tpu_custom_call" | custom-call | tf_op jit(solution)/shard_map/flow/pallas_call | solution.py:430
  11.9 15.2 %all_to_all.25.flow_ref = f32[16,1,128]{2,1,0:T(1,128)S(1)} all-to-all(f32[16,1,128]{2,1,0:T(1,128)S(1)} %get-tuple-element.17), channel_id=1, replica_groups=mesh['gz'=16,'xy'=32] {'gz'}, dimensions={0} | all-to-all | bytes 16384 | tf_op jit(solution)/shard_map/all_to_all | solution.py:389
  27.1 0.0 copy-done
  27.1 0.0 copy-done.3
  27.1 0.0 copy-done.5
  27.1 1.4 %render.1 = (f32[2,8]{1,0:T(2,128)S(1)}, bf16[32,136,128]{2,1,0:T(8,128)(2,1)S(1)}) custom-call(s32[2,2]{1,0:T(2,128)S(1)} %bitcast.23, f32[16,16]{1,0:T(8,128)S(1)} %copy-done.3, f32[16,1,128]{2,1,0:T(1,128)S(1)} %all_to_all.25.flow_ref, bf16[32,8,128]{2,1,0:T(8,128)(2,1)S(1)} %get-tuple-element.18.name_ref, bf16[2,512,512]{2,1,0:T(8,128)(2,1)S(1)} %bitcast.20), custom_call_target="tpu_custom_call" | custom-call | tf_op jit(solution)/shard_map/render/pallas_call | solution.py:443
  28.5 45.4 %conditional.1 = (bf16[32,136,128]{2,1,0:T(8,128)(2,1)S(1)}) conditional(s32[]{:T(128)} %convert_element_type.4, bf16[32,136,128]{2,1,0:T(8,128)(2,1)S(1)} %get-tuple-element.20, bf16[32,136,128]{2,1,0:T(8,128)(2,1)S(1)} %get-tuple-element.20), branch_computations={%region_0.1_spmd, %region_1.2_spmd} | conditional | bytes 6684680 | solution.py:457
  28.5 13.9 %all_to_all.23 = bf16[4,1088,128]{2,1,0:T(8,128)(2,1)S(1)} all-to-all(bf16[4,1088,128]{2,1,0:T(8,128)(2,1)S(1)} %bitcast.26), channel_id=1, replica_groups={{0,1,2,3},{4,5,6,7},{8,9,10,11},{12,13,14,15},{16,17,18,19},{20,21,22,2..., dimensions={0} | all-to-all | bytes 2228224 | tf_op jit(solution)/shard_map/cond/branch_1_fun/all_to_all | solution.py:389
  42.4 0.1 copy.10
  42.5 31.4 %all_to_all.24 = bf16[8,544,128]{2,1,0:T(8,128)(2,1)S(1)} all-to-all(bf16[8,544,128]{2,1,0:T(8,128)(2,1)S(1)} %bitcast.27), channel_id=1, replica_groups={{0,4,8,12,16,20,24,28},{1,5,9,13,17,21,25,29},{2,6,10,14,18,22,26,30},{..., dimensions={0} | all-to-all | bytes 2228224 | tf_op jit(solution)/shard_map/cond/branch_1_fun/all_to_all | solution.py:389
  73.9 1.0 %gather.1 = bf16[32,32,512]{2,1,0:T(8,128)(2,1)S(1)} custom-call(bf16[32,136,128]{2,1,0:T(8,128)(2,1)S(1)} %get-tuple-element.23.piece_ref), custom_call_target="tpu_custom_call" | custom-call | tf_op jit(solution)/shard_map/gather/pallas_call | solution.py:464
  74.9 22.9 %all_to_all.26.cell_ref = bf16[32,32,512]{2,1,0:T(8,128)(2,1)S(1)} all-to-all(bf16[32,32,512]{2,1,0:T(8,128)(2,1)S(1)} %gather.1), channel_id=1, replica_groups=mesh['gz'=16,'xy'=32] {'xy'}, dimensions={0} | all-to-all | bytes 2097152 | tf_op jit(solution)/shard_map/all_to_all | solution.py:389
  97.8 1.0 %place.1 = (f32[2,8]{1,0:T(2,128)}, bf16[2,32,16,512]{3,2,1,0:T(8,128)(2,1)}) custom-call(f32[2,8]{1,0:T(2,128)S(1)} %get-tuple-element.19.position_ref, bf16[32,32,512]{2,1,0:T(8,128)(2,1)S(1)} %all_to_all.26.cell_ref), custom_call_target="tpu_custom_call" | custom-call | tf_op jit(solution)/shard_map/place/pallas_call | solution.py:474
Async XLA Ops:
  0.6 9.4 %collective-permute-start = (bf16[1,8,128,128]{3,2,1,0:T(8,128)(2,1)}, bf16[1,8,128,128]{3,2,1,0:T(8,128)(2,1)S(1)}, u32[]{:S(2)}, u32[]{:S(2)}) collective-permute-start(bf16[1,8,128,128]{3,2,1,0:T(8,128)(2,1)} %param.10), channel_id=1, source_target_pairs={{0,32},{32,64},{64,96},{96,128},{128,160},{160,192},{192,224},{224... | collective-permute-start | bytes 786440 | tf_op jit(solution)/shard_map/ppermute | solution.py:414
  5.2 1.0 copy-start.2
  6.2 0.9 copy-start.7
  7.2 2.9 %copy-start.1 = (bf16[928,256]{1,0:T(8,128)(2,1)S(1)}, bf16[928,256]{1,0:T(8,128)(2,1)}, u32[]{:S(2)}) copy-start(bf16[928,256]{1,0:T(8,128)(2,1)} %constant.30.clone.inverse_ref) | copy-start | bytes 1425412
  7.2 2.9 %copy-start.4 = (s32[1,8,2]{1,2,0:T(2,128)S(1)}, s32[1,8,2]{1,2,0:T(2,128)}, u32[]{:S(2)}) copy-start(s32[1,8,2]{1,2,0:T(2,128)} %param.11) | copy-start | bytes 196
  7.2 2.9 %copy-start.6 = (s32[1,64,1]{1,2,0:T(1,128)S(1)}, s32[1,64,1]{1,2,0:T(1,128)}, u32[]{:S(2)}) copy-start(s32[1,64,1]{1,2,0:T(1,128)} %param.14) | copy-start | bytes 772
  7.9 19.1 %copy-start = (bf16[1,2,512,512]{3,2,1,0:T(8,128)(2,1)S(1)}, bf16[1,2,512,512]{3,2,1,0:T(8,128)(2,1)}, u32[]{:S(2)}) copy-start(bf16[1,2,512,512]{3,2,1,0:T(8,128)(2,1)} %param.12) | copy-start | bytes 3145732
  7.9 19.1 %copy-start.3 = (f32[16,16]{1,0:T(8,128)S(1)}, f32[16,16]{1,0:T(8,128)}, u32[]{:S(2)}) copy-start(f32[16,16]{1,0:T(8,128)} %constant.31.clone.map_ref) | copy-start | bytes 3076
  7.9 19.1 %copy-start.5 = (s32[1,2,2]{2,1,0:T(2,128)S(1)}, s32[1,2,2]{2,1,0:T(2,128)}, u32[]{:S(2)}) copy-start(s32[1,2,2]{2,1,0:T(2,128)} %param.13) | copy-start | bytes 52

commit v16 on v15

--- a/solution.py
+++ b/solution.py
@@ -324,17 +324,6 @@
     part = EXTENT // SHARE // tile_count
     parts = height // part
     depth = owners * tile_count * part
-    for d in range(owners):
-        for j in range(columns):
-            pieces = []
-            for t in range(tile_count):
-                at = (t * columns + j) * height
-                pieces.append(piece_ref[d, at : at + height, :].astype(F32))
-            for k in range(parts):
-                at = k * depth + d * tile_count * part
-                data_ref[at : at + tile_count * part, j * EXTENT : (j + 1) * EXTENT] = (
-                    jnp.concatenate([p[k * part : (k + 1) * part] for p in pieces], 0).astype(BF)
-                )
     lane = lax.broadcasted_iota(jnp.int32, (EXTENT, EXTENT), 1)
     sub = lax.broadcasted_iota(jnp.int32, (EXTENT, EXTENT), 0)
     same = lane % part == sub % part
@@ -343,19 +332,34 @@
         for start in range(0, owners, SHARE)
     ]
     each = EXTENT // part
+    picks = []
     for c in range(owners * out_rows // height // each):
         group = (sub // part + c * each).astype(F32)
         hits = [jnp.where(same & (name == group), 1.0, 0.0) for name in names]
         count = jnp.sum(sum(hits), axis=1, keepdims=True)
-        scale = 1.0 / jnp.maximum(count, 1.0)
-        pick = jnp.concatenate([hit.astype(BF) for hit in hits], 1)
-        totals = [
-            (dot(pick, data_ref[k * depth : (k + 1) * depth]) * scale).reshape(each, part, edge)
-            for k in range(parts)
-        ]
-        total = jnp.concatenate(totals, 1).astype(BF)
-        first, last = c * each * height // out_rows, (c + 1) * each * height // out_rows
-        out_ref[first:last] = total.reshape(last - first, out_rows, edge)
+        picks.append((jnp.concatenate([hit.astype(BF) for hit in hits], 1), 1.0 / jnp.maximum(count, 1.0)))
+    wide = edge // 2
+    for side in range(2):
+        for d in range(owners):
+            for j in range(side * columns // 2, (side + 1) * columns // 2):
+                pieces = []
+                for t in range(tile_count):
+                    at = (t * columns + j) * height
+                    pieces.append(piece_ref[d, at : at + height, :].astype(F32))
+                for k in range(parts):
+                    at = k * depth + d * tile_count * part
+                    data_ref[at : at + tile_count * part, j * EXTENT : (j + 1) * EXTENT] = (
+                        jnp.concatenate([p[k * part : (k + 1) * part] for p in pieces], 0).astype(BF)
+                    )
+        lanes = slice(side * wide, (side + 1) * wide)
+        for c, (pick, scale) in enumerate(picks):
+            totals = [
+                (dot(pick, data_ref[k * depth : (k + 1) * depth, lanes]) * scale).reshape(each, part, wide)
+                for k in range(parts)
+            ]
+            total = jnp.concatenate(totals, 1).astype(BF)
+            first, last = c * each * height // out_rows, (c + 1) * each * height // out_rows
+            out_ref[first:last, :, lanes] = total.reshape(last - first, out_rows, wide)
 
 
 def place_kernel(position_ref, cell_ref, moved_ref, out_ref, arrived):

time: 99.1 us -> 99.1 us (level)
  no operation moved by 1% of the time
where the time goes in v16:
time: 99.1 us; the launch traced here: 98.7 us
  blocking collectives  83.3 us (84%)
  Pallas kernels  6 us (6%)
  starting transfers between devices  4.59 us (5%)
  local copies, waits for them, and re-layouts  2.01 us (2%)
  waiting for transfers between devices  2 us (2%)
    all_to_all x4, blocking collectives, exchange(): lax.all_to_all(value, axis, split_axis=0, concat_axis=0, tiled=True, axis...  83.3 us
    ppermute x1, starting transfers between devices, body(): lax.ppermute(patches, 'gz', [(i, i + 1) for i in range(sections - 1)])  4.59 us
    ppermute x1, waiting for transfers between devices, body(): lax.ppermute(patches, 'gz', [(i, i + 1) for i in range(sections - 1)])  2 us
  transfers between devices with their start and end apart: 1, of which 1 were waited for; matrix products, arithmetic and copies ran while one was open for 0% of the time, Pallas kernels for 1%

profile of v16, /device:TPU:1, one launch (start us, length us, event | category | flops | bytes accessed | tf_op | source)
XLA Modules:
  0.0 98.7 jit_solution(6706370266518958389)
XLA Ops:
  0.6 4.6 %collective-permute-start = (bf16[1,8,128,128]{3,2,1,0:T(8,128)(2,1)}, bf16[1,8,128,128]{3,2,1,0:T(8,128)(2,1)S(1)}, u32[]{:S(2)}, u32[]{:S(2)}) collective-permute-start(bf16[1,8,128,128]{3,2,1,0:T(8,128)(2,1)} %param.10), channel_id=1, source_target_pairs={{0,32},{32,64},{64,96},{96,128},{128,160},{160,192},{192,224},{224... | collective-permute-start | bytes 786440 | tf_op jit(solution)/shard_map/ppermute | solution.py:418
  5.2 0.0 copy-start.2
  5.3 0.9 copy-done.2
  6.2 0.0 copy-start.7
  6.2 0.9 copy-done.7
  7.2 0.0 copy-start.1
  7.2 0.0 copy-start.4
  7.2 0.0 copy-start.6
  7.2 0.7 own.1
  7.9 0.0 copy-start
  7.9 0.0 copy-start.3
  7.9 0.0 copy-start.5
  7.9 0.1 add_bitcast_fusion.place_ref
  8.0 2.0 %collective-permute-done = bf16[1,8,128,128]{3,2,1,0:T(8,128)(2,1)S(1)} collective-permute-done((bf16[1,8,128,128]{3,2,1,0:T(8,128)(2,1)}, bf16[1,8,128,128]{3,2,1,0:T(8,128)(2,1)S(1)}, u32[]{:S(2)}, u32[]{:S(2)}) %collective-permute-start) | collective-permute-done | bytes 262176 | tf_op jit(solution)/shard_map/ppermute | solution.py:418
  10.0 0.0 copy-done.1
  10.0 0.0 copy-done.4
  10.0 0.0 copy-done.6
  10.0 1.9 %flow.1 = (f32[16,1,128]{2,1,0:T(1,128)S(1)}, bf16[32,8,128]{2,1,0:T(8,128)(2,1)S(1)}) custom-call(s32[1,2]{1,0:T(1,128)S(1)} %add_bitcast_fusion.place_ref, s32[2,8]{1,0:T(2,128)S(1)} %bitcast.22, s32[1,64]{1,0:T(1,128)S(1)} %bitcast.24, bf16[8,128,128]{2,1,0:T(8,128)(2,1)S(1)} %bitcast.21, f32[8,72,256]{2,1,0:T(8,128)S(1)} %get-tuple-element.15.spectrum_ref, ...), custom_call_target="tpu_custom_call" | custom-call | tf_op jit(solution)/shard_map/flow/pallas_call | solution.py:434
  11.9 15.2 %all_to_all.25.flow_ref = f32[16,1,128]{2,1,0:T(1,128)S(1)} all-to-all(f32[16,1,128]{2,1,0:T(1,128)S(1)} %get-tuple-element.17), channel_id=1, replica_groups=mesh['gz'=16,'xy'=32] {'gz'}, dimensions={0} | all-to-all | bytes 16384 | tf_op jit(solution)/shard_map/all_to_all | solution.py:393
  27.1 0.0 copy-done
  27.1 0.0 copy-done.3
  27.1 0.0 copy-done.5
  27.1 1.4 %render.1 = (f32[2,8]{1,0:T(2,128)S(1)}, bf16[32,136,128]{2,1,0:T(8,128)(2,1)S(1)}) custom-call(s32[2,2]{1,0:T(2,128)S(1)} %bitcast.23, f32[16,16]{1,0:T(8,128)S(1)} %copy-done.3, f32[16,1,128]{2,1,0:T(1,128)S(1)} %all_to_all.25.flow_ref, bf16[32,8,128]{2,1,0:T(8,128)(2,1)S(1)} %get-tuple-element.18.name_ref, bf16[2,512,512]{2,1,0:T(8,128)(2,1)S(1)} %bitcast.20), custom_call_target="tpu_custom_call" | custom-call | tf_op jit(solution)/shard_map/render/pallas_call | solution.py:447
  28.5 45.4 %conditional.1 = (bf16[32,136,128]{2,1,0:T(8,128)(2,1)S(1)}) conditional(s32[]{:T(128)} %convert_element_type.4, bf16[32,136,128]{2,1,0:T(8,128)(2,1)S(1)} %get-tuple-element.20, bf16[32,136,128]{2,1,0:T(8,128)(2,1)S(1)} %get-tuple-element.20), branch_computations={%region_0.1_spmd, %region_1.2_spmd} | conditional | bytes 6684680 | solution.py:461
  28.5 13.9 %all_to_all.23 = bf16[4,1088,128]{2,1,0:T(8,128)(2,1)S(1)} all-to-all(bf16[4,1088,128]{2,1,0:T(8,128)(2,1)S(1)} %bitcast.26), channel_id=1, replica_groups={{0,1,2,3},{4,5,6,7},{8,9,10,11},{12,13,14,15},{16,17,18,19},{20,21,22,2..., dimensions={0} | all-to-all | bytes 2228224 | tf_op jit(solution)/shard_map/cond/branch_1_fun/all_to_all | solution.py:393
  42.4 0.1 copy.10
  42.5 31.4 %all_to_all.24 = bf16[8,544,128]{2,1,0:T(8,128)(2,1)S(1)} all-to-all(bf16[8,544,128]{2,1,0:T(8,128)(2,1)S(1)} %bitcast.27), channel_id=1, replica_groups={{0,4,8,12,16,20,24,28},{1,5,9,13,17,21,25,29},{2,6,10,14,18,22,26,30},{..., dimensions={0} | all-to-all | bytes 2228224 | tf_op jit(solution)/shard_map/cond/branch_1_fun/all_to_all | solution.py:393
  73.9 1.0 %gather.1 = bf16[32,32,512]{2,1,0:T(8,128)(2,1)S(1)} custom-call(bf16[32,136,128]{2,1,0:T(8,128)(2,1)S(1)} %get-tuple-element.23.piece_ref), custom_call_target="tpu_custom_call" | custom-call | tf_op jit(solution)/shard_map/gather/pallas_call | solution.py:468
  74.9 22.9 %all_to_all.26.cell_ref = bf16[32,32,512]{2,1,0:T(8,128)(2,1)S(1)} all-to-all(bf16[32,32,512]{2,1,0:T(8,128)(2,1)S(1)} %gather.1), channel_id=1, replica_groups=mesh['gz'=16,'xy'=32] {'xy'}, dimensions={0} | all-to-all | bytes 2097152 | tf_op jit(solution)/shard_map/all_to_all | solution.py:393
  97.8 1.0 %place.1 = (f32[2,8]{1,0:T(2,128)}, bf16[2,32,16,512]{3,2,1,0:T(8,128)(2,1)}) custom-call(f32[2,8]{1,0:T(2,128)S(1)} %get-tuple-element.19.position_ref, bf16[32,32,512]{2,1,0:T(8,128)(2,1)S(1)} %all_to_all.26.cell_ref), custom_call_target="tpu_custom_call" | custom-call | tf_op jit(solution)/shard_map/place/pallas_call | solution.py:478
Async XLA Ops:
  0.6 9.4 %collective-permute-start = (bf16[1,8,128,128]{3,2,1,0:T(8,128)(2,1)}, bf16[1,8,128,128]{3,2,1,0:T(8,128)(2,1)S(1)}, u32[]{:S(2)}, u32[]{:S(2)}) collective-permute-start(bf16[1,8,128,128]{3,2,1,0:T(8,128)(2,1)} %param.10), channel_id=1, source_target_pairs={{0,32},{32,64},{64,96},{96,128},{128,160},{160,192},{192,224},{224... | collective-permute-start | bytes 786440 | tf_op jit(solution)/shard_map/ppermute | solution.py:418
  5.2 1.0 copy-start.2
  6.2 0.9 copy-start.7
  7.2 2.9 %copy-start.1 = (bf16[928,256]{1,0:T(8,128)(2,1)S(1)}, bf16[928,256]{1,0:T(8,128)(2,1)}, u32[]{:S(2)}) copy-start(bf16[928,256]{1,0:T(8,128)(2,1)} %constant.30.clone.inverse_ref) | copy-start | bytes 1425412
  7.2 2.9 %copy-start.4 = (s32[1,8,2]{1,2,0:T(2,128)S(1)}, s32[1,8,2]{1,2,0:T(2,128)}, u32[]{:S(2)}) copy-start(s32[1,8,2]{1,2,0:T(2,128)} %param.11) | copy-start | bytes 196
  7.2 2.9 %copy-start.6 = (s32[1,64,1]{1,2,0:T(1,128)S(1)}, s32[1,64,1]{1,2,0:T(1,128)}, u32[]{:S(2)}) copy-start(s32[1,64,1]{1,2,0:T(1,128)} %param.14) | copy-start | bytes 772
  7.9 19.1 %copy-start = (bf16[1,2,512,512]{3,2,1,0:T(8,128)(2,1)S(1)}, bf16[1,2,512,512]{3,2,1,0:T(8,128)(2,1)}, u32[]{:S(2)}) copy-start(bf16[1,2,512,512]{3,2,1,0:T(8,128)(2,1)} %param.12) | copy-start | bytes 3145732
  7.9 19.1 %copy-start.3 = (f32[16,16]{1,0:T(8,128)S(1)}, f32[16,16]{1,0:T(8,128)}, u32[]{:S(2)}) copy-start(f32[16,16]{1,0:T(8,128)} %constant.31.clone.map_ref) | copy-start | bytes 3076
  7.9 19.1 %copy-start.5 = (s32[1,2,2]{2,1,0:T(2,128)S(1)}, s32[1,2,2]{2,1,0:T(2,128)}, u32[]{:S(2)}) copy-start(s32[1,2,2]{2,1,0:T(2,128)} %param.13) | copy-start | bytes 52
